TPU v7x, 32 devices: a whole 2x2x4 slice. The times are simulated.
32 devices in a mesh: gx: 2 (over x), gy: 8 (over z, y), vert: 2 (over core).
Axes of the slice: x: 2, y: 2, z: 4, core: 2. Of those that a mesh axis runs over, the one named last changes fastest.
Arguments:
- distribution: float32 [32, 128, 4096], P('gx', 'gy', 'vert'), may hold values from -6 to 6
- density: float32 [32, 128], P('gx', 'gy'), may hold values from 0.3 to 3
- cell_type: int32 [32, 128], P('gx', 'gy'), may hold values from 0 to 2, as said below
- inflow: float32 [4096], P('vert'), may hold values from -6 to 6
Outputs:
- evolved: float32 [32, 128, 4096], P('gx', 'gy', 'vert')
Inputs may be any that keep to these rules, and one draw needn't show every extreme that they name: `cell_type`: 0 marks a gas cell, 1 a wall cell, 2 an inflow cell; most cells are gas cells.
All inputs are finite; a program needn't handle non-finite values.
Results may differ from a plain program's by a relative error of at most 0.0003.
Values sent between devices are 32-bit elements; how exact they have to be, the bound alone decides.
No kernel may reach another device: no remote copies, remote signals or barrier semaphores. Data moves between devices by JAX's collectives and lax.ppermute only.
A program may use at most 128 MiB of HBM per device.

v0:
```python
import functools
import math

import jax
import jax.numpy as jnp
from jax import lax
from jax.experimental import pallas as pl
from jax.experimental.pallas import tpu as pltpu
from jax.sharding import PartitionSpec as P

NVX = 64
STEPS = 2
HALF = NVX // 2
LANES = 128
GROUP = LANES // HALF

vel_max = 4.0
time_step = 0.1
grad_scale = 2.5
collision_rate = 0.2
spacing = 2.0 * vel_max / NVX
middle = 0.5 * (NVX - 1)

MIB = 1024 * 1024
WHOLE = pl.BlockSpec(memory_space=pltpu.VMEM)
SCALARS = pl.BlockSpec(memory_space=pltpu.SMEM)

EXPONENT = 0.125 * math.log2(math.e)
ENTRY_SCALE = grad_scale * spacing * spacing * math.sqrt(EXPONENT)


def room(mib):
    return pltpu.CompilerParams(vmem_limit_bytes=mib * MIB)


def in_vmem(value):
    return pltpu.with_memory_space_constraint(value, pltpu.VMEM)


def velocity_parts(index):
    row_portion = (index // NVX).astype(jnp.float32)
    col_part = (index % NVX).astype(jnp.float32)
    vel_x = (row_portion - middle) * spacing
    vel_y = (col_part - middle) * spacing
    return (vel_x, vel_y)


def iota(shape, dim):
    return lax.broadcasted_iota(jnp.int32, shape, dim)


def slot_order(slot):
    return lax.rem(slot, 2) * 2 + lax.div(slot, 2)


def entries_body(local, sources, here_ref, _density, _kind, hi_ref, lo_ref):
    me = here_ref[0]
    count = here_ref[1]
    groups = local // GROUP
    rows = 16
    lane = iota((1, LANES), 1)
    slot = slot_order(lane // HALF)
    vy = ((lane % HALF).astype(jnp.float32) - middle) * spacing
    out_x = [(me * local + g * GROUP + slot).astype(jnp.float32) for g in range(groups)]
    out_x = [(x - middle) * spacing for x in out_x]
    out_sq = [x * x + vy * vy for x in out_x]
    out_gauss = [jnp.exp(s * -0.25) for s in out_sq]

    def one(index, carry):
        source = lax.div(index, GROUP)
        r = lax.rem(index, GROUP)
        first = lax.rem(me + source, count) * local
        in_x_sq = []
        in_x_gauss = []
        for k in range(groups):
            wx = jnp.full((1, LANES), first + k * GROUP + r, jnp.int32).astype(jnp.float32)
            wx = (wx - middle) * spacing
            in_x_sq.append(wx * wx)
            in_x_gauss.append(jnp.exp(wx * wx * -0.25) * (0.5 / EXPONENT))
        for half in range(HALF // rows):
            wy = (iota((rows, LANES), 0) + half * rows).astype(jnp.float32)
            wy = (wy - middle) * spacing
            in_y_sq = EXPONENT * wy * wy
            in_y_gauss = jnp.exp(wy * wy * -0.25)
            dy_same = EXPONENT * ((vy - wy) ** 2 + spacing * spacing)
            dy_flip = EXPONENT * ((vy + wy) ** 2 + spacing * spacing)
            for m in range(1 - groups, groups):
                apart = (me * local - first + m * GROUP - r + slot).astype(jnp.float32) * spacing
                dx_sq = EXPONENT * apart * apart
                tables = []
                for dy in (dy_same, dy_flip):
                    distance = dx_sq + dy
                    inverse = lax.rsqrt(distance)
                    tables.append((distance, inverse, inverse * inverse))
                for g in range(max(0, m), min(groups, groups + m)):
                    k = g - m
                    energy = EXPONENT * (out_sq[g] - in_x_sq[k]) - in_y_sq
                    energy_sq = energy * energy
                    gauss = (out_gauss[g] * in_x_gauss[k]) * in_y_gauss
                    same, flip = (
                        inverse * (jnp.exp2(-distance - energy_sq * inverse_sq) - distance * gauss)
                        for distance, inverse, inverse_sq in tables
                    )
                    start = (k * GROUP + slot_order(r)) * HALF + half * rows
                    at = pl.ds(pl.multiple_of(start, rows), rows)
                    cols = slice(g * LANES, (g + 1) * LANES)
                    for parity, value in ((0, same + flip), (1, same - flip)):
                        high = value.astype(jnp.bfloat16)
                        hi_ref[source, parity, at, cols] = high
                        lo_ref[source, parity, at, cols] = (value - high.astype(jnp.float32)).astype(jnp.bfloat16)
        return carry

    lax.fori_loop(0, sources * GROUP, one, 0)


def make_entries(here, density, kind, local, sources):
    size = local * HALF
    count = sources * 2 * size * size
    shape = pltpu.VMEM((sources, 2, size, size), jnp.bfloat16)
    return pl.pallas_call(
        functools.partial(entries_body, local, sources),
        in_specs=[SCALARS, WHOLE, WHOLE],
        out_specs=[WHOLE, WHOLE],
        out_shape=[shape, shape],
        compiler_params=room(6),
        cost_estimate=pl.CostEstimate(flops=20 * count, bytes_accessed=4 * count, transcendentals=2 * count),
        name="kernel_entries",
    )(here, in_vmem(density), in_vmem(kind))


def minmod(a, b):
    return jnp.maximum(jnp.minimum(a, b), 0.0) + jnp.minimum(jnp.maximum(a, b), 0.0)


def fold_masks(rows):
    lane = iota((rows, LANES), 1)
    slot = lane // HALF
    even = slot % 2 == 0
    turned = jnp.where(even, 2 - slot, slot) * HALF + (HALF - 1) - lane % HALF
    return even, turned


def folded(a, b, even, turned):
    near = jnp.where(even, a, b)
    far = pltpu.roll(jnp.where(even, b, a), HALF, 1)
    lower = jnp.where(even, near, far)
    upper = jnp.take_along_axis(jnp.where(even, far, near), turned, axis=1)
    return lower + upper, lower - upper


def unfolded(lower, upper, even, turned):
    upper = jnp.take_along_axis(upper, turned, axis=1)
    near = jnp.where(even, lower, upper)
    far = pltpu.roll(jnp.where(even, upper, lower), LANES - HALF, 1)
    return jnp.where(even, near, far), jnp.where(even, far, near)


def transport_body(wide, rows_x, here_ref, field_ref, xhalo_ref, ylo_ref, yhi_ref, _hi, _lo, adv_ref, fold_ref, low_edge, high_edge):
    cells, local_len = field_ref.shape
    rows_y = cells // rows_x
    has_low = here_ref[2] > 0
    has_high = here_ref[3] > 0
    at_y = iota((rows_y, wide), 0)
    first_y = at_y == 0
    last_y = at_y == rows_y - 1
    even, turned = fold_masks(rows_y)

    def chunk(c, carry):
        cols = pl.ds(pl.multiple_of(c * wide, wide), wide)
        vx, vy = velocity_parts(here_ref[0] * local_len + c * wide + iota((1, wide), 1))
        ax = time_step * vx
        ay = time_step * vy
        bx = 0.5 * jnp.abs(ax) * (1.0 - jnp.abs(ax))
        by = 0.5 * jnp.abs(ay) * (1.0 - jnp.abs(ay))
        ahead_x = ax > 0
        ahead_y = ay > 0

        def face_y(f0, f1, f2):
            return ay * f1 + by * minmod(f1 - f0, f2 - f1)

        for x in range(rows_x):
            low_edge[x : x + 1] = field_ref[x * rows_y : x * rows_y + 1, cols]
            high_edge[x : x + 1] = field_ref[(x + 1) * rows_y - 1 : (x + 1) * rows_y, cols]
        low_edge[...] = face_y(ylo_ref[0, :, cols], ylo_ref[1, :, cols], low_edge[...])
        high_edge[...] = face_y(high_edge[...], yhi_ref[0, :, cols], yhi_ref[1, :, cols])

        def row(i):
            if i < 0:
                return jnp.where(has_low, xhalo_ref[i + 2, :, cols], 0.0)
            if i >= rows_x:
                return jnp.where(has_high, xhalo_ref[i - rows_x, :, cols], 0.0)
            return field_ref[i * rows_y : (i + 1) * rows_y, cols]

        near = [row(-2), row(-1), row(0)]
        low, high = near[1] - near[0], near[2] - near[1]
        face = [ax * near[1] + bx * minmod(low, high)]
        for i in range(rows_x + 1):
            near = [near[1], near[2], row(i + 1)]
            low, high = high, near[2] - near[1]
            face.append(ax * near[1] + bx * minmod(low, high))
            if i == 0:
                continue
            x = i - 1
            here = near[0]
            row_term = jnp.where(ahead_x, face[x + 1] - face[x], face[x + 2] - face[x + 1])
            below = jnp.where(first_y, ylo_ref[1, x : x + 1, cols], pltpu.roll(here, 1, 0))
            above = jnp.where(last_y, yhi_ref[0, x : x + 1, cols], pltpu.roll(here, rows_y - 1, 0))
            mine = face_y(below, here, above)
            mine_below = jnp.where(first_y, low_edge[x : x + 1], pltpu.roll(mine, 1, 0))
            mine_above = jnp.where(last_y, high_edge[x : x + 1], pltpu.roll(mine, rows_y - 1, 0))
            col_term = jnp.where(ahead_y, mine - mine_below, mine_above - mine)
            moved = here - row_term - col_term
            at = slice(x * rows_y, (x + 1) * rows_y)
            adv_ref[at, cols] = moved
            for part in range(wide // (2 * LANES)):
                first = 2 * part * LANES
                both = folded(moved[:, first : first + LANES], moved[:, first + LANES : first + 2 * LANES], even, turned)
                to = pl.ds(pl.multiple_of(c * (wide // 2) + part * LANES, LANES), LANES)
                fold_ref[0, at, to], fold_ref[1, at, to] = both
        return carry

    lax.fori_loop(0, local_len // wide, chunk, 0)


def transport(here, rows_x, field, xhalo, ylo, yhi, entries):
    cells, local_len = field.shape
    wide = 4 * LANES
    return pl.pallas_call(
        functools.partial(transport_body, wide, rows_x),
        in_specs=[SCALARS] + [WHOLE] * 6,
        out_specs=[WHOLE] * 2,
        out_shape=[pltpu.VMEM(field.shape, jnp.float32), pltpu.VMEM((2, cells, local_len // 2), jnp.float32)],
        scratch_shapes=[pltpu.VMEM((rows_x, wide), jnp.float32)] * 2,
        compiler_params=room(6),
        cost_estimate=pl.CostEstimate(flops=40 * cells * local_len, bytes_accessed=16 * cells * local_len, transcendentals=0),
        name="transport",
    )(here, in_vmem(field), in_vmem(xhalo), in_vmem(ylo), in_vmem(yhi), in_vmem(entries[0]), in_vmem(entries[1]))


def split_into(value_ref, high, low):
    for parity in range(2):
        value = value_ref[parity]
        rounded = value.astype(jnp.bfloat16)
        high[parity] = rounded
        low[parity] = (value - rounded.astype(jnp.float32)).astype(jnp.bfloat16)


def product(high, low, hi_ref, lo_ref, source, parity, cols):
    dot = functools.partial(jnp.dot, preferred_element_type=jnp.float32)
    tile = hi_ref[source, parity, :, cols]
    return dot(high[parity], tile) + (dot(low[parity], tile) + dot(high[parity], lo_ref[source, parity, :, cols]))


def own_body(wide, fold_ref, hi_ref, lo_ref, out_ref, high, low):
    split_into(fold_ref, high, low)
    for j in range(fold_ref.shape[2] // wide):
        cols = slice(j * wide, (j + 1) * wide)
        for parity in range(2):
            out_ref[parity, :, cols] = product(high, low, hi_ref, lo_ref, 0, parity, cols)


def own_gain(fold, entries):
    _, cells, size = fold.shape
    return pl.pallas_call(
        functools.partial(own_body, 2 * LANES),
        in_specs=[WHOLE] * 3,
        out_specs=WHOLE,
        out_shape=pltpu.VMEM(fold.shape, jnp.float32),
        scratch_shapes=[pltpu.VMEM(fold.shape, jnp.bfloat16)] * 2,
        compiler_params=room(8),
        cost_estimate=pl.CostEstimate(flops=12 * cells * size * size, bytes_accessed=8 * size * size + 16 * cells * size, transcendentals=0),
        name="own_gain",
    )(in_vmem(fold), in_vmem(entries[0]), in_vmem(entries[1]))


def collide_body(
    wide, rows_x, last, here_ref, fold_ref, hi_ref, lo_ref, part_ref, adv_ref, density_ref, type_ref, inflow_ref, *rest
):
    if last:
        out_ref, high, low, field, sems = rest
    else:
        field, up_ref, down_ref, xsend_ref, high, low = rest
    cells, local_len = adv_ref.shape
    rows_y = cells // rows_x
    split_into(fold_ref, high, low)
    even_slot, turned = fold_masks(cells)
    rate = jnp.broadcast_to(collision_rate * density_ref[...], (cells, LANES))
    gain_rate = rate * ENTRY_SCALE
    kind = jnp.broadcast_to(type_ref[...], (cells, LANES))
    wall = kind == 1
    inlet = kind == 2
    copies = []
    for j in range(local_len // (2 * wide)):
        cols = slice(j * wide, (j + 1) * wide)
        even, odd = (part_ref[p, :, cols] + product(high, low, hi_ref, lo_ref, 1, p, cols) for p in range(2))
        lower = even + odd
        upper = even - odd
        for part in range(wide // LANES):
            group = slice(part * LANES, (part + 1) * LANES)
            for side, gain in enumerate(unfolded(lower[:, group], upper[:, group], even_slot, turned)):
                first = 2 * (j * wide + part * LANES) + side * LANES
                at = slice(first, first + LANES)
                vx, vy = velocity_parts(here_ref[0] * local_len + first + iota((1, LANES), 1))
                nu = 1.0 + (vx * vx + vy * vy) / 8.0
                moved = adv_ref[:, at]
                done = moved + (gain_rate * gain - rate * (nu * moved))
                field[:, at] = jnp.where(wall, 0.0, jnp.where(inlet, inflow_ref[:, at], done))
        span = slice(2 * j * wide, 2 * (j + 1) * wide)
        if last:
            copy = pltpu.make_async_copy(field.at[:, span], out_ref.at[:, span], sems.at[j])
            copy.start()
            copies.append(copy)
        else:
            for layer in range(2):
                for x in range(rows_x):
                    first = x * rows_y + layer
                    down_ref[layer, x : x + 1, span] = field[first : first + 1, span]
                    first = (x + 1) * rows_y - 2 + layer
                    up_ref[layer, x : x + 1, span] = field[first : first + 1, span]
                first_row = field[layer * rows_y : (layer + 1) * rows_y, span]
                last_row = field[(rows_x - 2 + layer) * rows_y : (rows_x - 1 + layer) * rows_y, span]
                xsend_ref[layer, :, span] = jnp.where(here_ref[3] > 0, last_row, first_row)
    for copy in copies:
        copy.wait()


def collide(here, rows_x, fold, entries, part, advected, density, kind, inflow, last):
    _, cells, size = fold.shape
    local_len = advected.shape[1]
    wide = 2 * LANES
    halves = [pltpu.VMEM(fold.shape, jnp.bfloat16)] * 2
    if last:
        out_specs = pl.BlockSpec(memory_space=pl.ANY)
        out_shape = jax.ShapeDtypeStruct(advected.shape, jnp.float32)
        scratch = halves + [pltpu.VMEM(advected.shape, jnp.float32), pltpu.SemaphoreType.DMA((size // wide,))]
    else:
        edge_y = pltpu.VMEM((2, rows_x, local_len), jnp.float32)
        edge_x = pltpu.VMEM((2, cells // rows_x, local_len), jnp.float32)
        out_specs = [WHOLE] * 4
        out_shape = [pltpu.VMEM(advected.shape, jnp.float32), edge_y, edge_y, edge_x]
        scratch = halves
    return pl.pallas_call(
        functools.partial(collide_body, wide, rows_x, last),
        in_specs=[SCALARS] + [WHOLE] * 8,
        out_specs=out_specs,
        out_shape=out_shape,
        scratch_shapes=scratch,
        compiler_params=room(12),
        cost_estimate=pl.CostEstimate(flops=12 * cells * size * size, bytes_accessed=8 * size * size + 32 * cells * size, transcendentals=0),
        name="collide",
    )(here, in_vmem(fold), in_vmem(entries[0]), in_vmem(entries[1]), in_vmem(part), in_vmem(advected), density, kind, inflow)


def shifted(block, axis, by):
    count = lax.axis_size(axis)
    return lax.ppermute(block, axis, [(i, i + by) for i in range(count) if 0 <= i + by < count])


def per_device(distribution, density, cell_type, inflow):
    rows_x, rows_y, local_len = distribution.shape
    cells = rows_x * rows_y
    vert = lax.axis_index("vert")
    verts = lax.axis_size("vert")
    at_x = lax.axis_index("gx")
    size_x = lax.axis_size("gx")
    assert size_x == 2 and verts == 2
    here = jnp.stack([vert, jnp.int32(verts), (at_x > 0).astype(jnp.int32), (at_x < size_x - 1).astype(jnp.int32)])
    column_density = density.reshape(cells, 1)
    column_type = cell_type.reshape(cells, 1)
    row_inflow = inflow.reshape(1, local_len)
    swap = [(0, 1), (1, 0)]
    up = jnp.transpose(distribution[:, -2:], (1, 0, 2))
    down = jnp.transpose(distribution[:, :2], (1, 0, 2))
    send_x = jnp.where(at_x == 0, distribution[-2:], distribution[:2])
    field = distribution.reshape(cells, local_len)
    entries = None
    for step in range(STEPS):
        last = step == STEPS - 1
        ylo = shifted(up, "gy", 1)
        yhi = shifted(down, "gy", -1)
        xhalo = lax.ppermute(send_x, "gx", swap)
        if entries is None:
            entries = make_entries(here, column_density, column_type, local_len // NVX, verts)
        advected, fold = transport(here, rows_x, field, xhalo, ylo, yhi, entries)
        other = lax.ppermute(fold, "vert", swap)
        part = own_gain(fold, entries)
        out = collide(here, rows_x, other, entries, part, advected, column_density, column_type, row_inflow, last)
        if not last:
            field, up, down, send_x = out
    return out.reshape(rows_x, rows_y, local_len)


def solution(mesh):
    placed = (P("gx", "gy", "vert"), P("gx", "gy"), P("gx", "gy"), P("vert"))
    return jax.shard_map(
        per_device, mesh=mesh, in_specs=placed, out_specs=P("gx", "gy", "vert"), check_vma=False
    )
```

profile of v0, /device:TPU:19, one launch (start us, length us, event | category | flops | bytes accessed | tf_op | source)
XLA Modules:
  0.0 67.3 jit_solution(7738181901807237419)
XLA Ops:
  0.0 0.0 copy-start.2
  0.0 0.0 copy-start.3
  0.0 1.1 %slice_select_fusion = f32[2,16,2048]{2,1,0:T(8,128)S(1)} fusion(f32[16,16,2048]{2,1,0:T(8,128)} %param.4, pred[]{:T(512)S(6)} %eq.3), kind=kLoop, calls=%fused_computation.2 | loop fusion | flops 65536 | bytes 786433 | tf_op jit(solution)/shard_map/jit(_where)/select_n | solution.py:374
  1.1 0.3 collective-permute-start
  1.4 1.7 %fusion = (f32[16,2,2048]{2,1,0:T(2,128)S(1)}, f32[16,2,2048]{2,1,0:T(2,128)S(1)}) fusion(f32[16,16,2048]{2,1,0:T(8,128)} %param.4), kind=kLoop, calls=%fused_computation.4 | loop fusion | bytes 1048576 | tf_op jit(solution)/shard_map/slice | solution.py:373
  3.2 0.2 copy.20
  3.3 3.1 %collective-permute-start.1 = (f32[2,16,2048]{2,1,0:T(8,128)S(1)}, f32[2,16,2048]{2,1,0:T(8,128)S(1)}, u32[]{:S(2)}, u32[]{:S(2)}) collective-permute-start(f32[2,16,2048]{2,1,0:T(8,128)S(1)} %bitcast.15), channel_id=1, source_target_pairs={{0,2},{2,4},{4,6},{6,8},{8,10},{10,12},{12,14},{1,3},{3,5},{5,7},{... | collective-permute-start | bytes 786440 | tf_op jit(solution)/shard_map/ppermute | solution.py:356
  6.5 0.2 copy.19
  6.6 3.0 %collective-permute-start.2 = (f32[2,16,2048]{2,1,0:T(8,128)S(1)}, f32[2,16,2048]{2,1,0:T(8,128)S(1)}, u32[]{:S(2)}, u32[]{:S(2)}) collective-permute-start(f32[2,16,2048]{2,1,0:T(8,128)S(1)} %bitcast.16), channel_id=1, source_target_pairs={{2,0},{4,2},{6,4},{8,6},{10,8},{12,10},{14,12},{3,1},{5,3},{7,5},{... | collective-permute-start | bytes 786440 | tf_op jit(solution)/shard_map/ppermute | solution.py:356
  9.7 0.0 copy-done.2
  9.7 0.1 reshape.22._density.density_ref
  9.8 0.0 copy-done.3
  9.8 0.1 reshape.23._kind.type_ref
  9.9 0.1 pad_add_fusion.here_ref
  10.0 0.0 copy-start
  10.0 10.2 %kernel_entries.1 = (bf16[2,2,1024,1024]{3,2,1,0:T(8,128)(2,1)S(1)}, bf16[2,2,1024,1024]{3,2,1,0:T(8,128)(2,1)S(1)}) custom-call(s32[4]{0:T(128)S(1)} %pad_add_fusion.here_ref, f32[256,1]{1,0:T(8,128)S(1)} %reshape.22._density.density_ref, s32[256,1]{1,0:T(8,128)S(1)} %reshape.23._kind.type_ref), custom_call_target="tpu_custom_call" | custom-call | flops 83886080 | bytes 16777216 | tf_op jit(solution)/shard_map/kernel_entries/pallas_call | solution.py:120
  20.3 0.0 collective-permute-done.xhalo_ref
  20.3 0.0 collective-permute-done.1.ylo_ref
  20.3 0.0 collective-permute-done.2.yhi_ref
  20.3 0.0 copy-done
  20.3 4.2 %transport.2 = (f32[256,2048]{1,0:T(8,128)S(1)}, f32[2,256,1024]{2,1,0:T(8,128)S(1)}) custom-call(s32[4]{0:T(128)S(1)} %pad_add_fusion.here_ref, f32[256,2048]{1,0:T(8,128)S(1)} %bitcast.12, f32[2,16,2048]{2,1,0:T(8,128)S(1)} %collective-permute-done.xhalo_ref, f32[2,16,2048]{2,1,0:T(8,128)S(1)} %collective-permute-done.1.ylo_ref, ...), custom_call_target="tpu_custom_call" | custom-call | flops 20971520 | bytes 8388608 | tf_op jit(solution)/shard_map/transport/pallas_call | solution.py:228
  24.5 0.0 copy-start.1
  24.5 1.6 %collective-permute-start.3 = (f32[2,256,1024]{2,1,0:T(8,128)S(1)}, f32[2,256,1024]{2,1,0:T(8,128)S(1)}, u32[]{:S(2)}, u32[]{:S(2)}) collective-permute-start(f32[2,256,1024]{2,1,0:T(8,128)S(1)} %get-tuple-element.17.fold_ref), channel_id=1, source_target_pairs={{0,1},{1,0},{2,3},{3,2},{4,5},{5,4},{6,7},{7,6},{8,9},{9,8},{10,11... | collective-permute-start | bytes 6291464 | tf_op jit(solution)/shard_map/ppermute | solution.py:385
  26.1 3.6 %own_gain.2.part_ref = f32[2,256,1024]{2,1,0:T(8,128)S(1)} custom-call(f32[2,256,1024]{2,1,0:T(8,128)S(1)} %get-tuple-element.17.fold_ref, bf16[2,2,1024,1024]{3,2,1,0:T(8,128)(2,1)S(1)} %get-tuple-element.15._hi.hi_ref, bf16[2,2,1024,1024]{3,2,1,0:T(8,128)(2,1)S(1)} %get-tuple-element.16._lo.lo_ref), custom_call_target="tpu_custom_call" | custom-call | flops 3221225472 | bytes 12582912 | tf_op jit(solution)/shard_map/own_gain/pallas_call | solution.py:264
  29.7 0.2 collective-permute-done.3.fold_ref
  29.9 0.0 copy-done.1
  29.9 5.0 %collide.2 = (f32[256,2048]{1,0:T(8,128)S(1)}, f32[2,16,2048]{2,1,0:T(8,128)S(1)}, f32[2,16,2048]{2,1,0:T(8,128)S(1)}, f32[2,16,2048]{2,1,0:T(8,128)S(1)}) custom-call(s32[4]{0:T(128)S(1)} %pad_add_fusion.here_ref, f32[2,256,1024]{2,1,0:T(8,128)S(1)} %collective-permute-done.3.fold_ref, bf16[2,2,1024,1024]{3,2,1,0:T(8,128)(2,1)S(1)} %get-tuple-element.15._hi.hi_ref, ...), custom_call_target="tpu_custom_call" | custom-call | flops 3221225472 | bytes 16777216 | tf_op jit(solution)/shard_map/collide/pallas_call | solution.py:342
  34.9 1.3 %collective-permute-start.4 = (f32[2,16,2048]{2,1,0:T(8,128)S(1)}, f32[2,16,2048]{2,1,0:T(8,128)S(1)}, u32[]{:S(2)}, u32[]{:S(2)}) collective-permute-start(f32[2,16,2048]{2,1,0:T(8,128)S(1)} %get-tuple-element.20), channel_id=1, source_target_pairs={{0,16},{16,0},{1,17},{17,1},{2,18},{18,2},{3,19},{19,3},{4,20},{20... | collective-permute-start | bytes 786440 | tf_op jit(solution)/shard_map/ppermute | solution.py:381
  36.2 2.2 %collective-permute-start.5 = (f32[2,16,2048]{2,1,0:T(8,128)S(1)}, f32[2,16,2048]{2,1,0:T(8,128)S(1)}, u32[]{:S(2)}, u32[]{:S(2)}) collective-permute-start(f32[2,16,2048]{2,1,0:T(8,128)S(1)} %get-tuple-element.21), channel_id=1, source_target_pairs={{0,2},{2,4},{4,6},{6,8},{8,10},{10,12},{12,14},{1,3},{3,5},{5,7},{... | collective-permute-start | bytes 786440 | tf_op jit(solution)/shard_map/ppermute | solution.py:356
  38.5 4.1 %collective-permute-start.6 = (f32[2,16,2048]{2,1,0:T(8,128)S(1)}, f32[2,16,2048]{2,1,0:T(8,128)S(1)}, u32[]{:S(2)}, u32[]{:S(2)}) collective-permute-start(f32[2,16,2048]{2,1,0:T(8,128)S(1)} %get-tuple-element.22), channel_id=1, source_target_pairs={{2,0},{4,2},{6,4},{8,6},{10,8},{12,10},{14,12},{3,1},{5,3},{7,5},{... | collective-permute-start | bytes 786440 | tf_op jit(solution)/shard_map/ppermute | solution.py:356
  42.6 0.0 collective-permute-done.4.xhalo_ref
  42.6 3.6 %collective-permute-done.5.ylo_ref = f32[2,16,2048]{2,1,0:T(8,128)S(1)} collective-permute-done((f32[2,16,2048]{2,1,0:T(8,128)S(1)}, f32[2,16,2048]{2,1,0:T(8,128)S(1)}, u32[]{:S(2)}, u32[]{:S(2)}) %collective-permute-start.5) | collective-permute-done | bytes 262176 | tf_op jit(solution)/shard_map/ppermute | solution.py:356
  46.2 6.6 %collective-permute-done.6.yhi_ref = f32[2,16,2048]{2,1,0:T(8,128)S(1)} collective-permute-done((f32[2,16,2048]{2,1,0:T(8,128)S(1)}, f32[2,16,2048]{2,1,0:T(8,128)S(1)}, u32[]{:S(2)}, u32[]{:S(2)}) %collective-permute-start.6) | collective-permute-done | bytes 262176 | tf_op jit(solution)/shard_map/ppermute | solution.py:356
  52.8 4.2 %transport.3 = (f32[256,2048]{1,0:T(8,128)S(1)}, f32[2,256,1024]{2,1,0:T(8,128)S(1)}) custom-call(s32[4]{0:T(128)S(1)} %pad_add_fusion.here_ref, f32[256,2048]{1,0:T(8,128)S(1)} %get-tuple-element.19.field_ref, f32[2,16,2048]{2,1,0:T(8,128)S(1)} %collective-permute-done.4.xhalo_ref, f32[2,16,2048]{2,1,0:T(8,128)S(1)} %collective-permute-done.5.ylo_ref, ...), custom_call_target="tpu_custom_call" | custom-call | flops 20971520 | bytes 8388608 | tf_op jit(solution)/shard_map/transport/pallas_call | solution.py:228
  57.0 0.5 collective-permute-start.7
  57.6 3.6 %own_gain.3.part_ref = f32[2,256,1024]{2,1,0:T(8,128)S(1)} custom-call(f32[2,256,1024]{2,1,0:T(8,128)S(1)} %get-tuple-element.23.fold_ref, bf16[2,2,1024,1024]{3,2,1,0:T(8,128)(2,1)S(1)} %get-tuple-element.15._hi.hi_ref, bf16[2,2,1024,1024]{3,2,1,0:T(8,128)(2,1)S(1)} %get-tuple-element.16._lo.lo_ref), custom_call_target="tpu_custom_call" | custom-call | flops 3221225472 | bytes 12582912 | tf_op jit(solution)/shard_map/own_gain/pallas_call | solution.py:264
  61.2 0.1 collective-permute-done.7.fold_ref
  61.4 5.7 %collide.3 = f32[256,2048]{1,0:T(8,128)} custom-call(s32[4]{0:T(128)S(1)} %pad_add_fusion.here_ref, f32[2,256,1024]{2,1,0:T(8,128)S(1)} %collective-permute-done.7.fold_ref, bf16[2,2,1024,1024]{3,2,1,0:T(8,128)(2,1)S(1)} %get-tuple-element.15._hi.hi_ref, bf16[2,2,1024,1024]{3,2,1,0:T(8,128)(2,1)S(1)} %get-tuple-element.16._lo.lo_ref, ...), custom_call_target="tpu_custom_call" | custom-call | flops 3221225472 | bytes 16777216 | tf_op jit(solution)/shard_map/collide/pallas_call | solution.py:342
Async XLA Ops:
  0.0 9.7 %copy-start.2 = (f32[16,16]{1,0:T(8,128)S(1)}, f32[16,16]{1,0:T(8,128)}, u32[]{:S(2)}) copy-start(f32[16,16]{1,0:T(8,128)} %param.5) | copy-start | bytes 3076
  0.0 9.8 %copy-start.3 = (s32[16,16]{1,0:T(8,128)S(1)}, s32[16,16]{1,0:T(8,128)}, u32[]{:S(2)}) copy-start(s32[16,16]{1,0:T(8,128)} %param.6) | copy-start | bytes 3076
  1.1 19.2 %collective-permute-start = (f32[2,16,2048]{2,1,0:T(8,128)S(1)}, f32[2,16,2048]{2,1,0:T(8,128)S(1)}, u32[]{:S(2)}, u32[]{:S(2)}) collective-permute-start(f32[2,16,2048]{2,1,0:T(8,128)S(1)} %slice_select_fusion), channel_id=1, source_target_pairs={{0,16},{16,0},{1,17},{17,1},{2,18},{18,2},{3,19},{19,3},{4,20},{20... | collective-permute-start | bytes 786440 | tf_op jit(solution)/shard_map/ppermute | solution.py:381
  3.3 17.0 %collective-permute-start.1 = (f32[2,16,2048]{2,1,0:T(8,128)S(1)}, f32[2,16,2048]{2,1,0:T(8,128)S(1)}, u32[]{:S(2)}, u32[]{:S(2)}) collective-permute-start(f32[2,16,2048]{2,1,0:T(8,128)S(1)} %bitcast.15), channel_id=1, source_target_pairs={{0,2},{2,4},{4,6},{6,8},{8,10},{10,12},{12,14},{1,3},{3,5},{5,7},{... | collective-permute-start | bytes 786440 | tf_op jit(solution)/shard_map/ppermute | solution.py:356
  6.6 13.6 %collective-permute-start.2 = (f32[2,16,2048]{2,1,0:T(8,128)S(1)}, f32[2,16,2048]{2,1,0:T(8,128)S(1)}, u32[]{:S(2)}, u32[]{:S(2)}) collective-permute-start(f32[2,16,2048]{2,1,0:T(8,128)S(1)} %bitcast.16), channel_id=1, source_target_pairs={{2,0},{4,2},{6,4},{8,6},{10,8},{12,10},{14,12},{3,1},{5,3},{7,5},{... | collective-permute-start | bytes 786440 | tf_op jit(solution)/shard_map/ppermute | solution.py:356
  10.0 10.3 %copy-start = (f32[16,16,2048]{2,1,0:T(8,128)S(1)}, f32[16,16,2048]{2,1,0:T(8,128)}, u32[]{:S(2)}) copy-start(f32[16,16,2048]{2,1,0:T(8,128)} %param.4) | copy-start | bytes 6291460
  24.5 5.4 %copy-start.1 = (f32[2048]{0:T(1024)S(1)}, f32[2048]{0:T(1024)}, u32[]{:S(2)}) copy-start(f32[2048]{0:T(1024)} %param.7) | copy-start | bytes 24580
  24.5 5.4 %collective-permute-start.3 = (f32[2,256,1024]{2,1,0:T(8,128)S(1)}, f32[2,256,1024]{2,1,0:T(8,128)S(1)}, u32[]{:S(2)}, u32[]{:S(2)}) collective-permute-start(f32[2,256,1024]{2,1,0:T(8,128)S(1)} %get-tuple-element.17.fold_ref), channel_id=1, source_target_pairs={{0,1},{1,0},{2,3},{3,2},{4,5},{5,4},{6,7},{7,6},{8,9},{9,8},{10,11... | collective-permute-start | bytes 6291464 | tf_op jit(solution)/shard_map/ppermute | solution.py:385
  34.9 7.6 %collective-permute-start.4 = (f32[2,16,2048]{2,1,0:T(8,128)S(1)}, f32[2,16,2048]{2,1,0:T(8,128)S(1)}, u32[]{:S(2)}, u32[]{:S(2)}) collective-permute-start(f32[2,16,2048]{2,1,0:T(8,128)S(1)} %get-tuple-element.20), channel_id=1, source_target_pairs={{0,16},{16,0},{1,17},{17,1},{2,18},{18,2},{3,19},{19,3},{4,20},{20... | collective-permute-start | bytes 786440 | tf_op jit(solution)/shard_map/ppermute | solution.py:381
  36.2 10.0 %collective-permute-start.5 = (f32[2,16,2048]{2,1,0:T(8,128)S(1)}, f32[2,16,2048]{2,1,0:T(8,128)S(1)}, u32[]{:S(2)}, u32[]{:S(2)}) collective-permute-start(f32[2,16,2048]{2,1,0:T(8,128)S(1)} %get-tuple-element.21), channel_id=1, source_target_pairs={{0,2},{2,4},{4,6},{6,8},{8,10},{10,12},{12,14},{1,3},{3,5},{5,7},{... | collective-permute-start | bytes 786440 | tf_op jit(solution)/shard_map/ppermute | solution.py:356
  38.5 14.4 %collective-permute-start.6 = (f32[2,16,2048]{2,1,0:T(8,128)S(1)}, f32[2,16,2048]{2,1,0:T(8,128)S(1)}, u32[]{:S(2)}, u32[]{:S(2)}) collective-permute-start(f32[2,16,2048]{2,1,0:T(8,128)S(1)} %get-tuple-element.22), channel_id=1, source_target_pairs={{2,0},{4,2},{6,4},{8,6},{10,8},{12,10},{14,12},{3,1},{5,3},{7,5},{... | collective-permute-start | bytes 786440 | tf_op jit(solution)/shard_map/ppermute | solution.py:356
  57.0 4.3 %collective-permute-start.7 = (f32[2,256,1024]{2,1,0:T(8,128)S(1)}, f32[2,256,1024]{2,1,0:T(8,128)S(1)}, u32[]{:S(2)}, u32[]{:S(2)}) collective-permute-start(f32[2,256,1024]{2,1,0:T(8,128)S(1)} %get-tuple-element.23.fold_ref), channel_id=1, source_target_pairs={{0,1},{1,0},{2,3},{3,2},{4,5},{5,4},{6,7},{7,6},{8,9},{9,8},{10,11... | collective-permute-start | bytes 6291464 | tf_op jit(solution)/shard_map/ppermute | solution.py:385
where the time goes:
time: 67.5 us; the launch traced here: 67.3 us
  Pallas kernels  36.7 us (54%)
  starting transfers between devices  16.2 us (24%)
  waiting for transfers between devices  10.6 us (16%)
  local copies, waits for them, and re-layouts  2.26 us (3%)
  other arithmetic  1.17 us (2%)
    ppermute x4, starting transfers between devices, shifted(): lax.ppermute(block, axis, [(i, i + by) for i in range(count) if 0 <= i +...  12.5 us
    pallas_call x2, Pallas kernels, collide(): pl.pallas_call(functools.partial(collide_body, wide, rows_x, last), in_sp...  10.8 us
    ppermute x4, waiting for transfers between devices, shifted(): lax.ppermute(block, axis, [(i, i + by) for i in range(count) if 0 <= i +...  10.3 us
    pallas_call x1, Pallas kernels, make_entries(): pl.pallas_call(functools.partial(entries_body, local, sources), in_specs=...  10.2 us
    pallas_call x2, Pallas kernels, transport(): pl.pallas_call(functools.partial(transport_body, wide, rows_x), in_specs=...  8.42 us
    pallas_call x2, Pallas kernels, own_gain(): pl.pallas_call(functools.partial(own_body, 2 * LANES), in_specs=[WHOLE] *...  7.24 us
    ppermute x2, starting transfers between devices, per_device(): other = lax.ppermute(fold, 'vert', swap)  2.12 us
    slice x1, local copies, waits for them, and re-layouts, per_device(): down = jnp.transpose(distribution[:, :2], (1, 0, 2))  1.74 us
  transfers between devices with their start and end apart: 8, of which 4 were waited for; matrix products, arithmetic and copies ran while one was open for 3% of the time, Pallas kernels for 26%

commit v1 on v0

--- a/solution.py
+++ b/solution.py
@@ -53,79 +53,139 @@
     return lax.rem(slot, 2) * 2 + lax.div(slot, 2)
 
 
-def entries_body(local, sources, here_ref, _density, _kind, hi_ref, lo_ref):
+def write_entries(local, here_ref, source, hi_ref, lo_ref, r, half):
     me = here_ref[0]
-    count = here_ref[1]
+    first = lax.rem(me + source, here_ref[1]) * local
     groups = local // GROUP
-    rows = 16
+    rows = HALF // 2
     lane = iota((1, LANES), 1)
     slot = slot_order(lane // HALF)
     vy = ((lane % HALF).astype(jnp.float32) - middle) * spacing
-    out_x = [(me * local + g * GROUP + slot).astype(jnp.float32) for g in range(groups)]
-    out_x = [(x - middle) * spacing for x in out_x]
-    out_sq = [x * x + vy * vy for x in out_x]
-    out_gauss = [jnp.exp(s * -0.25) for s in out_sq]
+    wy = (iota((rows, LANES), 0) + half * rows).astype(jnp.float32)
+    wy = (wy - middle) * spacing
+    in_y_sq = EXPONENT * wy * wy
+    in_y_gauss = jnp.exp(wy * wy * -0.25)
+    dy_same = EXPONENT * ((vy - wy) ** 2 + spacing * spacing)
+    dy_flip = EXPONENT * ((vy + wy) ** 2 + spacing * spacing)
+    out_sq, out_gauss, in_sq, in_gauss = [], [], [], []
+    for k in range(groups):
+        vx = ((me * local + k * GROUP + slot).astype(jnp.float32) - middle) * spacing
+        out_sq.append(EXPONENT * (vx * vx + vy * vy))
+        out_gauss.append(jnp.exp((vx * vx + vy * vy) * -0.25))
+        wx = jnp.full((1, LANES), first + k * GROUP + r, jnp.int32).astype(jnp.float32)
+        wx = (wx - middle) * spacing
+        in_sq.append(EXPONENT * wx * wx)
+        in_gauss.append(jnp.exp(wx * wx * -0.25) * (0.5 / EXPONENT))
+    for m in range(1 - groups, groups):
+        apart = (me * local - first + m * GROUP - r + slot).astype(jnp.float32) * spacing
+        dx_sq = EXPONENT * apart * apart
+        tables = []
+        for dy in (dy_same, dy_flip):
+            distance = dx_sq + dy
+            inverse = lax.rsqrt(distance)
+            tables.append((distance, inverse, inverse * inverse))
+        for g in range(max(0, m), min(groups, groups + m)):
+            k = g - m
+            energy = (out_sq[g] - in_sq[k]) - in_y_sq
+            energy_sq = energy * energy
+            gauss = (out_gauss[g] * in_gauss[k]) * in_y_gauss
+            same, flip = (
+                inverse * (jnp.exp2(-distance - energy_sq * inverse_sq) - distance * gauss)
+                for distance, inverse, inverse_sq in tables
+            )
+            start = (k * GROUP + slot_order(r)) * HALF + half * rows
+            at = pl.ds(pl.multiple_of(start, rows), rows)
+            cols = slice(g * LANES, (g + 1) * LANES)
+            for parity, value in ((0, same + flip), (1, same - flip)):
+                high = value.astype(jnp.bfloat16)
+                hi_ref[source, parity, at, cols] = high
+                lo_ref[source, parity, at, cols] = (value - high.astype(jnp.float32)).astype(jnp.bfloat16)
+
+
+def entries_body(local, sources, here_ref, *rest):
+    hi_ref, lo_ref = rest[-2:]
 
     def one(index, carry):
-        source = lax.div(index, GROUP)
-        r = lax.rem(index, GROUP)
-        first = lax.rem(me + source, count) * local
-        in_x_sq = []
-        in_x_gauss = []
-        for k in range(groups):
-            wx = jnp.full((1, LANES), first + k * GROUP + r, jnp.int32).astype(jnp.float32)
-            wx = (wx - middle) * spacing
-            in_x_sq.append(wx * wx)
-            in_x_gauss.append(jnp.exp(wx * wx * -0.25) * (0.5 / EXPONENT))
-        for half in range(HALF // rows):
-            wy = (iota((rows, LANES), 0) + half * rows).astype(jnp.float32)
-            wy = (wy - middle) * spacing
-            in_y_sq = EXPONENT * wy * wy
-            in_y_gauss = jnp.exp(wy * wy * -0.25)
-            dy_same = EXPONENT * ((vy - wy) ** 2 + spacing * spacing)
-            dy_flip = EXPONENT * ((vy + wy) ** 2 + spacing * spacing)
-            for m in range(1 - groups, groups):
-                apart = (me * local - first + m * GROUP - r + slot).astype(jnp.float32) * spacing
-                dx_sq = EXPONENT * apart * apart
-                tables = []
-                for dy in (dy_same, dy_flip):
-                    distance = dx_sq + dy
-                    inverse = lax.rsqrt(distance)
-                    tables.append((distance, inverse, inverse * inverse))
-                for g in range(max(0, m), min(groups, groups + m)):
-                    k = g - m
-                    energy = EXPONENT * (out_sq[g] - in_x_sq[k]) - in_y_sq
-                    energy_sq = energy * energy
-                    gauss = (out_gauss[g] * in_x_gauss[k]) * in_y_gauss
-                    same, flip = (
-                        inverse * (jnp.exp2(-distance - energy_sq * inverse_sq) - distance * gauss)
-                        for distance, inverse, inverse_sq in tables
-                    )
-                    start = (k * GROUP + slot_order(r)) * HALF + half * rows
-                    at = pl.ds(pl.multiple_of(start, rows), rows)
-                    cols = slice(g * LANES, (g + 1) * LANES)
-                    for parity, value in ((0, same + flip), (1, same - flip)):
-                        high = value.astype(jnp.bfloat16)
-                        hi_ref[source, parity, at, cols] = high
-                        lo_ref[source, parity, at, cols] = (value - high.astype(jnp.float32)).astype(jnp.bfloat16)
+        source = lax.div(index, 2 * GROUP)
+        left = lax.rem(index, 2 * GROUP)
+        write_entries(local, here_ref, source, hi_ref, lo_ref, lax.div(left, 2), lax.rem(left, 2))
         return carry
 
-    lax.fori_loop(0, sources * GROUP, one, 0)
-
-
-def make_entries(here, density, kind, local, sources):
+    lax.fori_loop(0, sources * 2 * GROUP, one, 0)
+
+
+def make_entries(here, local, sources, ahead_of):
     size = local * HALF
     count = sources * 2 * size * size
     shape = pltpu.VMEM((sources, 2, size, size), jnp.bfloat16)
     return pl.pallas_call(
         functools.partial(entries_body, local, sources),
-        in_specs=[SCALARS, WHOLE, WHOLE],
+        in_specs=[SCALARS] + [WHOLE] * len(ahead_of),
         out_specs=[WHOLE, WHOLE],
         out_shape=[shape, shape],
         compiler_params=room(6),
         cost_estimate=pl.CostEstimate(flops=20 * count, bytes_accessed=4 * count, transcendentals=2 * count),
         name="kernel_entries",
-    )(here, in_vmem(density), in_vmem(kind))
+    )(here, *map(in_vmem, ahead_of))
+
+
+def pack_far(far, ahead, low_half):
+    count = far.shape[0] // 2
+    if ahead:
+        return jnp.where(low_half, pltpu.roll(far[count:], LANES - HALF, 1), far[:count])
+    return jnp.where(low_half, far[:count], pltpu.roll(far[count:], HALF, 1))
+
+
+def unpack_far(packed, ahead):
+    shift = HALF if ahead else LANES - HALF
+    parts = [packed[:, i : i + LANES] for i in range(0, packed.shape[1], LANES)]
+    turned = jnp.concatenate([pltpu.roll(p, shift, 1) for p in parts], axis=1)
+    return jnp.concatenate([packed, turned], axis=0)
+
+
+def write_edges(here_ref, rows_x, field, span, up_ref, down_ref, xsend_ref, far_ref):
+    rows_y = field.shape[0] // rows_x
+    for layer in range(2):
+        first_row = field[layer * rows_y : (layer + 1) * rows_y, span]
+        last_row = field[(rows_x - 2 + layer) * rows_y : (rows_x - 1 + layer) * rows_y, span]
+        xsend_ref[layer, :, span] = jnp.where(here_ref[3] > 0, last_row, first_row)
+    low_half = iota((rows_x // 2, LANES), 1) % NVX < HALF
+    for ahead, to_ref, near, far in ((True, up_ref, rows_y - 1, rows_y - 2), (False, down_ref, 0, 1)):
+        for x in range(rows_x):
+            to_ref[x : x + 1, span] = field[x * rows_y + near : x * rows_y + near + 1, span]
+            far_ref[x : x + 1, span] = field[x * rows_y + far : x * rows_y + far + 1, span]
+        for i in range(span.start, span.stop, LANES):
+            at = slice(i, i + LANES)
+            to_ref[rows_x:, at] = pack_far(far_ref[:, at], ahead, low_half)
+
+
+def edge_shapes(rows_x, rows_y, local_len):
+    edge_y = pltpu.VMEM((rows_x + rows_x // 2, local_len), jnp.float32)
+    return [edge_y, edge_y, pltpu.VMEM((2, rows_y, local_len), jnp.float32)]
+
+
+def stage_body(wide, rows_x, here_ref, from_ref, field, up_ref, down_ref, xsend_ref, far_ref, sems):
+    spans = [slice(i, i + wide) for i in range(0, field.shape[1], wide)]
+    copies = [pltpu.make_async_copy(from_ref.at[:, s], field.at[:, s], sems.at[i]) for i, s in enumerate(spans)]
+    for copy in copies:
+        copy.start()
+    for copy, span in zip(copies, spans):
+        copy.wait()
+        write_edges(here_ref, rows_x, field, span, up_ref, down_ref, xsend_ref, far_ref)
+
+
+def stage(here, rows_x, field):
+    cells, local_len = field.shape
+    wide = local_len // 4
+    return pl.pallas_call(
+        functools.partial(stage_body, wide, rows_x),
+        in_specs=[SCALARS, pl.BlockSpec(memory_space=pltpu.HBM)],
+        out_specs=[WHOLE] * 4,
+        out_shape=[pltpu.VMEM(field.shape, jnp.float32)] + edge_shapes(rows_x, cells // rows_x, local_len),
+        scratch_shapes=[pltpu.VMEM((rows_x, local_len), jnp.float32), pltpu.SemaphoreType.DMA((4,))],
+        compiler_params=room(4),
+        name="stage",
+    )(here, pltpu.with_memory_space_constraint(field, pltpu.HBM))
 
 
 def minmod(a, b):
@@ -155,7 +215,8 @@
     return jnp.where(even, near, far), jnp.where(even, far, near)
 
 
-def transport_body(wide, rows_x, here_ref, field_ref, xhalo_ref, ylo_ref, yhi_ref, _hi, _lo, adv_ref, fold_ref, low_edge, high_edge):
+def transport_body(wide, rows_x, here_ref, field_ref, xhalo_ref, ylo_ref, yhi_ref, *rest):
+    adv_ref, fold_ref, low_edge, high_edge = rest[-4:]
     cells, local_len = field_ref.shape
     rows_y = cells // rows_x
     has_low = here_ref[2] > 0
@@ -181,8 +242,10 @@
         for x in range(rows_x):
             low_edge[x : x + 1] = field_ref[x * rows_y : x * rows_y + 1, cols]
             high_edge[x : x + 1] = field_ref[(x + 1) * rows_y - 1 : (x + 1) * rows_y, cols]
-        low_edge[...] = face_y(ylo_ref[0, :, cols], ylo_ref[1, :, cols], low_edge[...])
-        high_edge[...] = face_y(high_edge[...], yhi_ref[0, :, cols], yhi_ref[1, :, cols])
+        low_far = unpack_far(ylo_ref[rows_x:, cols], True)
+        high_far = unpack_far(yhi_ref[rows_x:, cols], False)
+        low_edge[...] = face_y(low_far, ylo_ref[:rows_x, cols], low_edge[...])
+        high_edge[...] = face_y(high_edge[...], yhi_ref[:rows_x, cols], high_far)
 
         def row(i):
             if i < 0:
@@ -203,8 +266,8 @@
             x = i - 1
             here = near[0]
             row_term = jnp.where(ahead_x, face[x + 1] - face[x], face[x + 2] - face[x + 1])
-            below = jnp.where(first_y, ylo_ref[1, x : x + 1, cols], pltpu.roll(here, 1, 0))
-            above = jnp.where(last_y, yhi_ref[0, x : x + 1, cols], pltpu.roll(here, rows_y - 1, 0))
+            below = jnp.where(first_y, ylo_ref[x : x + 1, cols], pltpu.roll(here, 1, 0))
+            above = jnp.where(last_y, yhi_ref[x : x + 1, cols], pltpu.roll(here, rows_y - 1, 0))
             mine = face_y(below, here, above)
             mine_below = jnp.where(first_y, low_edge[x : x + 1], pltpu.roll(mine, 1, 0))
             mine_above = jnp.where(last_y, high_edge[x : x + 1], pltpu.roll(mine, rows_y - 1, 0))
@@ -227,14 +290,14 @@
     wide = 4 * LANES
     return pl.pallas_call(
         functools.partial(transport_body, wide, rows_x),
-        in_specs=[SCALARS] + [WHOLE] * 6,
+        in_specs=[SCALARS] + [WHOLE] * (4 + len(entries)),
         out_specs=[WHOLE] * 2,
         out_shape=[pltpu.VMEM(field.shape, jnp.float32), pltpu.VMEM((2, cells, local_len // 2), jnp.float32)],
         scratch_shapes=[pltpu.VMEM((rows_x, wide), jnp.float32)] * 2,
-        compiler_params=room(6),
+        compiler_params=room(4),
         cost_estimate=pl.CostEstimate(flops=40 * cells * local_len, bytes_accessed=16 * cells * local_len, transcendentals=0),
         name="transport",
-    )(here, in_vmem(field), in_vmem(xhalo), in_vmem(ylo), in_vmem(yhi), in_vmem(entries[0]), in_vmem(entries[1]))
+    )(here, in_vmem(field), in_vmem(xhalo), in_vmem(ylo), in_vmem(yhi), *map(in_vmem, entries))
 
 
 def split_into(value_ref, high, low):
@@ -270,7 +333,7 @@
         compiler_params=room(8),
         cost_estimate=pl.CostEstimate(flops=12 * cells * size * size, bytes_accessed=8 * size * size + 16 * cells * size, transcendentals=0),
         name="own_gain",
-    )(in_vmem(fold), in_vmem(entries[0]), in_vmem(entries[1]))
+    )(in_vmem(fold), *map(in_vmem, entries))
 
 
 def collide_body(
@@ -279,7 +342,7 @@
     if last:
         out_ref, high, low, field, sems = rest
     else:
-        field, up_ref, down_ref, xsend_ref, high, low = rest
+        field, up_ref, down_ref, xsend_ref, high, low, far_ref = rest
     cells, local_len = adv_ref.shape
     rows_y = cells // rows_x
     split_into(fold_ref, high, low)
@@ -311,15 +374,7 @@
             copy.start()
             copies.append(copy)
         else:
-            for layer in range(2):
-                for x in range(rows_x):
-                    first = x * rows_y + layer
-                    down_ref[layer, x : x + 1, span] = field[first : first + 1, span]
-                    first = (x + 1) * rows_y - 2 + layer
-                    up_ref[layer, x : x + 1, span] = field[first : first + 1, span]
-                first_row = field[layer * rows_y : (layer + 1) * rows_y, span]
-                last_row = field[(rows_x - 2 + layer) * rows_y : (rows_x - 1 + layer) * rows_y, span]
-                xsend_ref[layer, :, span] = jnp.where(here_ref[3] > 0, last_row, first_row)
+            write_edges(here_ref, rows_x, field, span, up_ref, down_ref, xsend_ref, far_ref)
     for copy in copies:
         copy.wait()
 
@@ -334,11 +389,9 @@
         out_shape = jax.ShapeDtypeStruct(advected.shape, jnp.float32)
         scratch = halves + [pltpu.VMEM(advected.shape, jnp.float32), pltpu.SemaphoreType.DMA((size // wide,))]
     else:
-        edge_y = pltpu.VMEM((2, rows_x, local_len), jnp.float32)
-        edge_x = pltpu.VMEM((2, cells // rows_x, local_len), jnp.float32)
         out_specs = [WHOLE] * 4
-        out_shape = [pltpu.VMEM(advected.shape, jnp.float32), edge_y, edge_y, edge_x]
-        scratch = halves
+        out_shape = [pltpu.VMEM(advected.shape, jnp.float32)] + edge_shapes(rows_x, cells // rows_x, local_len)
+        scratch = halves + [pltpu.VMEM((rows_x, local_len), jnp.float32)]
     return pl.pallas_call(
         functools.partial(collide_body, wide, rows_x, last),
         in_specs=[SCALARS] + [WHOLE] * 8,
@@ -369,10 +422,7 @@
     column_type = cell_type.reshape(cells, 1)
     row_inflow = inflow.reshape(1, local_len)
     swap = [(0, 1), (1, 0)]
-    up = jnp.transpose(distribution[:, -2:], (1, 0, 2))
-    down = jnp.transpose(distribution[:, :2], (1, 0, 2))
-    send_x = jnp.where(at_x == 0, distribution[-2:], distribution[:2])
-    field = distribution.reshape(cells, local_len)
+    field, up, down, send_x = stage(here, rows_x, distribution.reshape(cells, local_len))
     entries = None
     for step in range(STEPS):
         last = step == STEPS - 1
@@ -380,7 +430,7 @@
         yhi = shifted(down, "gy", -1)
         xhalo = lax.ppermute(send_x, "gx", swap)
         if entries is None:
-            entries = make_entries(here, column_density, column_type, local_len // NVX, verts)
+            entries = make_entries(here, local_len // NVX, verts, [column_density, column_type])
         advected, fold = transport(here, rows_x, field, xhalo, ylo, yhi, entries)
         other = lax.ppermute(fold, "vert", swap)
         part = own_gain(fold, entries)

time: 67.5 us -> 64.6 us (0.957)
  Pallas kernels: 36.7 us -> 39.8 us
  waiting for transfers between devices: 10.6 us -> 7.8 us
  local copies, waits for them, and re-layouts: 2.26 us -> 0.2 us
  other arithmetic: 1.17 us -> 0.08 us
    pallas_call x0 -> x1, Pallas kernels: none -> 2.87 us  [stage(): pl.pallas_call(functools.partial(stage_body, wide, rows_x), in_specs=[SCA...]
    ppermute x4, waiting for transfers between devices: 10.3 us -> 7.46 us  [shifted(): lax.ppermute(block, axis, [(i, i + by) for i in range(count) if 0 <= i +...]
    slice x1 -> x0, local copies, waits for them, and re-layouts: 1.74 us -> none  [per_device(): down = jnp.transpose(distribution[:, :2], (1, 0, 2))]
    select_n x1 -> x0, other arithmetic: 1.08 us -> none  [per_device(): send_x = jnp.where(at_x == 0, distribution[-2:], distribution[:2])]
  transfers between devices with their start and end apart: 8 -> 8, of which waited for: 4 -> 4; matrix products, arithmetic and copies ran while one was open for 3% -> 0% of each run, Pallas kernels for 26% -> 27%
where the time goes in v1:
time: 64.6 us; the launch traced here: 64.4 us
  Pallas kernels  39.8 us (62%)
  starting transfers between devices  16.2 us (25%)
  waiting for transfers between devices  7.8 us (12%)
    ppermute x4, starting transfers between devices, shifted(): lax.ppermute(block, axis, [(i, i + by) for i in range(count) if 0 <= i +...  12.5 us
    pallas_call x2, Pallas kernels, collide(): pl.pallas_call(functools.partial(collide_body, wide, rows_x, last), in_sp...  10.9 us
    pallas_call x1, Pallas kernels, make_entries(): pl.pallas_call(functools.partial(entries_body, local, sources), in_specs=...  10.4 us
    pallas_call x2, Pallas kernels, transport(): pl.pallas_call(functools.partial(transport_body, wide, rows_x), in_specs=...  8.47 us
    ppermute x4, waiting for transfers between devices, shifted(): lax.ppermute(block, axis, [(i, i + by) for i in range(count) if 0 <= i +...  7.46 us
    pallas_call x2, Pallas kernels, own_gain(): pl.pallas_call(functools.partial(own_body, 2 * LANES), in_specs=[WHOLE] *...  7.22 us
    pallas_call x1, Pallas kernels, stage(): pl.pallas_call(functools.partial(stage_body, wide, rows_x), in_specs=[SCA...  2.87 us
    ppermute x2, starting transfers between devices, per_device(): other = lax.ppermute(fold, 'vert', swap)  2.13 us
  transfers between devices with their start and end apart: 8, of which 4 were waited for; matrix products, arithmetic and copies ran while one was open for 0% of the time, Pallas kernels for 27%

profile of v1, /device:TPU:19, one launch (start us, length us, event | category | flops | bytes accessed | tf_op | source)
XLA Modules:
  0.0 64.4 jit_solution(16152446128143120524)
XLA Ops:
  0.0 0.0 copy-start.1
  0.0 0.0 copy-start.2
  0.0 0.1 pad_add_fusion.here_ref
  0.1 2.9 %stage.1 = (f32[256,2048]{1,0:T(8,128)S(1)}, f32[24,2048]{1,0:T(8,128)}, f32[24,2048]{1,0:T(8,128)S(1)}, f32[2,16,2048]{2,1,0:T(8,128)S(1)}) custom-call(s32[4]{0:T(128)S(1)} %pad_add_fusion.here_ref, f32[256,2048]{1,0:T(8,128)} %bitcast.8), custom_call_target="tpu_custom_call" | custom-call | tf_op jit(solution)/shard_map/stage/pallas_call | solution.py:180
  3.0 0.3 collective-permute-start
  3.3 3.1 %collective-permute-start.1 = (f32[24,2048]{1,0:T(8,128)}, f32[24,2048]{1,0:T(8,128)S(1)}, u32[]{:S(2)}, u32[]{:S(2)}) collective-permute-start(f32[24,2048]{1,0:T(8,128)} %get-tuple-element.21), channel_id=1, source_target_pairs={{0,2},{2,4},{4,6},{6,8},{8,10},{10,12},{12,14},{1,3},{3,5},{5,7},{... | collective-permute-start | bytes 589832 | tf_op jit(solution)/shard_map/ppermute | solution.py:409
  6.4 3.0 %collective-permute-start.2 = (f32[24,2048]{1,0:T(8,128)S(1)}, f32[24,2048]{1,0:T(8,128)S(1)}, u32[]{:S(2)}, u32[]{:S(2)}) collective-permute-start(f32[24,2048]{1,0:T(8,128)S(1)} %get-tuple-element.22), channel_id=1, source_target_pairs={{2,0},{4,2},{6,4},{8,6},{10,8},{12,10},{14,12},{3,1},{5,3},{7,5},{... | collective-permute-start | bytes 589832 | tf_op jit(solution)/shard_map/ppermute | solution.py:409
  9.5 0.0 copy-done.1
  9.5 0.1 reshape.22.rest_0_.density_ref
  9.6 0.0 copy-done.2
  9.6 0.1 reshape.23.rest_1_.type_ref
  9.7 10.4 %kernel_entries.1 = (bf16[2,2,1024,1024]{3,2,1,0:T(8,128)(2,1)S(1)}, bf16[2,2,1024,1024]{3,2,1,0:T(8,128)(2,1)S(1)}) custom-call(s32[4]{0:T(128)S(1)} %pad_add_fusion.here_ref, f32[256,1]{1,0:T(8,128)S(1)} %reshape.22.rest_0_.density_ref, s32[256,1]{1,0:T(8,128)S(1)} %reshape.23.rest_1_.type_ref), custom_call_target="tpu_custom_call" | custom-call | flops 83886080 | bytes 16777216 | tf_op jit(solution)/shard_map/kernel_entries/pallas_call | solution.py:121
  20.1 0.0 collective-permute-done.1.ylo_ref
  20.1 0.0 collective-permute-done.2.yhi_ref
  20.1 0.0 collective-permute-done.xhalo_ref
  20.1 4.2 %transport.2 = (f32[256,2048]{1,0:T(8,128)S(1)}, f32[2,256,1024]{2,1,0:T(8,128)S(1)}) custom-call(s32[4]{0:T(128)S(1)} %pad_add_fusion.here_ref, f32[256,2048]{1,0:T(8,128)S(1)} %get-tuple-element.19.field_ref, f32[2,16,2048]{2,1,0:T(8,128)S(1)} %collective-permute-done.xhalo_ref, f32[24,2048]{1,0:T(8,128)S(1)} %collective-permute-done.1.ylo_ref, ...), custom_call_target="tpu_custom_call" | custom-call | flops 20971520 | bytes 8388608 | tf_op jit(solution)/shard_map/transport/pallas_call | solution.py:291
  24.3 0.0 copy-start
  24.3 1.6 %collective-permute-start.3 = (f32[2,256,1024]{2,1,0:T(8,128)S(1)}, f32[2,256,1024]{2,1,0:T(8,128)S(1)}, u32[]{:S(2)}, u32[]{:S(2)}) collective-permute-start(f32[2,256,1024]{2,1,0:T(8,128)S(1)} %get-tuple-element.25.fold_ref), channel_id=1, source_target_pairs={{0,1},{1,0},{2,3},{3,2},{4,5},{5,4},{6,7},{7,6},{8,9},{9,8},{10,11... | collective-permute-start | bytes 6291464 | tf_op jit(solution)/shard_map/ppermute | solution.py:435
  25.9 3.6 %own_gain.2.part_ref = f32[2,256,1024]{2,1,0:T(8,128)S(1)} custom-call(f32[2,256,1024]{2,1,0:T(8,128)S(1)} %get-tuple-element.25.fold_ref, bf16[2,2,1024,1024]{3,2,1,0:T(8,128)(2,1)S(1)} %get-tuple-element.23.rest_0_.hi_ref, bf16[2,2,1024,1024]{3,2,1,0:T(8,128)(2,1)S(1)} %get-tuple-element.24.rest_1_.lo_ref), custom_call_target="tpu_custom_call" | custom-call | flops 3221225472 | bytes 12582912 | tf_op jit(solution)/shard_map/own_gain/pallas_call | solution.py:327
  29.5 0.2 collective-permute-done.3.fold_ref
  29.7 0.0 copy-done
  29.7 5.1 %collide.2 = (f32[256,2048]{1,0:T(8,128)S(1)}, f32[24,2048]{1,0:T(8,128)S(1)}, f32[24,2048]{1,0:T(8,128)S(1)}, f32[2,16,2048]{2,1,0:T(8,128)S(1)}) custom-call(s32[4]{0:T(128)S(1)} %pad_add_fusion.here_ref, f32[2,256,1024]{2,1,0:T(8,128)S(1)} %collective-permute-done.3.fold_ref, bf16[2,2,1024,1024]{3,2,1,0:T(8,128)(2,1)S(1)} %get-tuple-element.23.rest_0_.hi_ref, ...), custom_call_target="tpu_custom_call" | custom-call | flops 3221225472 | bytes 16777216 | tf_op jit(solution)/shard_map/collide/pallas_call | solution.py:395
  34.8 1.3 %collective-permute-start.4 = (f32[2,16,2048]{2,1,0:T(8,128)S(1)}, f32[2,16,2048]{2,1,0:T(8,128)S(1)}, u32[]{:S(2)}, u32[]{:S(2)}) collective-permute-start(f32[2,16,2048]{2,1,0:T(8,128)S(1)} %get-tuple-element.28), channel_id=1, source_target_pairs={{0,16},{16,0},{1,17},{17,1},{2,18},{18,2},{3,19},{19,3},{4,20},{20... | collective-permute-start | bytes 786440 | tf_op jit(solution)/shard_map/ppermute | solution.py:431
  36.1 2.2 %collective-permute-start.5 = (f32[24,2048]{1,0:T(8,128)S(1)}, f32[24,2048]{1,0:T(8,128)S(1)}, u32[]{:S(2)}, u32[]{:S(2)}) collective-permute-start(f32[24,2048]{1,0:T(8,128)S(1)} %get-tuple-element.29), channel_id=1, source_target_pairs={{0,2},{2,4},{4,6},{6,8},{8,10},{10,12},{12,14},{1,3},{3,5},{5,7},{... | collective-permute-start | bytes 589832 | tf_op jit(solution)/shard_map/ppermute | solution.py:409
  38.3 4.1 %collective-permute-start.6 = (f32[24,2048]{1,0:T(8,128)S(1)}, f32[24,2048]{1,0:T(8,128)S(1)}, u32[]{:S(2)}, u32[]{:S(2)}) collective-permute-start(f32[24,2048]{1,0:T(8,128)S(1)} %get-tuple-element.30), channel_id=1, source_target_pairs={{2,0},{4,2},{6,4},{8,6},{10,8},{12,10},{14,12},{3,1},{5,3},{7,5},{... | collective-permute-start | bytes 589832 | tf_op jit(solution)/shard_map/ppermute | solution.py:409
  42.5 2.2 %collective-permute-done.5.ylo_ref = f32[24,2048]{1,0:T(8,128)S(1)} collective-permute-done((f32[24,2048]{1,0:T(8,128)S(1)}, f32[24,2048]{1,0:T(8,128)S(1)}, u32[]{:S(2)}, u32[]{:S(2)}) %collective-permute-start.5) | collective-permute-done | bytes 196640 | tf_op jit(solution)/shard_map/ppermute | solution.py:409
  44.7 5.2 %collective-permute-done.6.yhi_ref = f32[24,2048]{1,0:T(8,128)S(1)} collective-permute-done((f32[24,2048]{1,0:T(8,128)S(1)}, f32[24,2048]{1,0:T(8,128)S(1)}, u32[]{:S(2)}, u32[]{:S(2)}) %collective-permute-start.6) | collective-permute-done | bytes 196640 | tf_op jit(solution)/shard_map/ppermute | solution.py:409
  49.9 0.0 collective-permute-done.4.xhalo_ref
  49.9 4.3 %transport.3 = (f32[256,2048]{1,0:T(8,128)S(1)}, f32[2,256,1024]{2,1,0:T(8,128)S(1)}) custom-call(s32[4]{0:T(128)S(1)} %pad_add_fusion.here_ref, f32[256,2048]{1,0:T(8,128)S(1)} %get-tuple-element.27.field_ref, f32[2,16,2048]{2,1,0:T(8,128)S(1)} %collective-permute-done.4.xhalo_ref, f32[24,2048]{1,0:T(8,128)S(1)} %collective-permute-done.5.ylo_ref, ...), custom_call_target="tpu_custom_call" | custom-call | flops 20971520 | bytes 8388608 | tf_op jit(solution)/shard_map/transport/pallas_call | solution.py:291
  54.2 0.5 collective-permute-start.7
  54.7 3.6 %own_gain.3.part_ref = f32[2,256,1024]{2,1,0:T(8,128)S(1)} custom-call(f32[2,256,1024]{2,1,0:T(8,128)S(1)} %get-tuple-element.31.fold_ref, bf16[2,2,1024,1024]{3,2,1,0:T(8,128)(2,1)S(1)} %get-tuple-element.23.rest_0_.hi_ref, bf16[2,2,1024,1024]{3,2,1,0:T(8,128)(2,1)S(1)} %get-tuple-element.24.rest_1_.lo_ref), custom_call_target="tpu_custom_call" | custom-call | flops 3221225472 | bytes 12582912 | tf_op jit(solution)/shard_map/own_gain/pallas_call | solution.py:327
  58.4 0.2 collective-permute-done.7.fold_ref
  58.5 5.7 %collide.3 = f32[256,2048]{1,0:T(8,128)} custom-call(s32[4]{0:T(128)S(1)} %pad_add_fusion.here_ref, f32[2,256,1024]{2,1,0:T(8,128)S(1)} %collective-permute-done.7.fold_ref, bf16[2,2,1024,1024]{3,2,1,0:T(8,128)(2,1)S(1)} %get-tuple-element.23.rest_0_.hi_ref, bf16[2,2,1024,1024]{3,2,1,0:T(8,128)(2,1)S(1)} %get-tuple-element.24.rest_1_.lo_ref, ...), custom_call_target="tpu_custom_call" | custom-call | flops 3221225472 | bytes 16777216 | tf_op jit(solution)/shard_map/collide/pallas_call | solution.py:395
Async XLA Ops:
  0.0 9.5 %copy-start.1 = (f32[16,16]{1,0:T(8,128)S(1)}, f32[16,16]{1,0:T(8,128)}, u32[]{:S(2)}) copy-start(f32[16,16]{1,0:T(8,128)} %param.5) | copy-start | bytes 3076
  0.0 9.6 %copy-start.2 = (s32[16,16]{1,0:T(8,128)S(1)}, s32[16,16]{1,0:T(8,128)}, u32[]{:S(2)}) copy-start(s32[16,16]{1,0:T(8,128)} %param.6) | copy-start | bytes 3076
  3.0 17.2 %collective-permute-start = (f32[2,16,2048]{2,1,0:T(8,128)S(1)}, f32[2,16,2048]{2,1,0:T(8,128)S(1)}, u32[]{:S(2)}, u32[]{:S(2)}) collective-permute-start(f32[2,16,2048]{2,1,0:T(8,128)S(1)} %get-tuple-element.20), channel_id=1, source_target_pairs={{0,16},{16,0},{1,17},{17,1},{2,18},{18,2},{3,19},{19,3},{4,20},{20... | collective-permute-start | bytes 786440 | tf_op jit(solution)/shard_map/ppermute | solution.py:431
  3.3 16.8 %collective-permute-start.1 = (f32[24,2048]{1,0:T(8,128)}, f32[24,2048]{1,0:T(8,128)S(1)}, u32[]{:S(2)}, u32[]{:S(2)}) collective-permute-start(f32[24,2048]{1,0:T(8,128)} %get-tuple-element.21), channel_id=1, source_target_pairs={{0,2},{2,4},{4,6},{6,8},{8,10},{10,12},{12,14},{1,3},{3,5},{5,7},{... | collective-permute-start | bytes 589832 | tf_op jit(solution)/shard_map/ppermute | solution.py:409
  6.4 13.7 %collective-permute-start.2 = (f32[24,2048]{1,0:T(8,128)S(1)}, f32[24,2048]{1,0:T(8,128)S(1)}, u32[]{:S(2)}, u32[]{:S(2)}) collective-permute-start(f32[24,2048]{1,0:T(8,128)S(1)} %get-tuple-element.22), channel_id=1, source_target_pairs={{2,0},{4,2},{6,4},{8,6},{10,8},{12,10},{14,12},{3,1},{5,3},{7,5},{... | collective-permute-start | bytes 589832 | tf_op jit(solution)/shard_map/ppermute | solution.py:409
  24.3 5.4 %copy-start = (f32[2048]{0:T(1024)S(1)}, f32[2048]{0:T(1024)}, u32[]{:S(2)}) copy-start(f32[2048]{0:T(1024)} %param.7) | copy-start | bytes 24580
  24.3 5.4 %collective-permute-start.3 = (f32[2,256,1024]{2,1,0:T(8,128)S(1)}, f32[2,256,1024]{2,1,0:T(8,128)S(1)}, u32[]{:S(2)}, u32[]{:S(2)}) collective-permute-start(f32[2,256,1024]{2,1,0:T(8,128)S(1)} %get-tuple-element.25.fold_ref), channel_id=1, source_target_pairs={{0,1},{1,0},{2,3},{3,2},{4,5},{5,4},{6,7},{7,6},{8,9},{9,8},{10,11... | collective-permute-start | bytes 6291464 | tf_op jit(solution)/shard_map/ppermute | solution.py:435
  34.8 15.1 %collective-permute-start.4 = (f32[2,16,2048]{2,1,0:T(8,128)S(1)}, f32[2,16,2048]{2,1,0:T(8,128)S(1)}, u32[]{:S(2)}, u32[]{:S(2)}) collective-permute-start(f32[2,16,2048]{2,1,0:T(8,128)S(1)} %get-tuple-element.28), channel_id=1, source_target_pairs={{0,16},{16,0},{1,17},{17,1},{2,18},{18,2},{3,19},{19,3},{4,20},{20... | collective-permute-start | bytes 786440 | tf_op jit(solution)/shard_map/ppermute | solution.py:431
  36.1 8.6 %collective-permute-start.5 = (f32[24,2048]{1,0:T(8,128)S(1)}, f32[24,2048]{1,0:T(8,128)S(1)}, u32[]{:S(2)}, u32[]{:S(2)}) collective-permute-start(f32[24,2048]{1,0:T(8,128)S(1)} %get-tuple-element.29), channel_id=1, source_target_pairs={{0,2},{2,4},{4,6},{6,8},{8,10},{10,12},{12,14},{1,3},{3,5},{5,7},{... | collective-permute-start | bytes 589832 | tf_op jit(solution)/shard_map/ppermute | solution.py:409
  38.3 11.6 %collective-permute-start.6 = (f32[24,2048]{1,0:T(8,128)S(1)}, f32[24,2048]{1,0:T(8,128)S(1)}, u32[]{:S(2)}, u32[]{:S(2)}) collective-permute-start(f32[24,2048]{1,0:T(8,128)S(1)} %get-tuple-element.30), channel_id=1, source_target_pairs={{2,0},{4,2},{6,4},{8,6},{10,8},{12,10},{14,12},{3,1},{5,3},{7,5},{... | collective-permute-start | bytes 589832 | tf_op jit(solution)/shard_map/ppermute | solution.py:409
  54.2 4.3 %collective-permute-start.7 = (f32[2,256,1024]{2,1,0:T(8,128)S(1)}, f32[2,256,1024]{2,1,0:T(8,128)S(1)}, u32[]{:S(2)}, u32[]{:S(2)}) collective-permute-start(f32[2,256,1024]{2,1,0:T(8,128)S(1)} %get-tuple-element.31.fold_ref), channel_id=1, source_target_pairs={{0,1},{1,0},{2,3},{3,2},{4,5},{5,4},{6,7},{7,6},{8,9},{9,8},{10,11... | collective-permute-start | bytes 6291464 | tf_op jit(solution)/shard_map/ppermute | solution.py:435

commit v2 on v1

--- a/solution.py
+++ b/solution.py
@@ -29,6 +29,9 @@
 ENTRY_SCALE = grad_scale * spacing * spacing * math.sqrt(EXPONENT)
 
 
+SMALL = pl.CostEstimate(flops=1, bytes_accessed=1, transcendentals=0)
+
+
 def room(mib):
     return pltpu.CompilerParams(vmem_limit_bytes=mib * MIB)
 
@@ -53,78 +56,73 @@
     return lax.rem(slot, 2) * 2 + lax.div(slot, 2)
 
 
-def write_entries(local, here_ref, source, hi_ref, lo_ref, r, half):
+def entries_body(local, sources, here_ref, *rest):
+    hi_ref, lo_ref, energy_ref, gauss_ref = rest[-4:]
     me = here_ref[0]
-    first = lax.rem(me + source, here_ref[1]) * local
     groups = local // GROUP
-    rows = HALF // 2
+    rows = 8
     lane = iota((1, LANES), 1)
     slot = slot_order(lane // HALF)
     vy = ((lane % HALF).astype(jnp.float32) - middle) * spacing
-    wy = (iota((rows, LANES), 0) + half * rows).astype(jnp.float32)
-    wy = (wy - middle) * spacing
-    in_y_sq = EXPONENT * wy * wy
-    in_y_gauss = jnp.exp(wy * wy * -0.25)
-    dy_same = EXPONENT * ((vy - wy) ** 2 + spacing * spacing)
-    dy_flip = EXPONENT * ((vy + wy) ** 2 + spacing * spacing)
-    out_sq, out_gauss, in_sq, in_gauss = [], [], [], []
-    for k in range(groups):
-        vx = ((me * local + k * GROUP + slot).astype(jnp.float32) - middle) * spacing
-        out_sq.append(EXPONENT * (vx * vx + vy * vy))
-        out_gauss.append(jnp.exp((vx * vx + vy * vy) * -0.25))
-        wx = jnp.full((1, LANES), first + k * GROUP + r, jnp.int32).astype(jnp.float32)
-        wx = (wx - middle) * spacing
-        in_sq.append(EXPONENT * wx * wx)
-        in_gauss.append(jnp.exp(wx * wx * -0.25) * (0.5 / EXPONENT))
-    for m in range(1 - groups, groups):
-        apart = (me * local - first + m * GROUP - r + slot).astype(jnp.float32) * spacing
-        dx_sq = EXPONENT * apart * apart
-        tables = []
-        for dy in (dy_same, dy_flip):
-            distance = dx_sq + dy
-            inverse = lax.rsqrt(distance)
-            tables.append((distance, inverse, inverse * inverse))
-        for g in range(max(0, m), min(groups, groups + m)):
-            k = g - m
-            energy = (out_sq[g] - in_sq[k]) - in_y_sq
-            energy_sq = energy * energy
-            gauss = (out_gauss[g] * in_gauss[k]) * in_y_gauss
-            same, flip = (
-                inverse * (jnp.exp2(-distance - energy_sq * inverse_sq) - distance * gauss)
-                for distance, inverse, inverse_sq in tables
-            )
-            start = (k * GROUP + slot_order(r)) * HALF + half * rows
-            at = pl.ds(pl.multiple_of(start, rows), rows)
-            cols = slice(g * LANES, (g + 1) * LANES)
-            for parity, value in ((0, same + flip), (1, same - flip)):
-                high = value.astype(jnp.bfloat16)
-                hi_ref[source, parity, at, cols] = high
-                lo_ref[source, parity, at, cols] = (value - high.astype(jnp.float32)).astype(jnp.bfloat16)
-
-
-def entries_body(local, sources, here_ref, *rest):
-    hi_ref, lo_ref = rest[-2:]
 
     def one(index, carry):
-        source = lax.div(index, 2 * GROUP)
-        left = lax.rem(index, 2 * GROUP)
-        write_entries(local, here_ref, source, hi_ref, lo_ref, lax.div(left, 2), lax.rem(left, 2))
+        source = lax.div(index, GROUP)
+        r = lax.rem(index, GROUP)
+        first = lax.rem(me + source, here_ref[1]) * local
+        pair, lanes = iota((groups * groups, LANES), 0), iota((groups * groups, LANES), 1)
+        out_x = ((me * local + pair // groups * GROUP + slot_order(lanes // HALF)).astype(jnp.float32) - middle) * spacing
+        out_y = ((lanes % HALF).astype(jnp.float32) - middle) * spacing
+        in_x = ((first + pair % groups * GROUP + r).astype(jnp.float32) - middle) * spacing
+        out_sq, in_sq = out_x * out_x + out_y * out_y, in_x * in_x
+        energy_ref[...] = EXPONENT * (out_sq - in_sq)
+        gauss_ref[...] = jnp.exp((out_sq + in_sq) * -0.25) * (0.5 / EXPONENT)
+        for part in range(HALF // rows):
+            wy = ((iota((rows, LANES), 0) + part * rows).astype(jnp.float32) - middle) * spacing
+            in_y_sq = EXPONENT * wy * wy
+            in_y_gauss = jnp.exp(wy * wy * -0.25)
+            dy_same = EXPONENT * ((vy - wy) ** 2 + spacing * spacing)
+            dy_flip = EXPONENT * ((vy + wy) ** 2 + spacing * spacing)
+            for m in range(1 - groups, groups):
+                apart = (me * local - first + m * GROUP - r + slot).astype(jnp.float32) * spacing
+                dx_sq = EXPONENT * apart * apart
+                same_sq, flip_sq = dx_sq + dy_same, dx_sq + dy_flip
+                same_inv, flip_inv = lax.rsqrt(same_sq), lax.rsqrt(flip_sq)
+                same_inv_sq, flip_inv_sq = same_inv * same_inv, flip_inv * flip_inv
+                same_top, flip_top = jnp.log2(same_inv) - same_sq, jnp.log2(flip_inv) - flip_sq
+                same_r, flip_r = same_sq * same_inv, flip_sq * flip_inv
+                sum_r, gap_r = same_r + flip_r, same_r - flip_r
+                for g in range(max(0, m), min(groups, groups + m)):
+                    k = g - m
+                    at = g * groups + k
+                    energy = energy_ref[at : at + 1, :] - in_y_sq
+                    energy_sq = energy * energy
+                    gauss = gauss_ref[at : at + 1, :] * in_y_gauss
+                    same = jnp.exp2(same_top - energy_sq * same_inv_sq)
+                    flip = jnp.exp2(flip_top - energy_sq * flip_inv_sq)
+                    to = (k * GROUP + slot_order(r)) * HALF + part * rows
+                    to = pl.ds(pl.multiple_of(to, rows), rows)
+                    cols = slice(g * LANES, (g + 1) * LANES)
+                    values = ((same + flip) - gauss * sum_r, (same - flip) - gauss * gap_r)
+                    for parity, value in enumerate(values):
+                        high = value.astype(jnp.bfloat16)
+                        hi_ref[source, parity, to, cols] = high
+                        lo_ref[source, parity, to, cols] = (value - high.astype(jnp.float32)).astype(jnp.bfloat16)
         return carry
 
-    lax.fori_loop(0, sources * 2 * GROUP, one, 0)
+    lax.fori_loop(0, sources * GROUP, one, 0)
 
 
 def make_entries(here, local, sources, ahead_of):
     size = local * HALF
-    count = sources * 2 * size * size
     shape = pltpu.VMEM((sources, 2, size, size), jnp.bfloat16)
     return pl.pallas_call(
         functools.partial(entries_body, local, sources),
         in_specs=[SCALARS] + [WHOLE] * len(ahead_of),
         out_specs=[WHOLE, WHOLE],
         out_shape=[shape, shape],
-        compiler_params=room(6),
-        cost_estimate=pl.CostEstimate(flops=20 * count, bytes_accessed=4 * count, transcendentals=2 * count),
+        scratch_shapes=[pltpu.VMEM(((local // GROUP) ** 2, LANES), jnp.float32)] * 2,
+        compiler_params=room(8),
+        cost_estimate=SMALL,
         name="kernel_entries",
     )(here, *map(in_vmem, ahead_of))
 
@@ -295,7 +293,7 @@
         out_shape=[pltpu.VMEM(field.shape, jnp.float32), pltpu.VMEM((2, cells, local_len // 2), jnp.float32)],
         scratch_shapes=[pltpu.VMEM((rows_x, wide), jnp.float32)] * 2,
         compiler_params=room(4),
-        cost_estimate=pl.CostEstimate(flops=40 * cells * local_len, bytes_accessed=16 * cells * local_len, transcendentals=0),
+        cost_estimate=SMALL,
         name="transport",
     )(here, in_vmem(field), in_vmem(xhalo), in_vmem(ylo), in_vmem(yhi), *map(in_vmem, entries))
 
@@ -331,7 +329,7 @@
         out_shape=pltpu.VMEM(fold.shape, jnp.float32),
         scratch_shapes=[pltpu.VMEM(fold.shape, jnp.bfloat16)] * 2,
         compiler_params=room(8),
-        cost_estimate=pl.CostEstimate(flops=12 * cells * size * size, bytes_accessed=8 * size * size + 16 * cells * size, transcendentals=0),
+        cost_estimate=SMALL,
         name="own_gain",
     )(in_vmem(fold), *map(in_vmem, entries))
 
@@ -399,7 +397,7 @@
         out_shape=out_shape,
         scratch_shapes=scratch,
         compiler_params=room(12),
-        cost_estimate=pl.CostEstimate(flops=12 * cells * size * size, bytes_accessed=8 * size * size + 32 * cells * size, transcendentals=0),
+        cost_estimate=SMALL,
         name="collide",
     )(here, in_vmem(fold), in_vmem(entries[0]), in_vmem(entries[1]), in_vmem(part), in_vmem(advected), density, kind, inflow)
 

time: 64.6 us -> 62.5 us (0.967)
  Pallas kernels: 39.8 us -> 37.7 us
    pallas_call x1, Pallas kernels: 10.4 us -> 8.26 us  [make_entries(): pl.pallas_call(functools.partial(entries_body, local, sources), in_specs=...]
  transfers between devices with their start and end apart: 8 -> 8, of which waited for: 4 -> 4; matrix products, arithmetic and copies ran while one was open for 0% -> 0% of each run, Pallas kernels for 27% -> 25%
where the time goes in v2:
time: 62.5 us; the launch traced here: 62.3 us
  Pallas kernels  37.7 us (60%)
  starting transfers between devices  16.2 us (26%)
  waiting for transfers between devices  7.8 us (12%)
    ppermute x4, starting transfers between devices, shifted(): lax.ppermute(block, axis, [(i, i + by) for i in range(count) if 0 <= i +...  12.5 us
    pallas_call x2, Pallas kernels, collide(): pl.pallas_call(functools.partial(collide_body, wide, rows_x, last), in_sp...  10.9 us
    pallas_call x2, Pallas kernels, transport(): pl.pallas_call(functools.partial(transport_body, wide, rows_x), in_specs=...  8.47 us
    pallas_call x1, Pallas kernels, make_entries(): pl.pallas_call(functools.partial(entries_body, local, sources), in_specs=...  8.26 us
    ppermute x4, waiting for transfers between devices, shifted(): lax.ppermute(block, axis, [(i, i + by) for i in range(count) if 0 <= i +...  7.46 us
    pallas_call x2, Pallas kernels, own_gain(): pl.pallas_call(functools.partial(own_body, 2 * LANES), in_specs=[WHOLE] *...  7.22 us
    pallas_call x1, Pallas kernels, stage(): pl.pallas_call(functools.partial(stage_body, wide, rows_x), in_specs=[SCA...  2.87 us
    ppermute x2, starting transfers between devices, per_device(): other = lax.ppermute(fold, 'vert', swap)  2.13 us
  transfers between devices with their start and end apart: 8, of which 4 were waited for; matrix products, arithmetic and copies ran while one was open for 0% of the time, Pallas kernels for 25%

profile of v2, /device:TPU:19, one launch (start us, length us, event | category | flops | bytes accessed | tf_op | source)
XLA Modules:
  0.0 62.3 jit_solution(7933407366472304139)
XLA Ops:
  0.0 0.0 copy-start.1
  0.0 0.0 copy-start.2
  0.0 0.1 pad_add_fusion.here_ref
  0.1 2.9 %stage.1 = (f32[256,2048]{1,0:T(8,128)S(1)}, f32[24,2048]{1,0:T(8,128)}, f32[24,2048]{1,0:T(8,128)S(1)}, f32[2,16,2048]{2,1,0:T(8,128)S(1)}) custom-call(s32[4]{0:T(128)S(1)} %pad_add_fusion.here_ref, f32[256,2048]{1,0:T(8,128)} %bitcast.8), custom_call_target="tpu_custom_call" | custom-call | tf_op jit(solution)/shard_map/stage/pallas_call | solution.py:178
  3.0 0.3 collective-permute-start
  3.3 3.1 %collective-permute-start.1 = (f32[24,2048]{1,0:T(8,128)}, f32[24,2048]{1,0:T(8,128)S(1)}, u32[]{:S(2)}, u32[]{:S(2)}) collective-permute-start(f32[24,2048]{1,0:T(8,128)} %get-tuple-element.21), channel_id=1, source_target_pairs={{0,2},{2,4},{4,6},{6,8},{8,10},{10,12},{12,14},{1,3},{3,5},{5,7},{... | collective-permute-start | bytes 589832 | tf_op jit(solution)/shard_map/ppermute | solution.py:407
  6.4 3.0 %collective-permute-start.2 = (f32[24,2048]{1,0:T(8,128)S(1)}, f32[24,2048]{1,0:T(8,128)S(1)}, u32[]{:S(2)}, u32[]{:S(2)}) collective-permute-start(f32[24,2048]{1,0:T(8,128)S(1)} %get-tuple-element.22), channel_id=1, source_target_pairs={{2,0},{4,2},{6,4},{8,6},{10,8},{12,10},{14,12},{3,1},{5,3},{7,5},{... | collective-permute-start | bytes 589832 | tf_op jit(solution)/shard_map/ppermute | solution.py:407
  9.5 0.0 copy-done.1
  9.5 0.1 reshape.22.rest_0_.density_ref
  9.6 0.0 copy-done.2
  9.6 0.1 reshape.23.rest_1_.type_ref
  9.7 8.3 %kernel_entries.1 = (bf16[2,2,1024,1024]{3,2,1,0:T(8,128)(2,1)S(1)}, bf16[2,2,1024,1024]{3,2,1,0:T(8,128)(2,1)S(1)}) custom-call(s32[4]{0:T(128)S(1)} %pad_add_fusion.here_ref, f32[256,1]{1,0:T(8,128)S(1)} %reshape.22.rest_0_.density_ref, s32[256,1]{1,0:T(8,128)S(1)} %reshape.23.rest_1_.type_ref), custom_call_target="tpu_custom_call" | custom-call | flops 1 | bytes 1 | tf_op jit(solution)/shard_map/kernel_entries/pallas_call | solution.py:118
  18.0 0.0 collective-permute-done.1.ylo_ref
  18.0 0.0 collective-permute-done.2.yhi_ref
  18.0 0.0 collective-permute-done.xhalo_ref
  18.0 4.2 %transport.2 = (f32[256,2048]{1,0:T(8,128)S(1)}, f32[2,256,1024]{2,1,0:T(8,128)S(1)}) custom-call(s32[4]{0:T(128)S(1)} %pad_add_fusion.here_ref, f32[256,2048]{1,0:T(8,128)S(1)} %get-tuple-element.19.field_ref, f32[2,16,2048]{2,1,0:T(8,128)S(1)} %collective-permute-done.xhalo_ref, f32[24,2048]{1,0:T(8,128)S(1)} %collective-permute-done.1.ylo_ref, ...), custom_call_target="tpu_custom_call" | custom-call | flops 1 | bytes 1 | tf_op jit(solution)/shard_map/transport/pallas_call | solution.py:289
  22.2 0.0 copy-start
  22.2 1.6 %collective-permute-start.3 = (f32[2,256,1024]{2,1,0:T(8,128)S(1)}, f32[2,256,1024]{2,1,0:T(8,128)S(1)}, u32[]{:S(2)}, u32[]{:S(2)}) collective-permute-start(f32[2,256,1024]{2,1,0:T(8,128)S(1)} %get-tuple-element.25.fold_ref), channel_id=1, source_target_pairs={{0,1},{1,0},{2,3},{3,2},{4,5},{5,4},{6,7},{7,6},{8,9},{9,8},{10,11... | collective-permute-start | bytes 6291464 | tf_op jit(solution)/shard_map/ppermute | solution.py:433
  23.8 3.6 %own_gain.2.part_ref = f32[2,256,1024]{2,1,0:T(8,128)S(1)} custom-call(f32[2,256,1024]{2,1,0:T(8,128)S(1)} %get-tuple-element.25.fold_ref, bf16[2,2,1024,1024]{3,2,1,0:T(8,128)(2,1)S(1)} %get-tuple-element.23.rest_0_.hi_ref, bf16[2,2,1024,1024]{3,2,1,0:T(8,128)(2,1)S(1)} %get-tuple-element.24.rest_1_.lo_ref), custom_call_target="tpu_custom_call" | custom-call | flops 1 | bytes 1 | tf_op jit(solution)/shard_map/own_gain/pallas_call | solution.py:325
  27.4 0.2 collective-permute-done.3.fold_ref
  27.6 0.0 copy-done
  27.6 5.1 %collide.2 = (f32[256,2048]{1,0:T(8,128)S(1)}, f32[24,2048]{1,0:T(8,128)S(1)}, f32[24,2048]{1,0:T(8,128)S(1)}, f32[2,16,2048]{2,1,0:T(8,128)S(1)}) custom-call(s32[4]{0:T(128)S(1)} %pad_add_fusion.here_ref, f32[2,256,1024]{2,1,0:T(8,128)S(1)} %collective-permute-done.3.fold_ref, bf16[2,2,1024,1024]{3,2,1,0:T(8,128)(2,1)S(1)} %get-tuple-element.23.rest_0_.hi_ref, ...), custom_call_target="tpu_custom_call" | custom-call | flops 1 | bytes 1 | tf_op jit(solution)/shard_map/collide/pallas_call | solution.py:393
  32.7 1.3 %collective-permute-start.4 = (f32[2,16,2048]{2,1,0:T(8,128)S(1)}, f32[2,16,2048]{2,1,0:T(8,128)S(1)}, u32[]{:S(2)}, u32[]{:S(2)}) collective-permute-start(f32[2,16,2048]{2,1,0:T(8,128)S(1)} %get-tuple-element.28), channel_id=1, source_target_pairs={{0,16},{16,0},{1,17},{17,1},{2,18},{18,2},{3,19},{19,3},{4,20},{20... | collective-permute-start | bytes 786440 | tf_op jit(solution)/shard_map/ppermute | solution.py:429
  34.0 2.2 %collective-permute-start.5 = (f32[24,2048]{1,0:T(8,128)S(1)}, f32[24,2048]{1,0:T(8,128)S(1)}, u32[]{:S(2)}, u32[]{:S(2)}) collective-permute-start(f32[24,2048]{1,0:T(8,128)S(1)} %get-tuple-element.29), channel_id=1, source_target_pairs={{0,2},{2,4},{4,6},{6,8},{8,10},{10,12},{12,14},{1,3},{3,5},{5,7},{... | collective-permute-start | bytes 589832 | tf_op jit(solution)/shard_map/ppermute | solution.py:407
  36.2 4.1 %collective-permute-start.6 = (f32[24,2048]{1,0:T(8,128)S(1)}, f32[24,2048]{1,0:T(8,128)S(1)}, u32[]{:S(2)}, u32[]{:S(2)}) collective-permute-start(f32[24,2048]{1,0:T(8,128)S(1)} %get-tuple-element.30), channel_id=1, source_target_pairs={{2,0},{4,2},{6,4},{8,6},{10,8},{12,10},{14,12},{3,1},{5,3},{7,5},{... | collective-permute-start | bytes 589832 | tf_op jit(solution)/shard_map/ppermute | solution.py:407
  40.3 2.2 %collective-permute-done.5.ylo_ref = f32[24,2048]{1,0:T(8,128)S(1)} collective-permute-done((f32[24,2048]{1,0:T(8,128)S(1)}, f32[24,2048]{1,0:T(8,128)S(1)}, u32[]{:S(2)}, u32[]{:S(2)}) %collective-permute-start.5) | collective-permute-done | bytes 196640 | tf_op jit(solution)/shard_map/ppermute | solution.py:407
  42.5 5.2 %collective-permute-done.6.yhi_ref = f32[24,2048]{1,0:T(8,128)S(1)} collective-permute-done((f32[24,2048]{1,0:T(8,128)S(1)}, f32[24,2048]{1,0:T(8,128)S(1)}, u32[]{:S(2)}, u32[]{:S(2)}) %collective-permute-start.6) | collective-permute-done | bytes 196640 | tf_op jit(solution)/shard_map/ppermute | solution.py:407
  47.8 0.0 collective-permute-done.4.xhalo_ref
  47.8 4.3 %transport.3 = (f32[256,2048]{1,0:T(8,128)S(1)}, f32[2,256,1024]{2,1,0:T(8,128)S(1)}) custom-call(s32[4]{0:T(128)S(1)} %pad_add_fusion.here_ref, f32[256,2048]{1,0:T(8,128)S(1)} %get-tuple-element.27.field_ref, f32[2,16,2048]{2,1,0:T(8,128)S(1)} %collective-permute-done.4.xhalo_ref, f32[24,2048]{1,0:T(8,128)S(1)} %collective-permute-done.5.ylo_ref, ...), custom_call_target="tpu_custom_call" | custom-call | flops 1 | bytes 1 | tf_op jit(solution)/shard_map/transport/pallas_call | solution.py:289
  52.0 0.5 collective-permute-start.7
  52.6 3.6 %own_gain.3.part_ref = f32[2,256,1024]{2,1,0:T(8,128)S(1)} custom-call(f32[2,256,1024]{2,1,0:T(8,128)S(1)} %get-tuple-element.31.fold_ref, bf16[2,2,1024,1024]{3,2,1,0:T(8,128)(2,1)S(1)} %get-tuple-element.23.rest_0_.hi_ref, bf16[2,2,1024,1024]{3,2,1,0:T(8,128)(2,1)S(1)} %get-tuple-element.24.rest_1_.lo_ref), custom_call_target="tpu_custom_call" | custom-call | flops 1 | bytes 1 | tf_op jit(solution)/shard_map/own_gain/pallas_call | solution.py:325
  56.2 0.2 collective-permute-done.7.fold_ref
  56.4 5.7 %collide.3 = f32[256,2048]{1,0:T(8,128)} custom-call(s32[4]{0:T(128)S(1)} %pad_add_fusion.here_ref, f32[2,256,1024]{2,1,0:T(8,128)S(1)} %collective-permute-done.7.fold_ref, bf16[2,2,1024,1024]{3,2,1,0:T(8,128)(2,1)S(1)} %get-tuple-element.23.rest_0_.hi_ref, bf16[2,2,1024,1024]{3,2,1,0:T(8,128)(2,1)S(1)} %get-tuple-element.24.rest_1_.lo_ref, ...), custom_call_target="tpu_custom_call" | custom-call | flops 1 | bytes 1 | tf_op jit(solution)/shard_map/collide/pallas_call | solution.py:393
Async XLA Ops:
  0.0 9.5 %copy-start.1 = (f32[16,16]{1,0:T(8,128)S(1)}, f32[16,16]{1,0:T(8,128)}, u32[]{:S(2)}) copy-start(f32[16,16]{1,0:T(8,128)} %param.5) | copy-start | bytes 3076
  0.0 9.6 %copy-start.2 = (s32[16,16]{1,0:T(8,128)S(1)}, s32[16,16]{1,0:T(8,128)}, u32[]{:S(2)}) copy-start(s32[16,16]{1,0:T(8,128)} %param.6) | copy-start | bytes 3076
  3.0 15.0 %collective-permute-start = (f32[2,16,2048]{2,1,0:T(8,128)S(1)}, f32[2,16,2048]{2,1,0:T(8,128)S(1)}, u32[]{:S(2)}, u32[]{:S(2)}) collective-permute-start(f32[2,16,2048]{2,1,0:T(8,128)S(1)} %get-tuple-element.20), channel_id=1, source_target_pairs={{0,16},{16,0},{1,17},{17,1},{2,18},{18,2},{3,19},{19,3},{4,20},{20... | collective-permute-start | bytes 786440 | tf_op jit(solution)/shard_map/ppermute | solution.py:429
  3.3 14.7 %collective-permute-start.1 = (f32[24,2048]{1,0:T(8,128)}, f32[24,2048]{1,0:T(8,128)S(1)}, u32[]{:S(2)}, u32[]{:S(2)}) collective-permute-start(f32[24,2048]{1,0:T(8,128)} %get-tuple-element.21), channel_id=1, source_target_pairs={{0,2},{2,4},{4,6},{6,8},{8,10},{10,12},{12,14},{1,3},{3,5},{5,7},{... | collective-permute-start | bytes 589832 | tf_op jit(solution)/shard_map/ppermute | solution.py:407
  6.4 11.5 %collective-permute-start.2 = (f32[24,2048]{1,0:T(8,128)S(1)}, f32[24,2048]{1,0:T(8,128)S(1)}, u32[]{:S(2)}, u32[]{:S(2)}) collective-permute-start(f32[24,2048]{1,0:T(8,128)S(1)} %get-tuple-element.22), channel_id=1, source_target_pairs={{2,0},{4,2},{6,4},{8,6},{10,8},{12,10},{14,12},{3,1},{5,3},{7,5},{... | collective-permute-start | bytes 589832 | tf_op jit(solution)/shard_map/ppermute | solution.py:407
  22.2 5.4 %copy-start = (f32[2048]{0:T(1024)S(1)}, f32[2048]{0:T(1024)}, u32[]{:S(2)}) copy-start(f32[2048]{0:T(1024)} %param.7) | copy-start | bytes 24580
  22.2 5.4 %collective-permute-start.3 = (f32[2,256,1024]{2,1,0:T(8,128)S(1)}, f32[2,256,1024]{2,1,0:T(8,128)S(1)}, u32[]{:S(2)}, u32[]{:S(2)}) collective-permute-start(f32[2,256,1024]{2,1,0:T(8,128)S(1)} %get-tuple-element.25.fold_ref), channel_id=1, source_target_pairs={{0,1},{1,0},{2,3},{3,2},{4,5},{5,4},{6,7},{7,6},{8,9},{9,8},{10,11... | collective-permute-start | bytes 6291464 | tf_op jit(solution)/shard_map/ppermute | solution.py:433
  32.7 15.1 %collective-permute-start.4 = (f32[2,16,2048]{2,1,0:T(8,128)S(1)}, f32[2,16,2048]{2,1,0:T(8,128)S(1)}, u32[]{:S(2)}, u32[]{:S(2)}) collective-permute-start(f32[2,16,2048]{2,1,0:T(8,128)S(1)} %get-tuple-element.28), channel_id=1, source_target_pairs={{0,16},{16,0},{1,17},{17,1},{2,18},{18,2},{3,19},{19,3},{4,20},{20... | collective-permute-start | bytes 786440 | tf_op jit(solution)/shard_map/ppermute | solution.py:429
  34.0 8.6 %collective-permute-start.5 = (f32[24,2048]{1,0:T(8,128)S(1)}, f32[24,2048]{1,0:T(8,128)S(1)}, u32[]{:S(2)}, u32[]{:S(2)}) collective-permute-start(f32[24,2048]{1,0:T(8,128)S(1)} %get-tuple-element.29), channel_id=1, source_target_pairs={{0,2},{2,4},{4,6},{6,8},{8,10},{10,12},{12,14},{1,3},{3,5},{5,7},{... | collective-permute-start | bytes 589832 | tf_op jit(solution)/shard_map/ppermute | solution.py:407
  36.2 11.6 %collective-permute-start.6 = (f32[24,2048]{1,0:T(8,128)S(1)}, f32[24,2048]{1,0:T(8,128)S(1)}, u32[]{:S(2)}, u32[]{:S(2)}) collective-permute-start(f32[24,2048]{1,0:T(8,128)S(1)} %get-tuple-element.30), channel_id=1, source_target_pairs={{2,0},{4,2},{6,4},{8,6},{10,8},{12,10},{14,12},{3,1},{5,3},{7,5},{... | collective-permute-start | bytes 589832 | tf_op jit(solution)/shard_map/ppermute | solution.py:407
  52.0 4.3 %collective-permute-start.7 = (f32[2,256,1024]{2,1,0:T(8,128)S(1)}, f32[2,256,1024]{2,1,0:T(8,128)S(1)}, u32[]{:S(2)}, u32[]{:S(2)}) collective-permute-start(f32[2,256,1024]{2,1,0:T(8,128)S(1)} %get-tuple-element.31.fold_ref), channel_id=1, source_target_pairs={{0,1},{1,0},{2,3},{3,2},{4,5},{5,4},{6,7},{7,6},{8,9},{9,8},{10,11... | collective-permute-start | bytes 6291464 | tf_op jit(solution)/shard_map/ppermute | solution.py:433

commit v3 on v2

--- a/solution.py
+++ b/solution.py
@@ -149,17 +149,19 @@
         xsend_ref[layer, :, span] = jnp.where(here_ref[3] > 0, last_row, first_row)
     low_half = iota((rows_x // 2, LANES), 1) % NVX < HALF
     for ahead, to_ref, near, far in ((True, up_ref, rows_y - 1, rows_y - 2), (False, down_ref, 0, 1)):
+        side = 1 if ahead else 0
         for x in range(rows_x):
             to_ref[x : x + 1, span] = field[x * rows_y + near : x * rows_y + near + 1, span]
-            far_ref[x : x + 1, span] = field[x * rows_y + far : x * rows_y + far + 1, span]
+            far_ref[side, x : x + 1, span] = field[x * rows_y + far : x * rows_y + far + 1, span]
         for i in range(span.start, span.stop, LANES):
             at = slice(i, i + LANES)
-            to_ref[rows_x:, at] = pack_far(far_ref[:, at], ahead, low_half)
+            to_ref[rows_x:, at] = pack_far(far_ref[side, :, at], ahead, low_half)
 
 
 def edge_shapes(rows_x, rows_y, local_len):
     edge_y = pltpu.VMEM((rows_x + rows_x // 2, local_len), jnp.float32)
-    return [edge_y, edge_y, pltpu.VMEM((2, rows_y, local_len), jnp.float32)]
+    layers_x = pltpu.VMEM((2, rows_y, local_len), jnp.float32)
+    return [edge_y, edge_y, layers_x, pltpu.VMEM((2, rows_x, local_len), jnp.float32)]
 
 
 def stage_body(wide, rows_x, here_ref, from_ref, field, up_ref, down_ref, xsend_ref, far_ref, sems):
@@ -178,9 +180,9 @@
     return pl.pallas_call(
         functools.partial(stage_body, wide, rows_x),
         in_specs=[SCALARS, pl.BlockSpec(memory_space=pltpu.HBM)],
-        out_specs=[WHOLE] * 4,
+        out_specs=[WHOLE] * 5,
         out_shape=[pltpu.VMEM(field.shape, jnp.float32)] + edge_shapes(rows_x, cells // rows_x, local_len),
-        scratch_shapes=[pltpu.VMEM((rows_x, local_len), jnp.float32), pltpu.SemaphoreType.DMA((4,))],
+        scratch_shapes=[pltpu.SemaphoreType.DMA((4,))],
         compiler_params=room(4),
         name="stage",
     )(here, pltpu.with_memory_space_constraint(field, pltpu.HBM))
@@ -213,8 +215,12 @@
     return jnp.where(even, near, far), jnp.where(even, far, near)
 
 
-def transport_body(wide, rows_x, here_ref, field_ref, xhalo_ref, ylo_ref, yhi_ref, *rest):
-    adv_ref, fold_ref, low_edge, high_edge = rest[-4:]
+def transport_body(wide, rows_x, whole, here_ref, field_ref, xhalo_ref, *rest):
+    if whole:
+        ylo_ref, yhi_ref = rest[:2]
+        adv_ref, fold_ref, low_edge, high_edge = rest[-4:]
+    else:
+        adv_ref, fold_ref = rest[-2:]
     cells, local_len = field_ref.shape
     rows_y = cells // rows_x
     has_low = here_ref[2] > 0
@@ -237,13 +243,14 @@
         def face_y(f0, f1, f2):
             return ay * f1 + by * minmod(f1 - f0, f2 - f1)
 
-        for x in range(rows_x):
-            low_edge[x : x + 1] = field_ref[x * rows_y : x * rows_y + 1, cols]
-            high_edge[x : x + 1] = field_ref[(x + 1) * rows_y - 1 : (x + 1) * rows_y, cols]
-        low_far = unpack_far(ylo_ref[rows_x:, cols], True)
-        high_far = unpack_far(yhi_ref[rows_x:, cols], False)
-        low_edge[...] = face_y(low_far, ylo_ref[:rows_x, cols], low_edge[...])
-        high_edge[...] = face_y(high_edge[...], yhi_ref[:rows_x, cols], high_far)
+        if whole:
+            for x in range(rows_x):
+                low_edge[x : x + 1] = field_ref[x * rows_y : x * rows_y + 1, cols]
+                high_edge[x : x + 1] = field_ref[(x + 1) * rows_y - 1 : (x + 1) * rows_y, cols]
+            low_far = unpack_far(ylo_ref[rows_x:, cols], True)
+            high_far = unpack_far(yhi_ref[rows_x:, cols], False)
+            low_edge[...] = face_y(low_far, ylo_ref[:rows_x, cols], low_edge[...])
+            high_edge[...] = face_y(high_edge[...], yhi_ref[:rows_x, cols], high_far)
 
         def row(i):
             if i < 0:
@@ -264,11 +271,17 @@
             x = i - 1
             here = near[0]
             row_term = jnp.where(ahead_x, face[x + 1] - face[x], face[x + 2] - face[x + 1])
-            below = jnp.where(first_y, ylo_ref[x : x + 1, cols], pltpu.roll(here, 1, 0))
-            above = jnp.where(last_y, yhi_ref[x : x + 1, cols], pltpu.roll(here, rows_y - 1, 0))
+            below, above = pltpu.roll(here, 1, 0), pltpu.roll(here, rows_y - 1, 0)
+            if whole:
+                below = jnp.where(first_y, ylo_ref[x : x + 1, cols], below)
+                above = jnp.where(last_y, yhi_ref[x : x + 1, cols], above)
             mine = face_y(below, here, above)
-            mine_below = jnp.where(first_y, low_edge[x : x + 1], pltpu.roll(mine, 1, 0))
-            mine_above = jnp.where(last_y, high_edge[x : x + 1], pltpu.roll(mine, rows_y - 1, 0))
+            if not whole:
+                mine = jnp.where(first_y | last_y, 0.0, mine)
+            mine_below, mine_above = pltpu.roll(mine, 1, 0), pltpu.roll(mine, rows_y - 1, 0)
+            if whole:
+                mine_below = jnp.where(first_y, low_edge[x : x + 1], mine_below)
+                mine_above = jnp.where(last_y, high_edge[x : x + 1], mine_above)
             col_term = jnp.where(ahead_y, mine - mine_below, mine_above - mine)
             moved = here - row_term - col_term
             at = slice(x * rows_y, (x + 1) * rows_y)
@@ -283,19 +296,92 @@
     lax.fori_loop(0, local_len // wide, chunk, 0)
 
 
-def transport(here, rows_x, field, xhalo, ylo, yhi, entries):
+def columns_body(wide, rows_x, here_ref, up_ref, down_ref, far_ref, ylo_ref, yhi_ref, adv_in, fold_in, *rest):
+    adv_ref, fold_ref, added, added_fold = rest[-4:]
+    cells, local_len = adv_in.shape
+    rows_y = cells // rows_x
+    half = rows_y // 2
+    masks = fold_masks(rows_x)
+
+    def chunk(c, carry):
+        cols = pl.ds(pl.multiple_of(c * wide, wide), wide)
+        fold_cols = pl.ds(pl.multiple_of(c * (wide // 2), wide // 2), wide // 2)
+        _, vy = velocity_parts(here_ref[0] * local_len + c * wide + iota((1, wide), 1))
+        ay = time_step * vy
+        by = 0.5 * jnp.abs(ay) * (1.0 - jnp.abs(ay))
+        ahead = ay > 0
+
+        def face(f0, f1, f2):
+            return ay * f1 + by * minmod(f1 - f0, f2 - f1)
+
+        low_near, low = ylo_ref[:rows_x, cols], down_ref[:rows_x, cols]
+        high, high_near = up_ref[:rows_x, cols], yhi_ref[:rows_x, cols]
+        before = face(unpack_far(ylo_ref[rows_x:, cols], True), low_near, low)
+        first = face(low_near, low, far_ref[0, :, cols])
+        last = face(far_ref[1, :, cols], high, high_near)
+        after = face(high, high_near, unpack_far(yhi_ref[rows_x:, cols], False))
+        parts = [
+            jnp.where(ahead, before - first, first),
+            jnp.where(ahead, first, 0.0),
+            jnp.where(ahead, 0.0, -last),
+            jnp.where(ahead, -last, last - after),
+        ]
+        for i, part in enumerate(parts):
+            at = slice(i * rows_x, (i + 1) * rows_x)
+            added[at] = part
+            for j in range(0, wide, 2 * LANES):
+                both = folded(part[:, j : j + LANES], part[:, j + LANES : j + 2 * LANES], *masks)
+                for parity in range(2):
+                    added_fold[parity, at, j // 2 : j // 2 + LANES] = both[parity]
+
+        def spread(ref, x, upper, at_y):
+            i = 2 if upper else 0
+            first, second = (ref[(i + k) * rows_x + x : (i + k) * rows_x + x + 1, :] for k in range(2))
+            place = half - 2 if upper else 0
+            return jnp.where(at_y == place, first, jnp.where(at_y == place + 1, second, 0.0))
+
+        at_y = iota((half, wide), 0)
+        at_y_fold = iota((half, wide // 2), 0)
+        for x in range(rows_x):
+            for upper in range(2):
+                rows = slice(x * rows_y + upper * half, x * rows_y + (upper + 1) * half)
+                adv_ref[rows, cols] = adv_in[rows, cols] + spread(added, x, upper, at_y)
+                for parity in range(2):
+                    more = spread(added_fold.at[parity], x, upper, at_y_fold)
+                    fold_ref[parity, rows, fold_cols] = fold_in[parity, rows, fold_cols] + more
+        return carry
+
+    lax.fori_loop(0, local_len // wide, chunk, 0)
+
+
+def transport(here, rows_x, field, xhalo, yhalos, entries):
     cells, local_len = field.shape
     wide = 4 * LANES
     return pl.pallas_call(
-        functools.partial(transport_body, wide, rows_x),
-        in_specs=[SCALARS] + [WHOLE] * (4 + len(entries)),
+        functools.partial(transport_body, wide, rows_x, bool(yhalos)),
+        in_specs=[SCALARS] + [WHOLE] * (2 + len(yhalos) + len(entries)),
         out_specs=[WHOLE] * 2,
         out_shape=[pltpu.VMEM(field.shape, jnp.float32), pltpu.VMEM((2, cells, local_len // 2), jnp.float32)],
-        scratch_shapes=[pltpu.VMEM((rows_x, wide), jnp.float32)] * 2,
+        scratch_shapes=[pltpu.VMEM((rows_x, wide), jnp.float32)] * (2 if yhalos else 0),
         compiler_params=room(4),
         cost_estimate=SMALL,
-        name="transport",
-    )(here, in_vmem(field), in_vmem(xhalo), in_vmem(ylo), in_vmem(yhi), *map(in_vmem, entries))
+        name="transport" if yhalos else "inner_transport",
+    )(here, *map(in_vmem, (field, xhalo, *yhalos, *entries)))
+
+
+def add_columns(here, rows_x, up, down, far, ylo, yhi, advected, fold, entries):
+    wide = 4 * LANES
+    return pl.pallas_call(
+        functools.partial(columns_body, wide, rows_x),
+        in_specs=[SCALARS] + [WHOLE] * (7 + len(entries)),
+        out_specs=[WHOLE] * 2,
+        out_shape=[pltpu.VMEM(advected.shape, jnp.float32), pltpu.VMEM(fold.shape, jnp.float32)],
+        scratch_shapes=[pltpu.VMEM((4 * rows_x, wide), jnp.float32), pltpu.VMEM((2, 4 * rows_x, wide // 2), jnp.float32)],
+        input_output_aliases={6: 0, 7: 1},
+        compiler_params=room(4),
+        cost_estimate=SMALL,
+        name="add_columns",
+    )(here, *map(in_vmem, (up, down, far, ylo, yhi, advected, fold, *entries)))
 
 
 def split_into(value_ref, high, low):
@@ -340,7 +426,7 @@
     if last:
         out_ref, high, low, field, sems = rest
     else:
-        field, up_ref, down_ref, xsend_ref, high, low, far_ref = rest
+        field, up_ref, down_ref, xsend_ref, far_ref, high, low = rest
     cells, local_len = adv_ref.shape
     rows_y = cells // rows_x
     split_into(fold_ref, high, low)
@@ -387,9 +473,9 @@
         out_shape = jax.ShapeDtypeStruct(advected.shape, jnp.float32)
         scratch = halves + [pltpu.VMEM(advected.shape, jnp.float32), pltpu.SemaphoreType.DMA((size // wide,))]
     else:
-        out_specs = [WHOLE] * 4
+        out_specs = [WHOLE] * 5
         out_shape = [pltpu.VMEM(advected.shape, jnp.float32)] + edge_shapes(rows_x, cells // rows_x, local_len)
-        scratch = halves + [pltpu.VMEM((rows_x, local_len), jnp.float32)]
+        scratch = halves
     return pl.pallas_call(
         functools.partial(collide_body, wide, rows_x, last),
         in_specs=[SCALARS] + [WHOLE] * 8,
@@ -420,7 +506,7 @@
     column_type = cell_type.reshape(cells, 1)
     row_inflow = inflow.reshape(1, local_len)
     swap = [(0, 1), (1, 0)]
-    field, up, down, send_x = stage(here, rows_x, distribution.reshape(cells, local_len))
+    field, up, down, send_x, far = stage(here, rows_x, distribution.reshape(cells, local_len))
     entries = None
     for step in range(STEPS):
         last = step == STEPS - 1
@@ -429,12 +515,16 @@
         xhalo = lax.ppermute(send_x, "gx", swap)
         if entries is None:
             entries = make_entries(here, local_len // NVX, verts, [column_density, column_type])
-        advected, fold = transport(here, rows_x, field, xhalo, ylo, yhi, entries)
+        if step == 0:
+            advected, fold = transport(here, rows_x, field, xhalo, [ylo, yhi], entries)
+        else:
+            advected, fold = transport(here, rows_x, field, xhalo, [], entries)
+            advected, fold = add_columns(here, rows_x, up, down, far, ylo, yhi, advected, fold, entries)
         other = lax.ppermute(fold, "vert", swap)
         part = own_gain(fold, entries)
         out = collide(here, rows_x, other, entries, part, advected, column_density, column_type, row_inflow, last)
         if not last:
-            field, up, down, send_x = out
+            field, up, down, send_x, far = out
     return out.reshape(rows_x, rows_y, local_len)
 
 

time: 62.5 us -> 60.5 us (0.968)
  waiting for transfers between devices: 7.8 us -> 3.8 us
  Pallas kernels: 37.7 us -> 39.7 us
    ppermute x4, waiting for transfers between devices: 7.46 us -> 3.46 us  [shifted(): lax.ppermute(block, axis, [(i, i + by) for i in range(count) if 0 <= i +...]
    pallas_call x2 -> x3, Pallas kernels: 8.47 us -> 10.5 us  [the longest x2 8.2 us: transport(): pl.pallas_call(functools.partial(transport_body, wide, rows_x, bool(yhalo...]
  transfers between devices with their start and end apart: 8 -> 8, of which waited for: 4 -> 3; matrix products, arithmetic and copies ran while one was open for 0% -> 0% of each run, Pallas kernels for 25% -> 32%
where the time goes in v3:
time: 60.5 us; the launch traced here: 60.3 us
  Pallas kernels  39.7 us (66%)
  starting transfers between devices  16.2 us (27%)
  waiting for transfers between devices  3.8 us (6%)
    ppermute x4, starting transfers between devices, shifted(): lax.ppermute(block, axis, [(i, i + by) for i in range(count) if 0 <= i +...  12.5 us
    pallas_call x2, Pallas kernels, collide(): pl.pallas_call(functools.partial(collide_body, wide, rows_x, last), in_sp...  10.9 us
    pallas_call x1, Pallas kernels, make_entries(): pl.pallas_call(functools.partial(entries_body, local, sources), in_specs=...  8.26 us
    pallas_call x2, Pallas kernels, transport(): pl.pallas_call(functools.partial(transport_body, wide, rows_x, bool(yhalo...  8.2 us
    pallas_call x2, Pallas kernels, own_gain(): pl.pallas_call(functools.partial(own_body, 2 * LANES), in_specs=[WHOLE] *...  7.22 us
    ppermute x4, waiting for transfers between devices, shifted(): lax.ppermute(block, axis, [(i, i + by) for i in range(count) if 0 <= i +...  3.46 us
    pallas_call x1, Pallas kernels, stage(): pl.pallas_call(functools.partial(stage_body, wide, rows_x), in_specs=[SCA...  2.9 us
    pallas_call x1, Pallas kernels, add_columns(): pl.pallas_call(functools.partial(columns_body, wide, rows_x), in_specs=[S...  2.25 us
  transfers between devices with their start and end apart: 8, of which 3 were waited for; matrix products, arithmetic and copies ran while one was open for 0% of the time, Pallas kernels for 32%

profile of v3, /device:TPU:19, one launch (start us, length us, event | category | flops | bytes accessed | tf_op | source)
XLA Modules:
  0.0 60.3 jit_solution(12123714641347329442)
XLA Ops:
  0.0 0.0 copy-start.1
  0.0 0.0 copy-start.2
  0.0 0.1 pad_add_fusion.here_ref
  0.1 2.9 %stage.1 = (f32[256,2048]{1,0:T(8,128)S(1)}, f32[24,2048]{1,0:T(8,128)}, f32[24,2048]{1,0:T(8,128)S(1)}, f32[2,16,2048]{2,1,0:T(8,128)S(1)}, f32[2,16,2048]{2,1,0:T(8,128)}) custom-call(s32[4]{0:T(128)S(1)} %pad_add_fusion.here_ref, f32[256,2048]{1,0:T(8,128)} %bitcast.8), custom_call_target="tpu_custom_call" | custom-call | tf_op jit(solution)/shard_map/stage/pallas_call | solution.py:180
  3.0 0.3 collective-permute-start
  3.3 3.1 %collective-permute-start.1 = (f32[24,2048]{1,0:T(8,128)}, f32[24,2048]{1,0:T(8,128)S(1)}, u32[]{:S(2)}, u32[]{:S(2)}) collective-permute-start(f32[24,2048]{1,0:T(8,128)} %get-tuple-element.24), channel_id=1, source_target_pairs={{0,2},{2,4},{4,6},{6,8},{8,10},{10,12},{12,14},{1,3},{3,5},{5,7},{... | collective-permute-start | bytes 589832 | tf_op jit(solution)/shard_map/ppermute | solution.py:493
  6.5 3.0 %collective-permute-start.2 = (f32[24,2048]{1,0:T(8,128)S(1)}, f32[24,2048]{1,0:T(8,128)S(1)}, u32[]{:S(2)}, u32[]{:S(2)}) collective-permute-start(f32[24,2048]{1,0:T(8,128)S(1)} %get-tuple-element.25), channel_id=1, source_target_pairs={{2,0},{4,2},{6,4},{8,6},{10,8},{12,10},{14,12},{3,1},{5,3},{7,5},{... | collective-permute-start | bytes 589832 | tf_op jit(solution)/shard_map/ppermute | solution.py:493
  9.5 0.0 copy-done.1
  9.5 0.1 reshape.22.rest_0_.density_ref
  9.6 0.0 copy-done.2
  9.6 0.1 reshape.23.rest_1_.type_ref
  9.7 8.3 %kernel_entries.1 = (bf16[2,2,1024,1024]{3,2,1,0:T(8,128)(2,1)S(1)}, bf16[2,2,1024,1024]{3,2,1,0:T(8,128)(2,1)S(1)}) custom-call(s32[4]{0:T(128)S(1)} %pad_add_fusion.here_ref, f32[256,1]{1,0:T(8,128)S(1)} %reshape.22.rest_0_.density_ref, s32[256,1]{1,0:T(8,128)S(1)} %reshape.23.rest_1_.type_ref), custom_call_target="tpu_custom_call" | custom-call | flops 1 | bytes 1 | tf_op jit(solution)/shard_map/kernel_entries/pallas_call | solution.py:118
  18.0 0.0 collective-permute-done.1.rest_0_
  18.0 0.0 collective-permute-done.2.rest_1_
  18.0 0.0 collective-permute-done.xhalo_ref
  18.0 4.2 %transport.1 = (f32[256,2048]{1,0:T(8,128)S(1)}, f32[2,256,1024]{2,1,0:T(8,128)S(1)}) custom-call(s32[4]{0:T(128)S(1)} %pad_add_fusion.here_ref, f32[256,2048]{1,0:T(8,128)S(1)} %get-tuple-element.22.field_ref, f32[2,16,2048]{2,1,0:T(8,128)S(1)} %collective-permute-done.xhalo_ref, f32[24,2048]{1,0:T(8,128)S(1)} %collective-permute-done.1.rest_0_, ...), custom_call_target="tpu_custom_call" | custom-call | flops 1 | bytes 1 | tf_op jit(solution)/shard_map/transport/pallas_call | solution.py:360
  22.2 0.0 copy-start
  22.2 1.6 %collective-permute-start.3 = (f32[2,256,1024]{2,1,0:T(8,128)S(1)}, f32[2,256,1024]{2,1,0:T(8,128)S(1)}, u32[]{:S(2)}, u32[]{:S(2)}) collective-permute-start(f32[2,256,1024]{2,1,0:T(8,128)S(1)} %get-tuple-element.28.fold_ref), channel_id=1, source_target_pairs={{0,1},{1,0},{2,3},{3,2},{4,5},{5,4},{6,7},{7,6},{8,9},{9,8},{10,11... | collective-permute-start | bytes 6291464 | tf_op jit(solution)/shard_map/ppermute | solution.py:523
  23.8 3.6 %own_gain.2.part_ref = f32[2,256,1024]{2,1,0:T(8,128)S(1)} custom-call(f32[2,256,1024]{2,1,0:T(8,128)S(1)} %get-tuple-element.28.fold_ref, bf16[2,2,1024,1024]{3,2,1,0:T(8,128)(2,1)S(1)} %get-tuple-element.26.rest_2_.hi_ref.rest_0_, bf16[2,2,1024,1024]{3,2,1,0:T(8,128)(2,1)S(1)} %get-tuple-element.27.rest_3_.lo_ref.rest_1_), custom_call_target="tpu_custom_call" | custom-call | flops 1 | bytes 1 | tf_op jit(solution)/shard_map/own_gain/pallas_call | solution.py:411
  27.4 0.2 collective-permute-done.3.fold_ref
  27.6 0.0 copy-done
  27.6 5.1 %collide.2 = (f32[256,2048]{1,0:T(8,128)S(1)}, f32[24,2048]{1,0:T(8,128)S(1)}, f32[24,2048]{1,0:T(8,128)S(1)}, f32[2,16,2048]{2,1,0:T(8,128)S(1)}, f32[2,16,2048]{2,1,0:T(8,128)S(1)}) custom-call(s32[4]{0:T(128)S(1)} %pad_add_fusion.here_ref, f32[2,256,1024]{2,1,0:T(8,128)S(1)} %collective-permute-done.3.fold_ref, ...), custom_call_target="tpu_custom_call" | custom-call | flops 1 | bytes 1 | tf_op jit(solution)/shard_map/collide/pallas_call | solution.py:479
  32.7 1.3 %collective-permute-start.6 = (f32[2,16,2048]{2,1,0:T(8,128)S(1)}, f32[2,16,2048]{2,1,0:T(8,128)S(1)}, u32[]{:S(2)}, u32[]{:S(2)}) collective-permute-start(f32[2,16,2048]{2,1,0:T(8,128)S(1)} %get-tuple-element.34), channel_id=1, source_target_pairs={{0,16},{16,0},{1,17},{17,1},{2,18},{18,2},{3,19},{19,3},{4,20},{20... | collective-permute-start | bytes 786440 | tf_op jit(solution)/shard_map/ppermute | solution.py:515
  34.0 2.2 %collective-permute-start.4 = (f32[24,2048]{1,0:T(8,128)S(1)}, f32[24,2048]{1,0:T(8,128)S(1)}, u32[]{:S(2)}, u32[]{:S(2)}) collective-permute-start(f32[24,2048]{1,0:T(8,128)S(1)} %get-tuple-element.30.up_ref), channel_id=1, source_target_pairs={{0,2},{2,4},{4,6},{6,8},{8,10},{10,12},{12,14},{1,3},{3,5},{5,7},{... | collective-permute-start | bytes 589832 | tf_op jit(solution)/shard_map/ppermute | solution.py:493
  36.2 4.1 %collective-permute-start.5 = (f32[24,2048]{1,0:T(8,128)S(1)}, f32[24,2048]{1,0:T(8,128)S(1)}, u32[]{:S(2)}, u32[]{:S(2)}) collective-permute-start(f32[24,2048]{1,0:T(8,128)S(1)} %get-tuple-element.31.down_ref), channel_id=1, source_target_pairs={{2,0},{4,2},{6,4},{8,6},{10,8},{12,10},{14,12},{3,1},{5,3},{7,5},{... | collective-permute-start | bytes 589832 | tf_op jit(solution)/shard_map/ppermute | solution.py:493
  40.4 0.0 collective-permute-done.6.xhalo_ref
  40.4 4.0 %inner_transport.1 = (f32[256,2048]{1,0:T(8,128)S(1)}, f32[2,256,1024]{2,1,0:T(8,128)S(1)}) custom-call(s32[4]{0:T(128)S(1)} %pad_add_fusion.here_ref, f32[256,2048]{1,0:T(8,128)S(1)} %get-tuple-element.33.field_ref, f32[2,16,2048]{2,1,0:T(8,128)S(1)} %collective-permute-done.6.xhalo_ref, ...), custom_call_target="tpu_custom_call" | custom-call | flops 1 | bytes 1 | tf_op jit(solution)/shard_map/inner_transport/pallas_call | solution.py:360
  44.4 0.0 collective-permute-done.4.ylo_ref
  44.4 3.4 %collective-permute-done.5.yhi_ref = f32[24,2048]{1,0:T(8,128)S(1)} collective-permute-done((f32[24,2048]{1,0:T(8,128)S(1)}, f32[24,2048]{1,0:T(8,128)S(1)}, u32[]{:S(2)}, u32[]{:S(2)}) %collective-permute-start.5) | collective-permute-done | bytes 196640 | tf_op jit(solution)/shard_map/ppermute | solution.py:493
  47.8 2.2 %add_columns.1 = (f32[256,2048]{1,0:T(8,128)S(1)}, f32[2,256,1024]{2,1,0:T(8,128)S(1)}) custom-call(s32[4]{0:T(128)S(1)} %pad_add_fusion.here_ref, f32[24,2048]{1,0:T(8,128)S(1)} %get-tuple-element.30.up_ref, f32[24,2048]{1,0:T(8,128)S(1)} %get-tuple-element.31.down_ref, ...), custom_call_target="tpu_custom_call", output_to_operand_aliasing={{0}: (6, {}), {1}: (7, {})} | custom-call | flops 1 | bytes 1 | tf_op jit(solution)/shard_map/add_columns/pallas_call | solution.py:374
  50.1 0.6 collective-permute-start.7
  50.6 3.6 %own_gain.3.part_ref = f32[2,256,1024]{2,1,0:T(8,128)S(1)} custom-call(f32[2,256,1024]{2,1,0:T(8,128)S(1)} %get-tuple-element.37.fold_ref, bf16[2,2,1024,1024]{3,2,1,0:T(8,128)(2,1)S(1)} %get-tuple-element.26.rest_2_.hi_ref.rest_0_, bf16[2,2,1024,1024]{3,2,1,0:T(8,128)(2,1)S(1)} %get-tuple-element.27.rest_3_.lo_ref.rest_1_), custom_call_target="tpu_custom_call" | custom-call | flops 1 | bytes 1 | tf_op jit(solution)/shard_map/own_gain/pallas_call | solution.py:411
  54.3 0.2 collective-permute-done.7.fold_ref
  54.4 5.7 %collide.3 = f32[256,2048]{1,0:T(8,128)} custom-call(s32[4]{0:T(128)S(1)} %pad_add_fusion.here_ref, f32[2,256,1024]{2,1,0:T(8,128)S(1)} %collective-permute-done.7.fold_ref, bf16[2,2,1024,1024]{3,2,1,0:T(8,128)(2,1)S(1)} %get-tuple-element.26.rest_2_.hi_ref.rest_0_, bf16[2,2,1024,1024]{3,2,1,0:T(8,128)(2,1)S(1)} %get-tuple-element.27.rest_3_.lo_ref.rest_1_, ...), custom_call_target="tpu_custom_call" | custom-call | flops 1 | bytes 1 | tf_op jit(solution)/shard_map/collide/pallas_call | solution.py:479
Async XLA Ops:
  0.0 9.5 %copy-start.1 = (f32[16,16]{1,0:T(8,128)S(1)}, f32[16,16]{1,0:T(8,128)}, u32[]{:S(2)}) copy-start(f32[16,16]{1,0:T(8,128)} %param.5) | copy-start | bytes 3076
  0.0 9.6 %copy-start.2 = (s32[16,16]{1,0:T(8,128)S(1)}, s32[16,16]{1,0:T(8,128)}, u32[]{:S(2)}) copy-start(s32[16,16]{1,0:T(8,128)} %param.6) | copy-start | bytes 3076
  3.0 15.0 %collective-permute-start = (f32[2,16,2048]{2,1,0:T(8,128)S(1)}, f32[2,16,2048]{2,1,0:T(8,128)S(1)}, u32[]{:S(2)}, u32[]{:S(2)}) collective-permute-start(f32[2,16,2048]{2,1,0:T(8,128)S(1)} %get-tuple-element.23), channel_id=1, source_target_pairs={{0,16},{16,0},{1,17},{17,1},{2,18},{18,2},{3,19},{19,3},{4,20},{20... | collective-permute-start | bytes 786440 | tf_op jit(solution)/shard_map/ppermute | solution.py:515
  3.3 14.7 %collective-permute-start.1 = (f32[24,2048]{1,0:T(8,128)}, f32[24,2048]{1,0:T(8,128)S(1)}, u32[]{:S(2)}, u32[]{:S(2)}) collective-permute-start(f32[24,2048]{1,0:T(8,128)} %get-tuple-element.24), channel_id=1, source_target_pairs={{0,2},{2,4},{4,6},{6,8},{8,10},{10,12},{12,14},{1,3},{3,5},{5,7},{... | collective-permute-start | bytes 589832 | tf_op jit(solution)/shard_map/ppermute | solution.py:493
  6.5 11.5 %collective-permute-start.2 = (f32[24,2048]{1,0:T(8,128)S(1)}, f32[24,2048]{1,0:T(8,128)S(1)}, u32[]{:S(2)}, u32[]{:S(2)}) collective-permute-start(f32[24,2048]{1,0:T(8,128)S(1)} %get-tuple-element.25), channel_id=1, source_target_pairs={{2,0},{4,2},{6,4},{8,6},{10,8},{12,10},{14,12},{3,1},{5,3},{7,5},{... | collective-permute-start | bytes 589832 | tf_op jit(solution)/shard_map/ppermute | solution.py:493
  22.2 5.4 %copy-start = (f32[2048]{0:T(1024)S(1)}, f32[2048]{0:T(1024)}, u32[]{:S(2)}) copy-start(f32[2048]{0:T(1024)} %param.7) | copy-start | bytes 24580
  22.2 5.4 %collective-permute-start.3 = (f32[2,256,1024]{2,1,0:T(8,128)S(1)}, f32[2,256,1024]{2,1,0:T(8,128)S(1)}, u32[]{:S(2)}, u32[]{:S(2)}) collective-permute-start(f32[2,256,1024]{2,1,0:T(8,128)S(1)} %get-tuple-element.28.fold_ref), channel_id=1, source_target_pairs={{0,1},{1,0},{2,3},{3,2},{4,5},{5,4},{6,7},{7,6},{8,9},{9,8},{10,11... | collective-permute-start | bytes 6291464 | tf_op jit(solution)/shard_map/ppermute | solution.py:523
  32.7 7.6 %collective-permute-start.6 = (f32[2,16,2048]{2,1,0:T(8,128)S(1)}, f32[2,16,2048]{2,1,0:T(8,128)S(1)}, u32[]{:S(2)}, u32[]{:S(2)}) collective-permute-start(f32[2,16,2048]{2,1,0:T(8,128)S(1)} %get-tuple-element.34), channel_id=1, source_target_pairs={{0,16},{16,0},{1,17},{17,1},{2,18},{18,2},{3,19},{19,3},{4,20},{20... | collective-permute-start | bytes 786440 | tf_op jit(solution)/shard_map/ppermute | solution.py:515
  34.0 10.4 %collective-permute-start.4 = (f32[24,2048]{1,0:T(8,128)S(1)}, f32[24,2048]{1,0:T(8,128)S(1)}, u32[]{:S(2)}, u32[]{:S(2)}) collective-permute-start(f32[24,2048]{1,0:T(8,128)S(1)} %get-tuple-element.30.up_ref), channel_id=1, source_target_pairs={{0,2},{2,4},{4,6},{6,8},{8,10},{10,12},{12,14},{1,3},{3,5},{5,7},{... | collective-permute-start | bytes 589832 | tf_op jit(solution)/shard_map/ppermute | solution.py:493
  36.2 11.6 %collective-permute-start.5 = (f32[24,2048]{1,0:T(8,128)S(1)}, f32[24,2048]{1,0:T(8,128)S(1)}, u32[]{:S(2)}, u32[]{:S(2)}) collective-permute-start(f32[24,2048]{1,0:T(8,128)S(1)} %get-tuple-element.31.down_ref), channel_id=1, source_target_pairs={{2,0},{4,2},{6,4},{8,6},{10,8},{12,10},{14,12},{3,1},{5,3},{7,5},{... | collective-permute-start | bytes 589832 | tf_op jit(solution)/shard_map/ppermute | solution.py:493
  50.1 4.3 %collective-permute-start.7 = (f32[2,256,1024]{2,1,0:T(8,128)S(1)}, f32[2,256,1024]{2,1,0:T(8,128)S(1)}, u32[]{:S(2)}, u32[]{:S(2)}) collective-permute-start(f32[2,256,1024]{2,1,0:T(8,128)S(1)} %get-tuple-element.37.fold_ref), channel_id=1, source_target_pairs={{0,1},{1,0},{2,3},{3,2},{4,5},{5,4},{6,7},{7,6},{8,9},{9,8},{10,11... | collective-permute-start | bytes 6291464 | tf_op jit(solution)/shard_map/ppermute | solution.py:523

commit v4 on v3

--- a/solution.py
+++ b/solution.py
@@ -141,21 +141,24 @@
     return jnp.concatenate([packed, turned], axis=0)
 
 
-def write_edges(here_ref, rows_x, field, span, up_ref, down_ref, xsend_ref, far_ref):
+def write_edges(here_ref, rows_x, field, span, one_ref, two_ref, xsend_ref, far_ref):
     rows_y = field.shape[0] // rows_x
     for layer in range(2):
         first_row = field[layer * rows_y : (layer + 1) * rows_y, span]
         last_row = field[(rows_x - 2 + layer) * rows_y : (rows_x - 1 + layer) * rows_y, span]
         xsend_ref[layer, :, span] = jnp.where(here_ref[3] > 0, last_row, first_row)
     low_half = iota((rows_x // 2, LANES), 1) % NVX < HALF
-    for ahead, to_ref, near, far in ((True, up_ref, rows_y - 1, rows_y - 2), (False, down_ref, 0, 1)):
-        side = 1 if ahead else 0
+    odd = here_ref[4]
+    for side, to_ref, down in ((0, one_ref, odd), (1, two_ref, 1 - odd)):
+        near = (1 - down) * (rows_y - 1)
+        far = down + (1 - down) * (rows_y - 2)
         for x in range(rows_x):
-            to_ref[x : x + 1, span] = field[x * rows_y + near : x * rows_y + near + 1, span]
-            far_ref[side, x : x + 1, span] = field[x * rows_y + far : x * rows_y + far + 1, span]
+            to_ref[x : x + 1, span] = field[pl.ds(x * rows_y + near, 1), span]
+            far_ref[side, x : x + 1, span] = field[pl.ds(x * rows_y + far, 1), span]
         for i in range(span.start, span.stop, LANES):
             at = slice(i, i + LANES)
-            to_ref[rows_x:, at] = pack_far(far_ref[side, :, at], ahead, low_half)
+            layer = far_ref[side, :, at]
+            to_ref[rows_x:, at] = jnp.where(down > 0, pack_far(layer, False, low_half), pack_far(layer, True, low_half))
 
 
 def edge_shapes(rows_x, rows_y, local_len):
@@ -164,14 +167,14 @@
     return [edge_y, edge_y, layers_x, pltpu.VMEM((2, rows_x, local_len), jnp.float32)]
 
 
-def stage_body(wide, rows_x, here_ref, from_ref, field, up_ref, down_ref, xsend_ref, far_ref, sems):
+def stage_body(wide, rows_x, here_ref, from_ref, field, one_ref, two_ref, xsend_ref, far_ref, sems):
     spans = [slice(i, i + wide) for i in range(0, field.shape[1], wide)]
     copies = [pltpu.make_async_copy(from_ref.at[:, s], field.at[:, s], sems.at[i]) for i, s in enumerate(spans)]
     for copy in copies:
         copy.start()
     for copy, span in zip(copies, spans):
         copy.wait()
-        write_edges(here_ref, rows_x, field, span, up_ref, down_ref, xsend_ref, far_ref)
+        write_edges(here_ref, rows_x, field, span, one_ref, two_ref, xsend_ref, far_ref)
 
 
 def stage(here, rows_x, field):
@@ -188,6 +191,13 @@
     )(here, pltpu.with_memory_space_constraint(field, pltpu.HBM))
 
 
+def beyond(here_ref, rows_x, one_ref, two_ref, cols):
+    odd = here_ref[4] > 0
+    one, two = one_ref[:, cols], two_ref[:, cols]
+    low, high = jnp.where(odd, one, two), jnp.where(odd, two, one)
+    return unpack_far(low[rows_x:], True), low[:rows_x], high[:rows_x], unpack_far(high[rows_x:], False)
+
+
 def minmod(a, b):
     return jnp.maximum(jnp.minimum(a, b), 0.0) + jnp.minimum(jnp.maximum(a, b), 0.0)
 
@@ -217,8 +227,8 @@
 
 def transport_body(wide, rows_x, whole, here_ref, field_ref, xhalo_ref, *rest):
     if whole:
-        ylo_ref, yhi_ref = rest[:2]
-        adv_ref, fold_ref, low_edge, high_edge = rest[-4:]
+        one_ref, two_ref = rest[:2]
+        adv_ref, fold_ref, low_edge, high_edge, low_near, high_near = rest[-6:]
     else:
         adv_ref, fold_ref = rest[-2:]
     cells, local_len = field_ref.shape
@@ -247,10 +257,9 @@
             for x in range(rows_x):
                 low_edge[x : x + 1] = field_ref[x * rows_y : x * rows_y + 1, cols]
                 high_edge[x : x + 1] = field_ref[(x + 1) * rows_y - 1 : (x + 1) * rows_y, cols]
-            low_far = unpack_far(ylo_ref[rows_x:, cols], True)
-            high_far = unpack_far(yhi_ref[rows_x:, cols], False)
-            low_edge[...] = face_y(low_far, ylo_ref[:rows_x, cols], low_edge[...])
-            high_edge[...] = face_y(high_edge[...], yhi_ref[:rows_x, cols], high_far)
+            low_far, low_near[...], high_near[...], high_far = beyond(here_ref, rows_x, one_ref, two_ref, cols)
+            low_edge[...] = face_y(low_far, low_near[...], low_edge[...])
+            high_edge[...] = face_y(high_edge[...], high_near[...], high_far)
 
         def row(i):
             if i < 0:
@@ -273,8 +282,8 @@
             row_term = jnp.where(ahead_x, face[x + 1] - face[x], face[x + 2] - face[x + 1])
             below, above = pltpu.roll(here, 1, 0), pltpu.roll(here, rows_y - 1, 0)
             if whole:
-                below = jnp.where(first_y, ylo_ref[x : x + 1, cols], below)
-                above = jnp.where(last_y, yhi_ref[x : x + 1, cols], above)
+                below = jnp.where(first_y, low_near[x : x + 1], below)
+                above = jnp.where(last_y, high_near[x : x + 1], above)
             mine = face_y(below, here, above)
             if not whole:
                 mine = jnp.where(first_y | last_y, 0.0, mine)
@@ -296,7 +305,7 @@
     lax.fori_loop(0, local_len // wide, chunk, 0)
 
 
-def columns_body(wide, rows_x, here_ref, up_ref, down_ref, far_ref, ylo_ref, yhi_ref, adv_in, fold_in, *rest):
+def columns_body(wide, rows_x, here_ref, one_ref, two_ref, far_ref, one_halo, two_halo, adv_in, fold_in, *rest):
     adv_ref, fold_ref, added, added_fold = rest[-4:]
     cells, local_len = adv_in.shape
     rows_y = cells // rows_x
@@ -314,12 +323,16 @@
         def face(f0, f1, f2):
             return ay * f1 + by * minmod(f1 - f0, f2 - f1)
 
-        low_near, low = ylo_ref[:rows_x, cols], down_ref[:rows_x, cols]
-        high, high_near = up_ref[:rows_x, cols], yhi_ref[:rows_x, cols]
-        before = face(unpack_far(ylo_ref[rows_x:, cols], True), low_near, low)
-        first = face(low_near, low, far_ref[0, :, cols])
-        last = face(far_ref[1, :, cols], high, high_near)
-        after = face(high, high_near, unpack_far(yhi_ref[rows_x:, cols], False))
+        low_far, low_near, high_near, high_far = beyond(here_ref, rows_x, one_halo, two_halo, cols)
+        odd = here_ref[4] > 0
+        one, two = one_ref[:rows_x, cols], two_ref[:rows_x, cols]
+        low, high = jnp.where(odd, one, two), jnp.where(odd, two, one)
+        one, two = far_ref[0, :, cols], far_ref[1, :, cols]
+        second, last_but_one = jnp.where(odd, one, two), jnp.where(odd, two, one)
+        before = face(low_far, low_near, low)
+        first = face(low_near, low, second)
+        last = face(last_but_one, high, high_near)
+        after = face(high, high_near, high_far)
         parts = [
             jnp.where(ahead, before - first, first),
             jnp.where(ahead, first, 0.0),
@@ -362,14 +375,14 @@
         in_specs=[SCALARS] + [WHOLE] * (2 + len(yhalos) + len(entries)),
         out_specs=[WHOLE] * 2,
         out_shape=[pltpu.VMEM(field.shape, jnp.float32), pltpu.VMEM((2, cells, local_len // 2), jnp.float32)],
-        scratch_shapes=[pltpu.VMEM((rows_x, wide), jnp.float32)] * (2 if yhalos else 0),
+        scratch_shapes=[pltpu.VMEM((rows_x, wide), jnp.float32)] * (4 if yhalos else 0),
         compiler_params=room(4),
         cost_estimate=SMALL,
         name="transport" if yhalos else "inner_transport",
     )(here, *map(in_vmem, (field, xhalo, *yhalos, *entries)))
 
 
-def add_columns(here, rows_x, up, down, far, ylo, yhi, advected, fold, entries):
+def add_columns(here, rows_x, one, two, far, one_halo, two_halo, advected, fold, entries):
     wide = 4 * LANES
     return pl.pallas_call(
         functools.partial(columns_body, wide, rows_x),
@@ -381,7 +394,7 @@
         compiler_params=room(4),
         cost_estimate=SMALL,
         name="add_columns",
-    )(here, *map(in_vmem, (up, down, far, ylo, yhi, advected, fold, *entries)))
+    )(here, *map(in_vmem, (one, two, far, one_halo, two_halo, advected, fold, *entries)))
 
 
 def split_into(value_ref, high, low):
@@ -426,7 +439,7 @@
     if last:
         out_ref, high, low, field, sems = rest
     else:
-        field, up_ref, down_ref, xsend_ref, far_ref, high, low = rest
+        field, one_ref, two_ref, xsend_ref, far_ref, high, low = rest
     cells, local_len = adv_ref.shape
     rows_y = cells // rows_x
     split_into(fold_ref, high, low)
@@ -458,7 +471,7 @@
             copy.start()
             copies.append(copy)
         else:
-            write_edges(here_ref, rows_x, field, span, up_ref, down_ref, xsend_ref, far_ref)
+            write_edges(here_ref, rows_x, field, span, one_ref, two_ref, xsend_ref, far_ref)
     for copy in copies:
         copy.wait()
 
@@ -488,9 +501,9 @@
     )(here, in_vmem(fold), in_vmem(entries[0]), in_vmem(entries[1]), in_vmem(part), in_vmem(advected), density, kind, inflow)
 
 
-def shifted(block, axis, by):
-    count = lax.axis_size(axis)
-    return lax.ppermute(block, axis, [(i, i + by) for i in range(count) if 0 <= i + by < count])
+def swapped(block, axis, first):
+    pairs = [(i, i + 1) for i in range(first, lax.axis_size(axis) - 1, 2)]
+    return lax.ppermute(block, axis, [pair for i, j in pairs for pair in ((i, j), (j, i))])
 
 
 def per_device(distribution, density, cell_type, inflow):
@@ -501,30 +514,30 @@
     at_x = lax.axis_index("gx")
     size_x = lax.axis_size("gx")
     assert size_x == 2 and verts == 2
-    here = jnp.stack([vert, jnp.int32(verts), (at_x > 0).astype(jnp.int32), (at_x < size_x - 1).astype(jnp.int32)])
+    here = jnp.stack([vert, jnp.int32(verts), (at_x > 0).astype(jnp.int32), (at_x < size_x - 1).astype(jnp.int32), lax.axis_index("gy") % 2])
     column_density = density.reshape(cells, 1)
     column_type = cell_type.reshape(cells, 1)
     row_inflow = inflow.reshape(1, local_len)
     swap = [(0, 1), (1, 0)]
-    field, up, down, send_x, far = stage(here, rows_x, distribution.reshape(cells, local_len))
+    field, one, two, send_x, far = stage(here, rows_x, distribution.reshape(cells, local_len))
     entries = None
     for step in range(STEPS):
         last = step == STEPS - 1
-        ylo = shifted(up, "gy", 1)
-        yhi = shifted(down, "gy", -1)
+        one_halo = swapped(one, "gy", 0)
+        two_halo = swapped(two, "gy", 1)
         xhalo = lax.ppermute(send_x, "gx", swap)
         if entries is None:
             entries = make_entries(here, local_len // NVX, verts, [column_density, column_type])
         if step == 0:
-            advected, fold = transport(here, rows_x, field, xhalo, [ylo, yhi], entries)
+            advected, fold = transport(here, rows_x, field, xhalo, [one_halo, two_halo], entries)
         else:
             advected, fold = transport(here, rows_x, field, xhalo, [], entries)
-            advected, fold = add_columns(here, rows_x, up, down, far, ylo, yhi, advected, fold, entries)
+            advected, fold = add_columns(here, rows_x, one, two, far, one_halo, two_halo, advected, fold, entries)
         other = lax.ppermute(fold, "vert", swap)
         part = own_gain(fold, entries)
         out = collide(here, rows_x, other, entries, part, advected, column_density, column_type, row_inflow, last)
         if not last:
-            field, up, down, send_x, far = out
+            field, one, two, send_x, far = out
     return out.reshape(rows_x, rows_y, local_len)
 
 

time: 60.5 us -> 57.2 us (0.945)
  the two profiles are of different devices: /device:TPU:19 before, /device:TPU:21 now
where the time goes in v4:
time: 57.2 us; the launch traced here: 57 us
  Pallas kernels  40 us (70%)
  starting transfers between devices  11 us (19%)
  waiting for transfers between devices  5.41 us (9%)
    pallas_call x2, Pallas kernels, collide(): pl.pallas_call(functools.partial(collide_body, wide, rows_x, last), in_sp...  11 us
    pallas_call x1, Pallas kernels, make_entries(): pl.pallas_call(functools.partial(entries_body, local, sources), in_specs=...  8.26 us
    pallas_call x2, Pallas kernels, transport(): pl.pallas_call(functools.partial(transport_body, wide, rows_x, bool(yhalo...  8.21 us
    pallas_call x2, Pallas kernels, own_gain(): pl.pallas_call(functools.partial(own_body, 2 * LANES), in_specs=[WHOLE] *...  7.22 us
    ppermute x4, starting transfers between devices, swapped(): lax.ppermute(block, axis, [pair for i, j in pairs for pair in ((i, j), (j...  6.57 us
    ppermute x2, waiting for transfers between devices, per_device(): xhalo = lax.ppermute(send_x, 'gx', swap)  5.06 us
    pallas_call x1, Pallas kernels, stage(): pl.pallas_call(functools.partial(stage_body, wide, rows_x), in_specs=[SCA...  2.97 us
    ppermute x2, starting transfers between devices, per_device(): other = lax.ppermute(fold, 'vert', swap)  2.85 us
  transfers between devices with their start and end apart: 8, of which 3 were waited for; matrix products, arithmetic and copies ran while one was open for 0% of the time, Pallas kernels for 34%

profile of v4, /device:TPU:21, one launch (start us, length us, event | category | flops | bytes accessed | tf_op | source)
XLA Modules:
  0.0 57.0 jit_solution(6589857006956000206)
XLA Ops:
  0.0 0.0 copy-start.1
  0.0 0.0 copy-start.2
  0.0 0.1 stack.27.here_ref
  0.1 3.0 %stage.1 = (f32[256,2048]{1,0:T(8,128)S(1)}, f32[24,2048]{1,0:T(8,128)}, f32[24,2048]{1,0:T(8,128)S(1)}, f32[2,16,2048]{2,1,0:T(8,128)S(1)}, f32[2,16,2048]{2,1,0:T(8,128)}) custom-call(s32[5]{0:T(128)S(1)} %stack.27.here_ref, f32[256,2048]{1,0:T(8,128)} %bitcast.9), custom_call_target="tpu_custom_call" | custom-call | tf_op jit(solution)/shard_map/stage/pallas_call | solution.py:183
  3.1 1.3 %collective-permute-start = (f32[2,16,2048]{2,1,0:T(8,128)S(1)}, f32[2,16,2048]{2,1,0:T(8,128)S(1)}, u32[]{:S(2)}, u32[]{:S(2)}) collective-permute-start(f32[2,16,2048]{2,1,0:T(8,128)S(1)} %get-tuple-element.23), channel_id=1, source_target_pairs={{0,16},{16,0},{1,17},{17,1},{2,18},{18,2},{3,19},{19,3},{4,20},{20... | collective-permute-start | bytes 786440 | tf_op jit(solution)/shard_map/ppermute | solution.py:528
  4.3 0.2 collective-permute-start.1
  4.6 4.1 %collective-permute-start.2 = (f32[24,2048]{1,0:T(8,128)S(1)}, f32[24,2048]{1,0:T(8,128)S(1)}, u32[]{:S(2)}, u32[]{:S(2)}) collective-permute-start(f32[24,2048]{1,0:T(8,128)S(1)} %get-tuple-element.25), channel_id=1, source_target_pairs={{2,4},{4,2},{6,8},{8,6},{10,12},{12,10},{3,5},{5,3},{7,9},{9,7},{1... | collective-permute-start | bytes 589832 | tf_op jit(solution)/shard_map/ppermute | solution.py:506
  8.7 0.0 copy-done.1
  8.7 0.1 reshape.22.rest_0_.density_ref
  8.8 0.0 copy-done.2
  8.9 0.1 reshape.23.rest_1_.type_ref
  9.0 8.3 %kernel_entries.1 = (bf16[2,2,1024,1024]{3,2,1,0:T(8,128)(2,1)S(1)}, bf16[2,2,1024,1024]{3,2,1,0:T(8,128)(2,1)S(1)}) custom-call(s32[5]{0:T(128)S(1)} %stack.27.here_ref, f32[256,1]{1,0:T(8,128)S(1)} %reshape.22.rest_0_.density_ref, s32[256,1]{1,0:T(8,128)S(1)} %reshape.23.rest_1_.type_ref), custom_call_target="tpu_custom_call" | custom-call | flops 1 | bytes 1 | tf_op jit(solution)/shard_map/kernel_entries/pallas_call | solution.py:118
  17.2 0.0 collective-permute-done.1.rest_0_
  17.2 0.0 collective-permute-done.2.rest_1_
  17.2 0.0 collective-permute-done.xhalo_ref
  17.3 4.2 %transport.1 = (f32[256,2048]{1,0:T(8,128)S(1)}, f32[2,256,1024]{2,1,0:T(8,128)S(1)}) custom-call(s32[5]{0:T(128)S(1)} %stack.27.here_ref, f32[256,2048]{1,0:T(8,128)S(1)} %get-tuple-element.22.field_ref, f32[2,16,2048]{2,1,0:T(8,128)S(1)} %collective-permute-done.xhalo_ref, f32[24,2048]{1,0:T(8,128)S(1)} %collective-permute-done.1.rest_0_, ...), custom_call_target="tpu_custom_call" | custom-call | flops 1 | bytes 1 | tf_op jit(solution)/shard_map/transport/pallas_call | solution.py:373
  21.5 0.0 copy-start
  21.5 1.6 %collective-permute-start.3 = (f32[2,256,1024]{2,1,0:T(8,128)S(1)}, f32[2,256,1024]{2,1,0:T(8,128)S(1)}, u32[]{:S(2)}, u32[]{:S(2)}) collective-permute-start(f32[2,256,1024]{2,1,0:T(8,128)S(1)} %get-tuple-element.28.fold_ref), channel_id=1, source_target_pairs={{0,1},{1,0},{2,3},{3,2},{4,5},{5,4},{6,7},{7,6},{8,9},{9,8},{10,11... | collective-permute-start | bytes 6291464 | tf_op jit(solution)/shard_map/ppermute | solution.py:536
  23.1 3.6 %own_gain.2.part_ref = f32[2,256,1024]{2,1,0:T(8,128)S(1)} custom-call(f32[2,256,1024]{2,1,0:T(8,128)S(1)} %get-tuple-element.28.fold_ref, bf16[2,2,1024,1024]{3,2,1,0:T(8,128)(2,1)S(1)} %get-tuple-element.26.rest_2_.hi_ref.rest_0_, bf16[2,2,1024,1024]{3,2,1,0:T(8,128)(2,1)S(1)} %get-tuple-element.27.rest_3_.lo_ref.rest_1_), custom_call_target="tpu_custom_call" | custom-call | flops 1 | bytes 1 | tf_op jit(solution)/shard_map/own_gain/pallas_call | solution.py:424
  26.7 0.2 collective-permute-done.3.fold_ref
  26.9 0.0 copy-done
  26.9 5.2 %collide.2 = (f32[256,2048]{1,0:T(8,128)S(1)}, f32[24,2048]{1,0:T(8,128)S(1)}, f32[24,2048]{1,0:T(8,128)S(1)}, f32[2,16,2048]{2,1,0:T(8,128)S(1)}, f32[2,16,2048]{2,1,0:T(8,128)S(1)}) custom-call(s32[5]{0:T(128)S(1)} %stack.27.here_ref, f32[2,256,1024]{2,1,0:T(8,128)S(1)} %collective-permute-done.3.fold_ref, ...), custom_call_target="tpu_custom_call" | custom-call | flops 1 | bytes 1 | tf_op jit(solution)/shard_map/collide/pallas_call | solution.py:492
  32.1 0.3 collective-permute-start.6
  32.4 0.0 collective-permute-start.4
  32.4 2.2 %collective-permute-start.5 = (f32[24,2048]{1,0:T(8,128)S(1)}, f32[24,2048]{1,0:T(8,128)S(1)}, u32[]{:S(2)}, u32[]{:S(2)}) collective-permute-start(f32[24,2048]{1,0:T(8,128)S(1)} %get-tuple-element.31.two_ref), channel_id=1, source_target_pairs={{2,4},{4,2},{6,8},{8,6},{10,12},{12,10},{3,5},{5,3},{7,9},{9,7},{1... | collective-permute-start | bytes 589832 | tf_op jit(solution)/shard_map/ppermute | solution.py:506
  34.6 5.1 %collective-permute-done.6.xhalo_ref = f32[2,16,2048]{2,1,0:T(8,128)S(1)} collective-permute-done((f32[2,16,2048]{2,1,0:T(8,128)S(1)}, f32[2,16,2048]{2,1,0:T(8,128)S(1)}, u32[]{:S(2)}, u32[]{:S(2)}) %collective-permute-start.6) | collective-permute-done | bytes 262176 | tf_op jit(solution)/shard_map/ppermute | solution.py:528
  39.6 4.0 %inner_transport.1 = (f32[256,2048]{1,0:T(8,128)S(1)}, f32[2,256,1024]{2,1,0:T(8,128)S(1)}) custom-call(s32[5]{0:T(128)S(1)} %stack.27.here_ref, f32[256,2048]{1,0:T(8,128)S(1)} %get-tuple-element.33.field_ref, f32[2,16,2048]{2,1,0:T(8,128)S(1)} %collective-permute-done.6.xhalo_ref, bf16[2,2,1024,1024]{3,2,1,0:T(8,128)(2,1)S(1)} %get-tuple-element.26.rest_2_.hi_ref.rest_0_, ...), custom_call_target="tpu_custom_call" | custom-call | flops 1 | bytes 1 | tf_op jit(solution)/shard_map/inner_transport/pallas_call | solution.py:373
  43.6 0.0 collective-permute-done.4.one_halo
  43.6 0.0 collective-permute-done.5.two_halo
  43.6 2.4 %add_columns.1 = (f32[256,2048]{1,0:T(8,128)S(1)}, f32[2,256,1024]{2,1,0:T(8,128)S(1)}) custom-call(s32[5]{0:T(128)S(1)} %stack.27.here_ref, f32[24,2048]{1,0:T(8,128)S(1)} %get-tuple-element.30.one_ref, f32[24,2048]{1,0:T(8,128)S(1)} %get-tuple-element.31.two_ref, ...), custom_call_target="tpu_custom_call", output_to_operand_aliasing={{0}: (6, {}), {1}: (7, {})} | custom-call | flops 1 | bytes 1 | tf_op jit(solution)/shard_map/add_columns/pallas_call | solution.py:387
  46.1 1.3 %collective-permute-start.7 = (f32[2,256,1024]{2,1,0:T(8,128)S(1)}, f32[2,256,1024]{2,1,0:T(8,128)S(1)}, u32[]{:S(2)}, u32[]{:S(2)}) collective-permute-start(f32[2,256,1024]{2,1,0:T(8,128)S(1)} %get-tuple-element.37.fold_ref), channel_id=1, source_target_pairs={{0,1},{1,0},{2,3},{3,2},{4,5},{5,4},{6,7},{7,6},{8,9},{9,8},{10,11... | collective-permute-start | bytes 6291464 | tf_op jit(solution)/shard_map/ppermute | solution.py:536
  47.3 3.6 %own_gain.3.part_ref = f32[2,256,1024]{2,1,0:T(8,128)S(1)} custom-call(f32[2,256,1024]{2,1,0:T(8,128)S(1)} %get-tuple-element.37.fold_ref, bf16[2,2,1024,1024]{3,2,1,0:T(8,128)(2,1)S(1)} %get-tuple-element.26.rest_2_.hi_ref.rest_0_, bf16[2,2,1024,1024]{3,2,1,0:T(8,128)(2,1)S(1)} %get-tuple-element.27.rest_3_.lo_ref.rest_1_), custom_call_target="tpu_custom_call" | custom-call | flops 1 | bytes 1 | tf_op jit(solution)/shard_map/own_gain/pallas_call | solution.py:424
  50.9 0.2 collective-permute-done.7.fold_ref
  51.1 5.7 %collide.3 = f32[256,2048]{1,0:T(8,128)} custom-call(s32[5]{0:T(128)S(1)} %stack.27.here_ref, f32[2,256,1024]{2,1,0:T(8,128)S(1)} %collective-permute-done.7.fold_ref, bf16[2,2,1024,1024]{3,2,1,0:T(8,128)(2,1)S(1)} %get-tuple-element.26.rest_2_.hi_ref.rest_0_, bf16[2,2,1024,1024]{3,2,1,0:T(8,128)(2,1)S(1)} %get-tuple-element.27.rest_3_.lo_ref.rest_1_, ...), custom_call_target="tpu_custom_call" | custom-call | flops 1 | bytes 1 | tf_op jit(solution)/shard_map/collide/pallas_call | solution.py:492
Async XLA Ops:
  0.0 8.7 %copy-start.1 = (f32[16,16]{1,0:T(8,128)S(1)}, f32[16,16]{1,0:T(8,128)}, u32[]{:S(2)}) copy-start(f32[16,16]{1,0:T(8,128)} %param.5) | copy-start | bytes 3076
  0.0 8.8 %copy-start.2 = (s32[16,16]{1,0:T(8,128)S(1)}, s32[16,16]{1,0:T(8,128)}, u32[]{:S(2)}) copy-start(s32[16,16]{1,0:T(8,128)} %param.6) | copy-start | bytes 3076
  3.1 14.2 %collective-permute-start = (f32[2,16,2048]{2,1,0:T(8,128)S(1)}, f32[2,16,2048]{2,1,0:T(8,128)S(1)}, u32[]{:S(2)}, u32[]{:S(2)}) collective-permute-start(f32[2,16,2048]{2,1,0:T(8,128)S(1)} %get-tuple-element.23), channel_id=1, source_target_pairs={{0,16},{16,0},{1,17},{17,1},{2,18},{18,2},{3,19},{19,3},{4,20},{20... | collective-permute-start | bytes 786440 | tf_op jit(solution)/shard_map/ppermute | solution.py:528
  4.3 12.9 %collective-permute-start.1 = (f32[24,2048]{1,0:T(8,128)}, f32[24,2048]{1,0:T(8,128)S(1)}, u32[]{:S(2)}, u32[]{:S(2)}) collective-permute-start(f32[24,2048]{1,0:T(8,128)} %get-tuple-element.24), channel_id=1, source_target_pairs={{0,2},{2,0},{4,6},{6,4},{8,10},{10,8},{12,14},{14,12},{1,3},{3,1},... | collective-permute-start | bytes 589832 | tf_op jit(solution)/shard_map/ppermute | solution.py:506
  4.6 12.7 %collective-permute-start.2 = (f32[24,2048]{1,0:T(8,128)S(1)}, f32[24,2048]{1,0:T(8,128)S(1)}, u32[]{:S(2)}, u32[]{:S(2)}) collective-permute-start(f32[24,2048]{1,0:T(8,128)S(1)} %get-tuple-element.25), channel_id=1, source_target_pairs={{2,4},{4,2},{6,8},{8,6},{10,12},{12,10},{3,5},{5,3},{7,9},{9,7},{1... | collective-permute-start | bytes 589832 | tf_op jit(solution)/shard_map/ppermute | solution.py:506
  21.5 5.4 %copy-start = (f32[2048]{0:T(1024)S(1)}, f32[2048]{0:T(1024)}, u32[]{:S(2)}) copy-start(f32[2048]{0:T(1024)} %param.7) | copy-start | bytes 24580
  21.5 5.4 %collective-permute-start.3 = (f32[2,256,1024]{2,1,0:T(8,128)S(1)}, f32[2,256,1024]{2,1,0:T(8,128)S(1)}, u32[]{:S(2)}, u32[]{:S(2)}) collective-permute-start(f32[2,256,1024]{2,1,0:T(8,128)S(1)} %get-tuple-element.28.fold_ref), channel_id=1, source_target_pairs={{0,1},{1,0},{2,3},{3,2},{4,5},{5,4},{6,7},{7,6},{8,9},{9,8},{10,11... | collective-permute-start | bytes 6291464 | tf_op jit(solution)/shard_map/ppermute | solution.py:536
  32.1 7.6 %collective-permute-start.6 = (f32[2,16,2048]{2,1,0:T(8,128)S(1)}, f32[2,16,2048]{2,1,0:T(8,128)S(1)}, u32[]{:S(2)}, u32[]{:S(2)}) collective-permute-start(f32[2,16,2048]{2,1,0:T(8,128)S(1)} %get-tuple-element.34), channel_id=1, source_target_pairs={{0,16},{16,0},{1,17},{17,1},{2,18},{18,2},{3,19},{19,3},{4,20},{20... | collective-permute-start | bytes 786440 | tf_op jit(solution)/shard_map/ppermute | solution.py:528
  32.4 11.3 %collective-permute-start.4 = (f32[24,2048]{1,0:T(8,128)S(1)}, f32[24,2048]{1,0:T(8,128)S(1)}, u32[]{:S(2)}, u32[]{:S(2)}) collective-permute-start(f32[24,2048]{1,0:T(8,128)S(1)} %get-tuple-element.30.one_ref), channel_id=1, source_target_pairs={{0,2},{2,0},{4,6},{6,4},{8,10},{10,8},{12,14},{14,12},{1,3},{3,1},... | collective-permute-start | bytes 589832 | tf_op jit(solution)/shard_map/ppermute | solution.py:506
  32.4 11.3 %collective-permute-start.5 = (f32[24,2048]{1,0:T(8,128)S(1)}, f32[24,2048]{1,0:T(8,128)S(1)}, u32[]{:S(2)}, u32[]{:S(2)}) collective-permute-start(f32[24,2048]{1,0:T(8,128)S(1)} %get-tuple-element.31.two_ref), channel_id=1, source_target_pairs={{2,4},{4,2},{6,8},{8,6},{10,12},{12,10},{3,5},{5,3},{7,9},{9,7},{1... | collective-permute-start | bytes 589832 | tf_op jit(solution)/shard_map/ppermute | solution.py:506
  46.1 5.1 %collective-permute-start.7 = (f32[2,256,1024]{2,1,0:T(8,128)S(1)}, f32[2,256,1024]{2,1,0:T(8,128)S(1)}, u32[]{:S(2)}, u32[]{:S(2)}) collective-permute-start(f32[2,256,1024]{2,1,0:T(8,128)S(1)} %get-tuple-element.37.fold_ref), channel_id=1, source_target_pairs={{0,1},{1,0},{2,3},{3,2},{4,5},{5,4},{6,7},{7,6},{8,9},{9,8},{10,11... | collective-permute-start | bytes 6291464 | tf_op jit(solution)/shard_map/ppermute | solution.py:536

commit v5 on v4

--- a/solution.py
+++ b/solution.py
@@ -23,13 +23,18 @@
 
 MIB = 1024 * 1024
 WHOLE = pl.BlockSpec(memory_space=pltpu.VMEM)
-SCALARS = pl.BlockSpec(memory_space=pltpu.SMEM)
 
 EXPONENT = 0.125 * math.log2(math.e)
 ENTRY_SCALE = grad_scale * spacing * spacing * math.sqrt(EXPONENT)
 
 
 SMALL = pl.CostEstimate(flops=1, bytes_accessed=1, transcendentals=0)
+
+
+def place():
+    at_x = lax.axis_index("gx")
+    more = (at_x > 0, at_x < lax.axis_size("gx") - 1)
+    return [lax.axis_index("vert"), lax.axis_size("vert"), *(m.astype(jnp.int32) for m in more), lax.axis_index("gy") % 2]
 
 
 def room(mib):
@@ -56,7 +61,8 @@
     return lax.rem(slot, 2) * 2 + lax.div(slot, 2)
 
 
-def entries_body(local, sources, here_ref, *rest):
+def entries_body(local, sources, *rest):
+    here_ref = place()
     hi_ref, lo_ref, energy_ref, gauss_ref = rest[-4:]
     me = here_ref[0]
     groups = local // GROUP
@@ -112,19 +118,19 @@
     lax.fori_loop(0, sources * GROUP, one, 0)
 
 
-def make_entries(here, local, sources, ahead_of):
+def make_entries(local, sources, ahead_of):
     size = local * HALF
     shape = pltpu.VMEM((sources, 2, size, size), jnp.bfloat16)
     return pl.pallas_call(
         functools.partial(entries_body, local, sources),
-        in_specs=[SCALARS] + [WHOLE] * len(ahead_of),
+        in_specs=[WHOLE] * len(ahead_of),
         out_specs=[WHOLE, WHOLE],
         out_shape=[shape, shape],
         scratch_shapes=[pltpu.VMEM(((local // GROUP) ** 2, LANES), jnp.float32)] * 2,
         compiler_params=room(8),
         cost_estimate=SMALL,
         name="kernel_entries",
-    )(here, *map(in_vmem, ahead_of))
+    )(*map(in_vmem, ahead_of))
 
 
 def pack_far(far, ahead, low_half):
@@ -141,24 +147,46 @@
     return jnp.concatenate([packed, turned], axis=0)
 
 
-def write_edges(here_ref, rows_x, field, span, one_ref, two_ref, xsend_ref, far_ref):
+def outer_columns(field, rows_x, span, upper):
     rows_y = field.shape[0] // rows_x
+    half = rows_y // 2
+    at = iota((half, span.stop - span.start), 0)
+    shift = 1 - half if upper else 0
+    nears, fars = [], []
+    for first in range(0, rows_x, half):
+        near = far = None
+        for s in range(half):
+            start = (first + s) * rows_y + (half if upper else 0)
+            turned = pltpu.roll(field[start : start + half, span], (s + shift) % half, 0)
+            near = turned if near is None else jnp.where(at == s, turned, near)
+            beside = (s - 1 if upper else s + 1) % half
+            far = turned if far is None else jnp.where(at == beside, turned, far)
+        nears.append(near)
+        fars.append(pltpu.roll(far, 1 if upper else half - 1, 0))
+    return jnp.concatenate(nears, axis=0), jnp.concatenate(fars, axis=0)
+
+
+def write_edges(here_ref, rows_x, field, span, edge_refs):
+    one_ref, two_ref, xsend_ref, far_ref = edge_refs
+    rows_y = field.shape[0] // rows_x
+    to_next = here_ref[3] > 0
     for layer in range(2):
-        first_row = field[layer * rows_y : (layer + 1) * rows_y, span]
-        last_row = field[(rows_x - 2 + layer) * rows_y : (rows_x - 1 + layer) * rows_y, span]
-        xsend_ref[layer, :, span] = jnp.where(here_ref[3] > 0, last_row, first_row)
+        low_row, high_row = (field[x * rows_y : (x + 1) * rows_y, span] for x in (layer, rows_x - 2 + layer))
+        xsend_ref[layer, :, span] = jnp.where(to_next, high_row, low_row)
+    odd = here_ref[4] > 0
+    low_near, low_far = outer_columns(field, rows_x, span, False)
+    high_near, high_far = outer_columns(field, rows_x, span, True)
+    one_ref[:rows_x, span] = jnp.where(odd, low_near, high_near)
+    two_ref[:rows_x, span] = jnp.where(odd, high_near, low_near)
+    far_ref[0, :, span] = jnp.where(odd, low_far, high_far)
+    far_ref[1, :, span] = jnp.where(odd, high_far, low_far)
     low_half = iota((rows_x // 2, LANES), 1) % NVX < HALF
-    odd = here_ref[4]
-    for side, to_ref, down in ((0, one_ref, odd), (1, two_ref, 1 - odd)):
-        near = (1 - down) * (rows_y - 1)
-        far = down + (1 - down) * (rows_y - 2)
-        for x in range(rows_x):
-            to_ref[x : x + 1, span] = field[pl.ds(x * rows_y + near, 1), span]
-            far_ref[side, x : x + 1, span] = field[pl.ds(x * rows_y + far, 1), span]
-        for i in range(span.start, span.stop, LANES):
-            at = slice(i, i + LANES)
-            layer = far_ref[side, :, at]
-            to_ref[rows_x:, at] = jnp.where(down > 0, pack_far(layer, False, low_half), pack_far(layer, True, low_half))
+    for i in range(0, span.stop - span.start, LANES):
+        at = slice(span.start + i, span.start + i + LANES)
+        low = pack_far(low_far[:, i : i + LANES], False, low_half)
+        high = pack_far(high_far[:, i : i + LANES], True, low_half)
+        one_ref[rows_x:, at] = jnp.where(odd, low, high)
+        two_ref[rows_x:, at] = jnp.where(odd, high, low)
 
 
 def edge_shapes(rows_x, rows_y, local_len):
@@ -167,28 +195,30 @@
     return [edge_y, edge_y, layers_x, pltpu.VMEM((2, rows_x, local_len), jnp.float32)]
 
 
-def stage_body(wide, rows_x, here_ref, from_ref, field, one_ref, two_ref, xsend_ref, far_ref, sems):
+def stage_body(wide, rows_x, from_ref, field, *rest):
+    here_ref = place()
+    *edge_refs, sems = rest
     spans = [slice(i, i + wide) for i in range(0, field.shape[1], wide)]
     copies = [pltpu.make_async_copy(from_ref.at[:, s], field.at[:, s], sems.at[i]) for i, s in enumerate(spans)]
     for copy in copies:
         copy.start()
     for copy, span in zip(copies, spans):
         copy.wait()
-        write_edges(here_ref, rows_x, field, span, one_ref, two_ref, xsend_ref, far_ref)
-
-
-def stage(here, rows_x, field):
+        write_edges(here_ref, rows_x, field, span, edge_refs)
+
+
+def stage(rows_x, field):
     cells, local_len = field.shape
     wide = local_len // 4
     return pl.pallas_call(
         functools.partial(stage_body, wide, rows_x),
-        in_specs=[SCALARS, pl.BlockSpec(memory_space=pltpu.HBM)],
+        in_specs=[pl.BlockSpec(memory_space=pltpu.HBM)],
         out_specs=[WHOLE] * 5,
         out_shape=[pltpu.VMEM(field.shape, jnp.float32)] + edge_shapes(rows_x, cells // rows_x, local_len),
         scratch_shapes=[pltpu.SemaphoreType.DMA((4,))],
         compiler_params=room(4),
         name="stage",
-    )(here, pltpu.with_memory_space_constraint(field, pltpu.HBM))
+    )(pltpu.with_memory_space_constraint(field, pltpu.HBM))
 
 
 def beyond(here_ref, rows_x, one_ref, two_ref, cols):
@@ -225,9 +255,10 @@
     return jnp.where(even, near, far), jnp.where(even, far, near)
 
 
-def transport_body(wide, rows_x, whole, here_ref, field_ref, xhalo_ref, *rest):
+def transport_body(wide, rows_x, whole, field_ref, xhalo_ref, *rest):
+    here_ref = place()
     if whole:
-        one_ref, two_ref = rest[:2]
+        one_halo, two_halo, one_ref, two_ref = rest[:4]
         adv_ref, fold_ref, low_edge, high_edge, low_near, high_near = rest[-6:]
     else:
         adv_ref, fold_ref = rest[-2:]
@@ -254,12 +285,11 @@
             return ay * f1 + by * minmod(f1 - f0, f2 - f1)
 
         if whole:
-            for x in range(rows_x):
-                low_edge[x : x + 1] = field_ref[x * rows_y : x * rows_y + 1, cols]
-                high_edge[x : x + 1] = field_ref[(x + 1) * rows_y - 1 : (x + 1) * rows_y, cols]
-            low_far, low_near[...], high_near[...], high_far = beyond(here_ref, rows_x, one_ref, two_ref, cols)
-            low_edge[...] = face_y(low_far, low_near[...], low_edge[...])
-            high_edge[...] = face_y(high_edge[...], high_near[...], high_far)
+            low_far, low_near[...], high_near[...], high_far = beyond(here_ref, rows_x, one_halo, two_halo, cols)
+            odd = here_ref[4] > 0
+            one, two = one_ref[:rows_x, cols], two_ref[:rows_x, cols]
+            low_edge[...] = face_y(low_far, low_near[...], jnp.where(odd, one, two))
+            high_edge[...] = face_y(jnp.where(odd, two, one), high_near[...], high_far)
 
         def row(i):
             if i < 0:
@@ -280,18 +310,19 @@
             x = i - 1
             here = near[0]
             row_term = jnp.where(ahead_x, face[x + 1] - face[x], face[x + 2] - face[x + 1])
-            below, above = pltpu.roll(here, 1, 0), pltpu.roll(here, rows_y - 1, 0)
             if whole:
-                below = jnp.where(first_y, low_near[x : x + 1], below)
-                above = jnp.where(last_y, high_near[x : x + 1], above)
-            mine = face_y(below, here, above)
-            if not whole:
+                below = jnp.where(first_y, low_near[x : x + 1], pltpu.roll(here, 1, 0))
+                above = jnp.where(last_y, high_near[x : x + 1], pltpu.roll(here, rows_y - 1, 0))
+                mine = face_y(below, here, above)
+                mine_below = jnp.where(first_y, low_edge[x : x + 1], pltpu.roll(mine, 1, 0))
+                mine_above = jnp.where(last_y, high_edge[x : x + 1], pltpu.roll(mine, rows_y - 1, 0))
+                col_term = jnp.where(ahead_y, mine - mine_below, mine_above - mine)
+            else:
+                rise = here - pltpu.roll(here, 1, 0)
+                mine = ay * here + by * minmod(rise, pltpu.roll(rise, rows_y - 1, 0))
                 mine = jnp.where(first_y | last_y, 0.0, mine)
-            mine_below, mine_above = pltpu.roll(mine, 1, 0), pltpu.roll(mine, rows_y - 1, 0)
-            if whole:
-                mine_below = jnp.where(first_y, low_edge[x : x + 1], mine_below)
-                mine_above = jnp.where(last_y, high_edge[x : x + 1], mine_above)
-            col_term = jnp.where(ahead_y, mine - mine_below, mine_above - mine)
+                step = mine - pltpu.roll(mine, 1, 0)
+                col_term = jnp.where(ahead_y, step, pltpu.roll(step, rows_y - 1, 0))
             moved = here - row_term - col_term
             at = slice(x * rows_y, (x + 1) * rows_y)
             adv_ref[at, cols] = moved
@@ -305,12 +336,32 @@
     lax.fori_loop(0, local_len // wide, chunk, 0)
 
 
-def columns_body(wide, rows_x, here_ref, one_ref, two_ref, far_ref, one_halo, two_halo, adv_in, fold_in, *rest):
-    adv_ref, fold_ref, added, added_fold = rest[-4:]
+def columns_body(wide, rows_x, one_ref, two_ref, far_ref, one_halo, two_halo, adv_in, fold_in, *rest):
+    here_ref = place()
+    adv_ref, fold_ref = rest[-2:]
     cells, local_len = adv_in.shape
     rows_y = cells // rows_x
     half = rows_y // 2
     masks = fold_masks(rows_x)
+
+    def spread(parts, from_ref, to_ref, cols):
+        at = iota((half, parts[0].shape[1]), 0)
+        even = at % 2 == 0
+        for first in range(0, rows_x, half):
+            for upper in range(2):
+                a, b = (part[first : first + half] for part in parts[2 * upper : 2 * upper + 2])
+                b = pltpu.roll(b, 1, 0)
+                pairs = jnp.where(even, a, b), jnp.where(even, b, a)
+                place = upper * (half - 2)
+                here = (at == place) | (at == place + 1)
+                done = []
+                for s in range(half):
+                    start = (first + s) * rows_y + upper * half
+                    rows = slice(start, start + half)
+                    more = jnp.where(here, pltpu.roll(pairs[s % 2], (place - s) % half, 0), 0.0)
+                    done.append((rows, from_ref[rows, cols] + more))
+                for rows, value in done:
+                    to_ref[rows, cols] = value
 
     def chunk(c, carry):
         cols = pl.ds(pl.multiple_of(c * wide, wide), wide)
@@ -339,62 +390,45 @@
             jnp.where(ahead, 0.0, -last),
             jnp.where(ahead, -last, last - after),
         ]
-        for i, part in enumerate(parts):
-            at = slice(i * rows_x, (i + 1) * rows_x)
-            added[at] = part
-            for j in range(0, wide, 2 * LANES):
-                both = folded(part[:, j : j + LANES], part[:, j + LANES : j + 2 * LANES], *masks)
-                for parity in range(2):
-                    added_fold[parity, at, j // 2 : j // 2 + LANES] = both[parity]
-
-        def spread(ref, x, upper, at_y):
-            i = 2 if upper else 0
-            first, second = (ref[(i + k) * rows_x + x : (i + k) * rows_x + x + 1, :] for k in range(2))
-            place = half - 2 if upper else 0
-            return jnp.where(at_y == place, first, jnp.where(at_y == place + 1, second, 0.0))
-
-        at_y = iota((half, wide), 0)
-        at_y_fold = iota((half, wide // 2), 0)
-        for x in range(rows_x):
-            for upper in range(2):
-                rows = slice(x * rows_y + upper * half, x * rows_y + (upper + 1) * half)
-                adv_ref[rows, cols] = adv_in[rows, cols] + spread(added, x, upper, at_y)
-                for parity in range(2):
-                    more = spread(added_fold.at[parity], x, upper, at_y_fold)
-                    fold_ref[parity, rows, fold_cols] = fold_in[parity, rows, fold_cols] + more
+        spread(parts, adv_in, adv_ref, cols)
+        both = []
+        for part in parts:
+            pairs = [folded(part[:, j : j + LANES], part[:, j + LANES : j + 2 * LANES], *masks) for j in range(0, wide, 2 * LANES)]
+            both.append([jnp.concatenate(tiles, axis=1) for tiles in zip(*pairs)])
+        for parity in range(2):
+            spread([pair[parity] for pair in both], fold_in.at[parity], fold_ref.at[parity], fold_cols)
         return carry
 
     lax.fori_loop(0, local_len // wide, chunk, 0)
 
 
-def transport(here, rows_x, field, xhalo, yhalos, entries):
+def transport(rows_x, field, xhalo, yhalos, entries):
     cells, local_len = field.shape
     wide = 4 * LANES
     return pl.pallas_call(
         functools.partial(transport_body, wide, rows_x, bool(yhalos)),
-        in_specs=[SCALARS] + [WHOLE] * (2 + len(yhalos) + len(entries)),
+        in_specs=[WHOLE] * (2 + len(yhalos) + len(entries)),
         out_specs=[WHOLE] * 2,
         out_shape=[pltpu.VMEM(field.shape, jnp.float32), pltpu.VMEM((2, cells, local_len // 2), jnp.float32)],
         scratch_shapes=[pltpu.VMEM((rows_x, wide), jnp.float32)] * (4 if yhalos else 0),
         compiler_params=room(4),
         cost_estimate=SMALL,
         name="transport" if yhalos else "inner_transport",
-    )(here, *map(in_vmem, (field, xhalo, *yhalos, *entries)))
-
-
-def add_columns(here, rows_x, one, two, far, one_halo, two_halo, advected, fold, entries):
+    )(*map(in_vmem, (field, xhalo, *yhalos, *entries)))
+
+
+def add_columns(rows_x, one, two, far, one_halo, two_halo, advected, fold, entries):
     wide = 4 * LANES
     return pl.pallas_call(
         functools.partial(columns_body, wide, rows_x),
-        in_specs=[SCALARS] + [WHOLE] * (7 + len(entries)),
+        in_specs=[WHOLE] * (7 + len(entries)),
         out_specs=[WHOLE] * 2,
         out_shape=[pltpu.VMEM(advected.shape, jnp.float32), pltpu.VMEM(fold.shape, jnp.float32)],
-        scratch_shapes=[pltpu.VMEM((4 * rows_x, wide), jnp.float32), pltpu.VMEM((2, 4 * rows_x, wide // 2), jnp.float32)],
-        input_output_aliases={6: 0, 7: 1},
+        input_output_aliases={5: 0, 6: 1},
         compiler_params=room(4),
         cost_estimate=SMALL,
         name="add_columns",
-    )(here, *map(in_vmem, (one, two, far, one_halo, two_halo, advected, fold, *entries)))
+    )(*map(in_vmem, (one, two, far, one_halo, two_halo, advected, fold, *entries)))
 
 
 def split_into(value_ref, high, low):
@@ -434,18 +468,18 @@
 
 
 def collide_body(
-    wide, rows_x, last, here_ref, fold_ref, hi_ref, lo_ref, part_ref, adv_ref, density_ref, type_ref, inflow_ref, *rest
+    wide, rows_x, last, fold_ref, hi_ref, lo_ref, part_ref, adv_ref, density_ref, type_ref, inflow_ref, *rest
 ):
+    here_ref = place()
     if last:
         out_ref, high, low, field, sems = rest
     else:
-        field, one_ref, two_ref, xsend_ref, far_ref, high, low = rest
+        field, *edge_refs, high, low = rest
     cells, local_len = adv_ref.shape
     rows_y = cells // rows_x
     split_into(fold_ref, high, low)
     even_slot, turned = fold_masks(cells)
     rate = jnp.broadcast_to(collision_rate * density_ref[...], (cells, LANES))
-    gain_rate = rate * ENTRY_SCALE
     kind = jnp.broadcast_to(type_ref[...], (cells, LANES))
     wall = kind == 1
     inlet = kind == 2
@@ -463,20 +497,21 @@
                 vx, vy = velocity_parts(here_ref[0] * local_len + first + iota((1, LANES), 1))
                 nu = 1.0 + (vx * vx + vy * vy) / 8.0
                 moved = adv_ref[:, at]
-                done = moved + (gain_rate * gain - rate * (nu * moved))
+                done = moved + rate * (ENTRY_SCALE * gain - nu * moved)
                 field[:, at] = jnp.where(wall, 0.0, jnp.where(inlet, inflow_ref[:, at], done))
-        span = slice(2 * j * wide, 2 * (j + 1) * wide)
-        if last:
-            copy = pltpu.make_async_copy(field.at[:, span], out_ref.at[:, span], sems.at[j])
-            copy.start()
-            copies.append(copy)
-        else:
-            write_edges(here_ref, rows_x, field, span, one_ref, two_ref, xsend_ref, far_ref)
+            span = slice(first - LANES, first + LANES)
+            if last:
+                i = first // (2 * LANES)
+                copy = pltpu.make_async_copy(field.at[:, span], out_ref.at[:, span], sems.at[i])
+                copy.start()
+                copies.append(copy)
+            else:
+                write_edges(here_ref, rows_x, field, span, edge_refs)
     for copy in copies:
         copy.wait()
 
 
-def collide(here, rows_x, fold, entries, part, advected, density, kind, inflow, last):
+def collide(rows_x, fold, entries, part, advected, density, kind, inflow, last):
     _, cells, size = fold.shape
     local_len = advected.shape[1]
     wide = 2 * LANES
@@ -484,21 +519,21 @@
     if last:
         out_specs = pl.BlockSpec(memory_space=pl.ANY)
         out_shape = jax.ShapeDtypeStruct(advected.shape, jnp.float32)
-        scratch = halves + [pltpu.VMEM(advected.shape, jnp.float32), pltpu.SemaphoreType.DMA((size // wide,))]
+        scratch = halves + [pltpu.VMEM(advected.shape, jnp.float32), pltpu.SemaphoreType.DMA((size // LANES,))]
     else:
         out_specs = [WHOLE] * 5
         out_shape = [pltpu.VMEM(advected.shape, jnp.float32)] + edge_shapes(rows_x, cells // rows_x, local_len)
         scratch = halves
     return pl.pallas_call(
         functools.partial(collide_body, wide, rows_x, last),
-        in_specs=[SCALARS] + [WHOLE] * 8,
+        in_specs=[WHOLE] * 8,
         out_specs=out_specs,
         out_shape=out_shape,
         scratch_shapes=scratch,
         compiler_params=room(12),
         cost_estimate=SMALL,
         name="collide",
-    )(here, in_vmem(fold), in_vmem(entries[0]), in_vmem(entries[1]), in_vmem(part), in_vmem(advected), density, kind, inflow)
+    )(in_vmem(fold), in_vmem(entries[0]), in_vmem(entries[1]), in_vmem(part), in_vmem(advected), density, kind, inflow)
 
 
 def swapped(block, axis, first):
@@ -514,12 +549,11 @@
     at_x = lax.axis_index("gx")
     size_x = lax.axis_size("gx")
     assert size_x == 2 and verts == 2
-    here = jnp.stack([vert, jnp.int32(verts), (at_x > 0).astype(jnp.int32), (at_x < size_x - 1).astype(jnp.int32), lax.axis_index("gy") % 2])
     column_density = density.reshape(cells, 1)
     column_type = cell_type.reshape(cells, 1)
     row_inflow = inflow.reshape(1, local_len)
     swap = [(0, 1), (1, 0)]
-    field, one, two, send_x, far = stage(here, rows_x, distribution.reshape(cells, local_len))
+    field, one, two, send_x, far = stage(rows_x, distribution.reshape(cells, local_len))
     entries = None
     for step in range(STEPS):
         last = step == STEPS - 1
@@ -527,15 +561,15 @@
         two_halo = swapped(two, "gy", 1)
         xhalo = lax.ppermute(send_x, "gx", swap)
         if entries is None:
-            entries = make_entries(here, local_len // NVX, verts, [column_density, column_type])
+            entries = make_entries(local_len // NVX, verts, [column_density, column_type])
         if step == 0:
-            advected, fold = transport(here, rows_x, field, xhalo, [one_halo, two_halo], entries)
+            advected, fold = transport(rows_x, field, xhalo, [one_halo, two_halo, one, two], entries)
         else:
-            advected, fold = transport(here, rows_x, field, xhalo, [], entries)
-            advected, fold = add_columns(here, rows_x, one, two, far, one_halo, two_halo, advected, fold, entries)
+            advected, fold = transport(rows_x, field, xhalo, [], entries)
+            advected, fold = add_columns(rows_x, one, two, far, one_halo, two_halo, advected, fold, entries)
         other = lax.ppermute(fold, "vert", swap)
         part = own_gain(fold, entries)
-        out = collide(here, rows_x, other, entries, part, advected, column_density, column_type, row_inflow, last)
+        out = collide(rows_x, other, entries, part, advected, column_density, column_type, row_inflow, last)
         if not last:
             field, one, two, send_x, far = out
     return out.reshape(rows_x, rows_y, local_len)

time: 57.2 us -> 52.2 us (0.913)
  the two profiles are of different devices: /device:TPU:21 before, /device:TPU:19 now
where the time goes in v5:
time: 52.2 us; the launch traced here: 51.6 us
  Pallas kernels  35.1 us (67%)
  starting transfers between devices  12.8 us (25%)
  waiting for transfers between devices  3.23 us (6%)
    pallas_call x2, Pallas kernels, collide(): pl.pallas_call(functools.partial(collide_body, wide, rows_x, last), in_sp...  9.55 us
    pallas_call x1, Pallas kernels, make_entries(): pl.pallas_call(functools.partial(entries_body, local, sources), in_specs=...  7.71 us
    ppermute x4, starting transfers between devices, swapped(): lax.ppermute(block, axis, [pair for i, j in pairs for pair in ((i, j), (j...  7.7 us
    pallas_call x2, Pallas kernels, own_gain(): pl.pallas_call(functools.partial(own_body, 2 * LANES), in_specs=[WHOLE] *...  7.2 us
    pallas_call x2, Pallas kernels, transport(): pl.pallas_call(functools.partial(transport_body, wide, rows_x, bool(yhalo...  6.92 us
    ppermute x2, starting transfers between devices, per_device(): other = lax.ppermute(fold, 'vert', swap)  3.49 us
    pallas_call x1, Pallas kernels, stage(): pl.pallas_call(functools.partial(stage_body, wide, rows_x), in_specs=[pl....  2.43 us
    ppermute x2, waiting for transfers between devices, per_device(): xhalo = lax.ppermute(send_x, 'gx', swap)  1.84 us
  transfers between devices with their start and end apart: 8, of which 4 were waited for; matrix products, arithmetic and copies ran while one was open for 0% of the time, Pallas kernels for 35%

profile of v5, /device:TPU:19, one launch (start us, length us, event | category | flops | bytes accessed | tf_op | source)
XLA Modules:
  0.0 51.6 jit_solution(17898377078421062308)
XLA Ops:
  0.0 0.0 copy-start.1
  0.0 0.0 copy-start.2
  0.0 2.4 %stage.1 = (f32[256,2048]{1,0:T(8,128)S(1)}, f32[24,2048]{1,0:T(8,128)S(1)}, f32[24,2048]{1,0:T(8,128)S(1)}, f32[2,16,2048]{2,1,0:T(8,128)}, f32[2,16,2048]{2,1,0:T(8,128)}) custom-call(f32[256,2048]{1,0:T(8,128)} %bitcast.5), custom_call_target="tpu_custom_call" | custom-call | tf_op jit(solution)/shard_map/stage/pallas_call | solution.py:213
  2.4 0.3 collective-permute-start
  2.8 1.2 %collective-permute-start.1 = (f32[24,2048]{1,0:T(8,128)S(1)}, f32[24,2048]{1,0:T(8,128)S(1)}, u32[]{:S(2)}, u32[]{:S(2)}) collective-permute-start(f32[24,2048]{1,0:T(8,128)S(1)} %get-tuple-element.24.rest_2_), channel_id=1, source_target_pairs={{0,2},{2,0},{4,6},{6,4},{8,10},{10,8},{12,14},{14,12},{1,3},{3,1},... | collective-permute-start | bytes 589832 | tf_op jit(solution)/shard_map/ppermute | solution.py:541
  4.0 2.0 %collective-permute-start.2 = (f32[24,2048]{1,0:T(8,128)S(1)}, f32[24,2048]{1,0:T(8,128)S(1)}, u32[]{:S(2)}, u32[]{:S(2)}) collective-permute-start(f32[24,2048]{1,0:T(8,128)S(1)} %get-tuple-element.25.rest_3_), channel_id=1, source_target_pairs={{2,4},{4,2},{6,8},{8,6},{10,12},{12,10},{3,5},{5,3},{7,9},{9,7},{1... | collective-permute-start | bytes 589832 | tf_op jit(solution)/shard_map/ppermute | solution.py:541
  6.0 0.0 copy-done.1
  6.0 0.1 reshape.20.rest_0_.density_ref
  6.1 0.0 copy-done.2
  6.1 0.1 reshape.21.rest_1_.type_ref
  6.2 7.7 %kernel_entries.1 = (bf16[2,2,1024,1024]{3,2,1,0:T(8,128)(2,1)S(1)}, bf16[2,2,1024,1024]{3,2,1,0:T(8,128)(2,1)S(1)}) custom-call(f32[256,1]{1,0:T(8,128)S(1)} %reshape.20.rest_0_.density_ref, s32[256,1]{1,0:T(8,128)S(1)} %reshape.21.rest_1_.type_ref), custom_call_target="tpu_custom_call" | custom-call | flops 1 | bytes 1 | tf_op jit(solution)/shard_map/kernel_entries/pallas_call | solution.py:124
  14.0 0.0 collective-permute-done.1.rest_0_
  14.0 0.0 collective-permute-done.2.rest_1_
  14.0 0.0 collective-permute-done.xhalo_ref
  14.0 3.6 %transport.1 = (f32[256,2048]{1,0:T(8,128)S(1)}, f32[2,256,1024]{2,1,0:T(8,128)S(1)}) custom-call(f32[256,2048]{1,0:T(8,128)S(1)} %get-tuple-element.22.field_ref, f32[2,16,2048]{2,1,0:T(8,128)S(1)} %collective-permute-done.xhalo_ref, f32[24,2048]{1,0:T(8,128)S(1)} %collective-permute-done.1.rest_0_, f32[24,2048]{1,0:T(8,128)S(1)} %collective-permute-done.2.rest_1_, ...), custom_call_target="tpu_custom_call" | custom-call | flops 1 | bytes 1 | tf_op jit(solution)/shard_map/transport/pallas_call | solution.py:408
  17.6 0.0 copy-start
  17.6 1.6 %collective-permute-start.3 = (f32[2,256,1024]{2,1,0:T(8,128)S(1)}, f32[2,256,1024]{2,1,0:T(8,128)S(1)}, u32[]{:S(2)}, u32[]{:S(2)}) collective-permute-start(f32[2,256,1024]{2,1,0:T(8,128)S(1)} %get-tuple-element.28.fold_ref), channel_id=1, source_target_pairs={{0,1},{1,0},{2,3},{3,2},{4,5},{5,4},{6,7},{7,6},{8,9},{9,8},{10,11... | collective-permute-start | bytes 6291464 | tf_op jit(solution)/shard_map/ppermute | solution.py:570
  19.2 3.6 %own_gain.2.part_ref = f32[2,256,1024]{2,1,0:T(8,128)S(1)} custom-call(f32[2,256,1024]{2,1,0:T(8,128)S(1)} %get-tuple-element.28.fold_ref, bf16[2,2,1024,1024]{3,2,1,0:T(8,128)(2,1)S(1)} %get-tuple-element.26.rest_4_.hi_ref.rest_0_, bf16[2,2,1024,1024]{3,2,1,0:T(8,128)(2,1)S(1)} %get-tuple-element.27.rest_5_.lo_ref.rest_1_), custom_call_target="tpu_custom_call" | custom-call | flops 1 | bytes 1 | tf_op jit(solution)/shard_map/own_gain/pallas_call | solution.py:458
  22.8 0.2 collective-permute-done.3.fold_ref
  23.0 0.0 copy-done
  23.0 4.4 %collide.2 = (f32[256,2048]{1,0:T(8,128)S(1)}, f32[24,2048]{1,0:T(8,128)S(1)}, f32[24,2048]{1,0:T(8,128)S(1)}, f32[2,16,2048]{2,1,0:T(8,128)S(1)}, f32[2,16,2048]{2,1,0:T(8,128)S(1)}) custom-call(f32[2,256,1024]{2,1,0:T(8,128)S(1)} %collective-permute-done.3.fold_ref, bf16[2,2,1024,1024]{3,2,1,0:T(8,128)(2,1)S(1)} %get-tuple-element.26.rest_4_.hi_ref.rest_0_, ...), custom_call_target="tpu_custom_call" | custom-call | flops 1 | bytes 1 | tf_op jit(solution)/shard_map/collide/pallas_call | solution.py:527
  27.4 1.3 %collective-permute-start.6 = (f32[2,16,2048]{2,1,0:T(8,128)S(1)}, f32[2,16,2048]{2,1,0:T(8,128)S(1)}, u32[]{:S(2)}, u32[]{:S(2)}) collective-permute-start(f32[2,16,2048]{2,1,0:T(8,128)S(1)} %get-tuple-element.34), channel_id=1, source_target_pairs={{0,16},{16,0},{1,17},{17,1},{2,18},{18,2},{3,19},{19,3},{4,20},{20... | collective-permute-start | bytes 786440 | tf_op jit(solution)/shard_map/ppermute | solution.py:562
  28.7 2.4 %collective-permute-start.4 = (f32[24,2048]{1,0:T(8,128)S(1)}, f32[24,2048]{1,0:T(8,128)S(1)}, u32[]{:S(2)}, u32[]{:S(2)}) collective-permute-start(f32[24,2048]{1,0:T(8,128)S(1)} %get-tuple-element.30.one_ref), channel_id=1, source_target_pairs={{0,2},{2,0},{4,6},{6,4},{8,10},{10,8},{12,14},{14,12},{1,3},{3,1},... | collective-permute-start | bytes 589832 | tf_op jit(solution)/shard_map/ppermute | solution.py:541
  31.0 2.1 %collective-permute-start.5 = (f32[24,2048]{1,0:T(8,128)S(1)}, f32[24,2048]{1,0:T(8,128)S(1)}, u32[]{:S(2)}, u32[]{:S(2)}) collective-permute-start(f32[24,2048]{1,0:T(8,128)S(1)} %get-tuple-element.31.two_ref), channel_id=1, source_target_pairs={{2,4},{4,2},{6,8},{8,6},{10,12},{12,10},{3,5},{5,3},{7,9},{9,7},{1... | collective-permute-start | bytes 589832 | tf_op jit(solution)/shard_map/ppermute | solution.py:541
  33.1 1.8 %collective-permute-done.6.xhalo_ref = f32[2,16,2048]{2,1,0:T(8,128)S(1)} collective-permute-done((f32[2,16,2048]{2,1,0:T(8,128)S(1)}, f32[2,16,2048]{2,1,0:T(8,128)S(1)}, u32[]{:S(2)}, u32[]{:S(2)}) %collective-permute-start.6) | collective-permute-done | bytes 262176 | tf_op jit(solution)/shard_map/ppermute | solution.py:562
  35.0 3.3 %inner_transport.1 = (f32[256,2048]{1,0:T(8,128)S(1)}, f32[2,256,1024]{2,1,0:T(8,128)S(1)}) custom-call(f32[256,2048]{1,0:T(8,128)S(1)} %get-tuple-element.33.field_ref, f32[2,16,2048]{2,1,0:T(8,128)S(1)} %collective-permute-done.6.xhalo_ref, bf16[2,2,1024,1024]{3,2,1,0:T(8,128)(2,1)S(1)} %get-tuple-element.26.rest_4_.hi_ref.rest_0_, ...), custom_call_target="tpu_custom_call" | custom-call | flops 1 | bytes 1 | tf_op jit(solution)/shard_map/inner_transport/pallas_call | solution.py:408
  38.3 0.0 collective-permute-done.4.one_halo
  38.3 1.0 %collective-permute-done.5.two_halo = f32[24,2048]{1,0:T(8,128)S(1)} collective-permute-done((f32[24,2048]{1,0:T(8,128)S(1)}, f32[24,2048]{1,0:T(8,128)S(1)}, u32[]{:S(2)}, u32[]{:S(2)}) %collective-permute-start.5) | collective-permute-done | bytes 196640 | tf_op jit(solution)/shard_map/ppermute | solution.py:541
  39.3 1.3 %add_columns.1 = (f32[256,2048]{1,0:T(8,128)S(1)}, f32[2,256,1024]{2,1,0:T(8,128)S(1)}) custom-call(f32[24,2048]{1,0:T(8,128)S(1)} %get-tuple-element.30.one_ref, f32[24,2048]{1,0:T(8,128)S(1)} %get-tuple-element.31.two_ref, f32[2,16,2048]{2,1,0:T(8,128)S(1)} %get-tuple-element.32.far_ref, ...), custom_call_target="tpu_custom_call", output_to_operand_aliasing={{0}: (5, {}), {1}: (6, {})} | custom-call | flops 1 | bytes 1 | tf_op jit(solution)/shard_map/add_columns/pallas_call | solution.py:422
  40.6 1.9 %collective-permute-start.7 = (f32[2,256,1024]{2,1,0:T(8,128)S(1)}, f32[2,256,1024]{2,1,0:T(8,128)S(1)}, u32[]{:S(2)}, u32[]{:S(2)}) collective-permute-start(f32[2,256,1024]{2,1,0:T(8,128)S(1)} %get-tuple-element.37.fold_ref), channel_id=1, source_target_pairs={{0,1},{1,0},{2,3},{3,2},{4,5},{5,4},{6,7},{7,6},{8,9},{9,8},{10,11... | collective-permute-start | bytes 6291464 | tf_op jit(solution)/shard_map/ppermute | solution.py:570
  42.5 3.6 %own_gain.3.part_ref = f32[2,256,1024]{2,1,0:T(8,128)S(1)} custom-call(f32[2,256,1024]{2,1,0:T(8,128)S(1)} %get-tuple-element.37.fold_ref, bf16[2,2,1024,1024]{3,2,1,0:T(8,128)(2,1)S(1)} %get-tuple-element.26.rest_4_.hi_ref.rest_0_, bf16[2,2,1024,1024]{3,2,1,0:T(8,128)(2,1)S(1)} %get-tuple-element.27.rest_5_.lo_ref.rest_1_), custom_call_target="tpu_custom_call" | custom-call | flops 1 | bytes 1 | tf_op jit(solution)/shard_map/own_gain/pallas_call | solution.py:458
  46.1 0.2 collective-permute-done.7.fold_ref
  46.3 5.2 %collide.3 = f32[256,2048]{1,0:T(8,128)} custom-call(f32[2,256,1024]{2,1,0:T(8,128)S(1)} %collective-permute-done.7.fold_ref, bf16[2,2,1024,1024]{3,2,1,0:T(8,128)(2,1)S(1)} %get-tuple-element.26.rest_4_.hi_ref.rest_0_, bf16[2,2,1024,1024]{3,2,1,0:T(8,128)(2,1)S(1)} %get-tuple-element.27.rest_5_.lo_ref.rest_1_, f32[2,256,1024]{2,1,0:T(8,128)S(1)} %own_gain.3.part_ref, ...), custom_call_target="tpu_custom_call" | custom-call | flops 1 | bytes 1 | tf_op jit(solution)/shard_map/collide/pallas_call | solution.py:527
Async XLA Ops:
  0.0 6.0 %copy-start.1 = (f32[16,16]{1,0:T(8,128)S(1)}, f32[16,16]{1,0:T(8,128)}, u32[]{:S(2)}) copy-start(f32[16,16]{1,0:T(8,128)} %param.5) | copy-start | bytes 3076
  0.0 6.1 %copy-start.2 = (s32[16,16]{1,0:T(8,128)S(1)}, s32[16,16]{1,0:T(8,128)}, u32[]{:S(2)}) copy-start(s32[16,16]{1,0:T(8,128)} %param.6) | copy-start | bytes 3076
  2.4 11.6 %collective-permute-start = (f32[2,16,2048]{2,1,0:T(8,128)}, f32[2,16,2048]{2,1,0:T(8,128)S(1)}, u32[]{:S(2)}, u32[]{:S(2)}) collective-permute-start(f32[2,16,2048]{2,1,0:T(8,128)} %get-tuple-element.23), channel_id=1, source_target_pairs={{0,16},{16,0},{1,17},{17,1},{2,18},{18,2},{3,19},{19,3},{4,20},{20... | collective-permute-start | bytes 786440 | tf_op jit(solution)/shard_map/ppermute | solution.py:562
  2.8 11.2 %collective-permute-start.1 = (f32[24,2048]{1,0:T(8,128)S(1)}, f32[24,2048]{1,0:T(8,128)S(1)}, u32[]{:S(2)}, u32[]{:S(2)}) collective-permute-start(f32[24,2048]{1,0:T(8,128)S(1)} %get-tuple-element.24.rest_2_), channel_id=1, source_target_pairs={{0,2},{2,0},{4,6},{6,4},{8,10},{10,8},{12,14},{14,12},{1,3},{3,1},... | collective-permute-start | bytes 589832 | tf_op jit(solution)/shard_map/ppermute | solution.py:541
  4.0 10.0 %collective-permute-start.2 = (f32[24,2048]{1,0:T(8,128)S(1)}, f32[24,2048]{1,0:T(8,128)S(1)}, u32[]{:S(2)}, u32[]{:S(2)}) collective-permute-start(f32[24,2048]{1,0:T(8,128)S(1)} %get-tuple-element.25.rest_3_), channel_id=1, source_target_pairs={{2,4},{4,2},{6,8},{8,6},{10,12},{12,10},{3,5},{5,3},{7,9},{9,7},{1... | collective-permute-start | bytes 589832 | tf_op jit(solution)/shard_map/ppermute | solution.py:541
  17.6 5.4 %copy-start = (f32[2048]{0:T(1024)S(1)}, f32[2048]{0:T(1024)}, u32[]{:S(2)}) copy-start(f32[2048]{0:T(1024)} %param.7) | copy-start | bytes 24580
  17.6 5.4 %collective-permute-start.3 = (f32[2,256,1024]{2,1,0:T(8,128)S(1)}, f32[2,256,1024]{2,1,0:T(8,128)S(1)}, u32[]{:S(2)}, u32[]{:S(2)}) collective-permute-start(f32[2,256,1024]{2,1,0:T(8,128)S(1)} %get-tuple-element.28.fold_ref), channel_id=1, source_target_pairs={{0,1},{1,0},{2,3},{3,2},{4,5},{5,4},{6,7},{7,6},{8,9},{9,8},{10,11... | collective-permute-start | bytes 6291464 | tf_op jit(solution)/shard_map/ppermute | solution.py:570
  27.4 7.6 %collective-permute-start.6 = (f32[2,16,2048]{2,1,0:T(8,128)S(1)}, f32[2,16,2048]{2,1,0:T(8,128)S(1)}, u32[]{:S(2)}, u32[]{:S(2)}) collective-permute-start(f32[2,16,2048]{2,1,0:T(8,128)S(1)} %get-tuple-element.34), channel_id=1, source_target_pairs={{0,16},{16,0},{1,17},{17,1},{2,18},{18,2},{3,19},{19,3},{4,20},{20... | collective-permute-start | bytes 786440 | tf_op jit(solution)/shard_map/ppermute | solution.py:562
  28.7 9.6 %collective-permute-start.4 = (f32[24,2048]{1,0:T(8,128)S(1)}, f32[24,2048]{1,0:T(8,128)S(1)}, u32[]{:S(2)}, u32[]{:S(2)}) collective-permute-start(f32[24,2048]{1,0:T(8,128)S(1)} %get-tuple-element.30.one_ref), channel_id=1, source_target_pairs={{0,2},{2,0},{4,6},{6,4},{8,10},{10,8},{12,14},{14,12},{1,3},{3,1},... | collective-permute-start | bytes 589832 | tf_op jit(solution)/shard_map/ppermute | solution.py:541
  31.0 8.2 %collective-permute-start.5 = (f32[24,2048]{1,0:T(8,128)S(1)}, f32[24,2048]{1,0:T(8,128)S(1)}, u32[]{:S(2)}, u32[]{:S(2)}) collective-permute-start(f32[24,2048]{1,0:T(8,128)S(1)} %get-tuple-element.31.two_ref), channel_id=1, source_target_pairs={{2,4},{4,2},{6,8},{8,6},{10,12},{12,10},{3,5},{5,3},{7,9},{9,7},{1... | collective-permute-start | bytes 589832 | tf_op jit(solution)/shard_map/ppermute | solution.py:541
  40.6 5.7 %collective-permute-start.7 = (f32[2,256,1024]{2,1,0:T(8,128)S(1)}, f32[2,256,1024]{2,1,0:T(8,128)S(1)}, u32[]{:S(2)}, u32[]{:S(2)}) collective-permute-start(f32[2,256,1024]{2,1,0:T(8,128)S(1)} %get-tuple-element.37.fold_ref), channel_id=1, source_target_pairs={{0,1},{1,0},{2,3},{3,2},{4,5},{5,4},{6,7},{7,6},{8,9},{9,8},{10,11... | collective-permute-start | bytes 6291464 | tf_op jit(solution)/shard_map/ppermute | solution.py:570

commit v6 on v5

--- a/solution.py
+++ b/solution.py
@@ -445,41 +445,48 @@
     return dot(high[parity], tile) + (dot(low[parity], tile) + dot(high[parity], lo_ref[source, parity, :, cols]))
 
 
-def own_body(wide, fold_ref, hi_ref, lo_ref, out_ref, high, low):
+def own_body(wide, fold_ref, hi_ref, lo_ref, adv_ref, density_ref, out_ref, keep_ref, high, low):
+    here_ref = place()
     split_into(fold_ref, high, low)
     for j in range(fold_ref.shape[2] // wide):
         cols = slice(j * wide, (j + 1) * wide)
         for parity in range(2):
             out_ref[parity, :, cols] = product(high, low, hi_ref, lo_ref, 0, parity, cols)
-
-
-def own_gain(fold, entries):
+    cells, local_len = adv_ref.shape
+    rate = jnp.broadcast_to(collision_rate * density_ref[...], (cells, LANES))
+    for first in range(0, local_len, LANES):
+        at = slice(first, first + LANES)
+        vx, vy = velocity_parts(here_ref[0] * local_len + first + iota((1, LANES), 1))
+        nu = 1.0 + (vx * vx + vy * vy) / 8.0
+        keep_ref[:, at] = adv_ref[:, at] * (1.0 - rate * nu)
+
+
+def own_gain(fold, entries, advected, density):
     _, cells, size = fold.shape
     return pl.pallas_call(
         functools.partial(own_body, 2 * LANES),
-        in_specs=[WHOLE] * 3,
-        out_specs=WHOLE,
-        out_shape=pltpu.VMEM(fold.shape, jnp.float32),
+        in_specs=[WHOLE] * 5,
+        out_specs=[WHOLE] * 2,
+        out_shape=[pltpu.VMEM(fold.shape, jnp.float32), pltpu.VMEM(advected.shape, jnp.float32)],
         scratch_shapes=[pltpu.VMEM(fold.shape, jnp.bfloat16)] * 2,
         compiler_params=room(8),
         cost_estimate=SMALL,
         name="own_gain",
-    )(in_vmem(fold), *map(in_vmem, entries))
+    )(*map(in_vmem, (fold, *entries, advected, density)))
 
 
 def collide_body(
-    wide, rows_x, last, fold_ref, hi_ref, lo_ref, part_ref, adv_ref, density_ref, type_ref, inflow_ref, *rest
+    wide, rows_x, last, fold_ref, hi_ref, lo_ref, part_ref, keep_ref, density_ref, type_ref, inflow_ref, *rest
 ):
     here_ref = place()
     if last:
         out_ref, high, low, field, sems = rest
     else:
         field, *edge_refs, high, low = rest
-    cells, local_len = adv_ref.shape
-    rows_y = cells // rows_x
+    cells, local_len = keep_ref.shape
     split_into(fold_ref, high, low)
     even_slot, turned = fold_masks(cells)
-    rate = jnp.broadcast_to(collision_rate * density_ref[...], (cells, LANES))
+    gain_rate = jnp.broadcast_to(collision_rate * ENTRY_SCALE * density_ref[...], (cells, LANES))
     kind = jnp.broadcast_to(type_ref[...], (cells, LANES))
     wall = kind == 1
     inlet = kind == 2
@@ -494,10 +501,7 @@
             for side, gain in enumerate(unfolded(lower[:, group], upper[:, group], even_slot, turned)):
                 first = 2 * (j * wide + part * LANES) + side * LANES
                 at = slice(first, first + LANES)
-                vx, vy = velocity_parts(here_ref[0] * local_len + first + iota((1, LANES), 1))
-                nu = 1.0 + (vx * vx + vy * vy) / 8.0
-                moved = adv_ref[:, at]
-                done = moved + rate * (ENTRY_SCALE * gain - nu * moved)
+                done = keep_ref[:, at] + gain_rate * gain
                 field[:, at] = jnp.where(wall, 0.0, jnp.where(inlet, inflow_ref[:, at], done))
             span = slice(first - LANES, first + LANES)
             if last:
@@ -511,18 +515,18 @@
         copy.wait()
 
 
-def collide(rows_x, fold, entries, part, advected, density, kind, inflow, last):
+def collide(rows_x, fold, entries, part, kept, density, kind, inflow, last):
     _, cells, size = fold.shape
-    local_len = advected.shape[1]
+    local_len = kept.shape[1]
     wide = 2 * LANES
     halves = [pltpu.VMEM(fold.shape, jnp.bfloat16)] * 2
     if last:
         out_specs = pl.BlockSpec(memory_space=pl.ANY)
-        out_shape = jax.ShapeDtypeStruct(advected.shape, jnp.float32)
-        scratch = halves + [pltpu.VMEM(advected.shape, jnp.float32), pltpu.SemaphoreType.DMA((size // LANES,))]
+        out_shape = jax.ShapeDtypeStruct(kept.shape, jnp.float32)
+        scratch = halves + [pltpu.VMEM(kept.shape, jnp.float32), pltpu.SemaphoreType.DMA((size // LANES,))]
     else:
         out_specs = [WHOLE] * 5
-        out_shape = [pltpu.VMEM(advected.shape, jnp.float32)] + edge_shapes(rows_x, cells // rows_x, local_len)
+        out_shape = [pltpu.VMEM(kept.shape, jnp.float32)] + edge_shapes(rows_x, cells // rows_x, local_len)
         scratch = halves
     return pl.pallas_call(
         functools.partial(collide_body, wide, rows_x, last),
@@ -533,7 +537,7 @@
         compiler_params=room(12),
         cost_estimate=SMALL,
         name="collide",
-    )(in_vmem(fold), in_vmem(entries[0]), in_vmem(entries[1]), in_vmem(part), in_vmem(advected), density, kind, inflow)
+    )(in_vmem(fold), in_vmem(entries[0]), in_vmem(entries[1]), in_vmem(part), in_vmem(kept), density, kind, inflow)
 
 
 def swapped(block, axis, first):
@@ -568,8 +572,8 @@
             advected, fold = transport(rows_x, field, xhalo, [], entries)
             advected, fold = add_columns(rows_x, one, two, far, one_halo, two_halo, advected, fold, entries)
         other = lax.ppermute(fold, "vert", swap)
-        part = own_gain(fold, entries)
-        out = collide(rows_x, other, entries, part, advected, column_density, column_type, row_inflow, last)
+        part, kept = own_gain(fold, entries, advected, column_density)
+        out = collide(rows_x, other, entries, part, kept, column_density, column_type, row_inflow, last)
         if not last:
             field, one, two, send_x, far = out
     return out.reshape(rows_x, rows_y, local_len)

time: 52.2 us -> 51.7 us (level)
  transfers between devices with their start and end apart: 8 -> 8, of which waited for: 4 -> 4; matrix products, arithmetic and copies ran while one was open for 0% -> 0% of each run, Pallas kernels for 35% -> 36%
where the time goes in v6:
time: 51.7 us; the launch traced here: 51.1 us
  Pallas kernels  34.9 us (68%)
  starting transfers between devices  12.8 us (25%)
  waiting for transfers between devices  3 us (6%)
    pallas_call x2, Pallas kernels, collide(): pl.pallas_call(functools.partial(collide_body, wide, rows_x, last), in_sp...  9.11 us
    pallas_call x1, Pallas kernels, make_entries(): pl.pallas_call(functools.partial(entries_body, local, sources), in_specs=...  7.71 us
    ppermute x4, starting transfers between devices, swapped(): lax.ppermute(block, axis, [pair for i, j in pairs for pair in ((i, j), (j...  7.7 us
    pallas_call x2, Pallas kernels, own_gain(): pl.pallas_call(functools.partial(own_body, 2 * LANES), in_specs=[WHOLE] *...  7.43 us
    pallas_call x2, Pallas kernels, transport(): pl.pallas_call(functools.partial(transport_body, wide, rows_x, bool(yhalo...  6.92 us
    ppermute x2, starting transfers between devices, per_device(): other = lax.ppermute(fold, 'vert', swap)  3.48 us
    pallas_call x1, Pallas kernels, stage(): pl.pallas_call(functools.partial(stage_body, wide, rows_x), in_specs=[pl....  2.43 us
    ppermute x2, waiting for transfers between devices, per_device(): xhalo = lax.ppermute(send_x, 'gx', swap)  1.85 us
  transfers between devices with their start and end apart: 8, of which 4 were waited for; matrix products, arithmetic and copies ran while one was open for 0% of the time, Pallas kernels for 36%

profile of v6, /device:TPU:19, one launch (start us, length us, event | category | flops | bytes accessed | tf_op | source)
XLA Modules:
  0.0 51.1 jit_solution(13252881052908718302)
XLA Ops:
  0.0 0.0 copy-start.1
  0.0 0.0 copy-start.2
  0.0 2.4 %stage.1 = (f32[256,2048]{1,0:T(8,128)S(1)}, f32[24,2048]{1,0:T(8,128)S(1)}, f32[24,2048]{1,0:T(8,128)S(1)}, f32[2,16,2048]{2,1,0:T(8,128)}, f32[2,16,2048]{2,1,0:T(8,128)}) custom-call(f32[256,2048]{1,0:T(8,128)} %bitcast.5), custom_call_target="tpu_custom_call" | custom-call | tf_op jit(solution)/shard_map/stage/pallas_call | solution.py:213
  2.4 0.3 collective-permute-start
  2.8 1.2 %collective-permute-start.1 = (f32[24,2048]{1,0:T(8,128)S(1)}, f32[24,2048]{1,0:T(8,128)S(1)}, u32[]{:S(2)}, u32[]{:S(2)}) collective-permute-start(f32[24,2048]{1,0:T(8,128)S(1)} %get-tuple-element.28.rest_2_), channel_id=1, source_target_pairs={{0,2},{2,0},{4,6},{6,4},{8,10},{10,8},{12,14},{14,12},{1,3},{3,1},... | collective-permute-start | bytes 589832 | tf_op jit(solution)/shard_map/ppermute | solution.py:545
  4.0 2.0 %collective-permute-start.2 = (f32[24,2048]{1,0:T(8,128)S(1)}, f32[24,2048]{1,0:T(8,128)S(1)}, u32[]{:S(2)}, u32[]{:S(2)}) collective-permute-start(f32[24,2048]{1,0:T(8,128)S(1)} %get-tuple-element.29.rest_3_), channel_id=1, source_target_pairs={{2,4},{4,2},{6,8},{8,6},{10,12},{12,10},{3,5},{5,3},{7,9},{9,7},{1... | collective-permute-start | bytes 589832 | tf_op jit(solution)/shard_map/ppermute | solution.py:545
  6.0 0.0 copy-done.1
  6.0 0.1 reshape.20.rest_0_.density_ref
  6.1 0.0 copy-done.2
  6.1 0.1 reshape.21.rest_1_.type_ref
  6.2 7.7 %kernel_entries.1 = (bf16[2,2,1024,1024]{3,2,1,0:T(8,128)(2,1)S(1)}, bf16[2,2,1024,1024]{3,2,1,0:T(8,128)(2,1)S(1)}) custom-call(f32[256,1]{1,0:T(8,128)S(1)} %reshape.20.rest_0_.density_ref, s32[256,1]{1,0:T(8,128)S(1)} %reshape.21.rest_1_.type_ref), custom_call_target="tpu_custom_call" | custom-call | flops 1 | bytes 1 | tf_op jit(solution)/shard_map/kernel_entries/pallas_call | solution.py:124
  14.0 0.0 collective-permute-done.1.rest_0_
  14.0 0.0 collective-permute-done.2.rest_1_
  14.0 0.0 collective-permute-done.xhalo_ref
  14.0 3.6 %transport.1 = (f32[256,2048]{1,0:T(8,128)S(1)}, f32[2,256,1024]{2,1,0:T(8,128)S(1)}) custom-call(f32[256,2048]{1,0:T(8,128)S(1)} %get-tuple-element.26.field_ref, f32[2,16,2048]{2,1,0:T(8,128)S(1)} %collective-permute-done.xhalo_ref, f32[24,2048]{1,0:T(8,128)S(1)} %collective-permute-done.1.rest_0_, f32[24,2048]{1,0:T(8,128)S(1)} %collective-permute-done.2.rest_1_, ...), custom_call_target="tpu_custom_call" | custom-call | flops 1 | bytes 1 | tf_op jit(solution)/shard_map/transport/pallas_call | solution.py:408
  17.6 1.6 %collective-permute-start.3 = (f32[2,256,1024]{2,1,0:T(8,128)S(1)}, f32[2,256,1024]{2,1,0:T(8,128)S(1)}, u32[]{:S(2)}, u32[]{:S(2)}) collective-permute-start(f32[2,256,1024]{2,1,0:T(8,128)S(1)} %get-tuple-element.32.fold_ref), channel_id=1, source_target_pairs={{0,1},{1,0},{2,3},{3,2},{4,5},{5,4},{6,7},{7,6},{8,9},{9,8},{10,11... | collective-permute-start | bytes 6291464 | tf_op jit(solution)/shard_map/ppermute | solution.py:574
  19.2 0.0 copy-start
  19.2 3.7 %own_gain.2 = (f32[2,256,1024]{2,1,0:T(8,128)S(1)}, f32[256,2048]{1,0:T(8,128)S(1)}) custom-call(f32[2,256,1024]{2,1,0:T(8,128)S(1)} %get-tuple-element.32.fold_ref, bf16[2,2,1024,1024]{3,2,1,0:T(8,128)(2,1)S(1)} %get-tuple-element.30.rest_4_.hi_ref.rest_0_, bf16[2,2,1024,1024]{3,2,1,0:T(8,128)(2,1)S(1)} %get-tuple-element.31.rest_5_.lo_ref.rest_1_, ...), custom_call_target="tpu_custom_call" | custom-call | flops 1 | bytes 1 | tf_op jit(solution)/shard_map/own_gain/pallas_call | solution.py:466
  22.9 0.1 collective-permute-done.3.fold_ref
  23.0 0.0 copy-done
  23.0 4.2 %collide.2 = (f32[256,2048]{1,0:T(8,128)S(1)}, f32[24,2048]{1,0:T(8,128)S(1)}, f32[24,2048]{1,0:T(8,128)S(1)}, f32[2,16,2048]{2,1,0:T(8,128)S(1)}, f32[2,16,2048]{2,1,0:T(8,128)S(1)}) custom-call(f32[2,256,1024]{2,1,0:T(8,128)S(1)} %collective-permute-done.3.fold_ref, bf16[2,2,1024,1024]{3,2,1,0:T(8,128)(2,1)S(1)} %get-tuple-element.30.rest_4_.hi_ref.rest_0_, ...), custom_call_target="tpu_custom_call" | custom-call | flops 1 | bytes 1 | tf_op jit(solution)/shard_map/collide/pallas_call | solution.py:531
  27.2 1.3 %collective-permute-start.6 = (f32[2,16,2048]{2,1,0:T(8,128)S(1)}, f32[2,16,2048]{2,1,0:T(8,128)S(1)}, u32[]{:S(2)}, u32[]{:S(2)}) collective-permute-start(f32[2,16,2048]{2,1,0:T(8,128)S(1)} %get-tuple-element.40), channel_id=1, source_target_pairs={{0,16},{16,0},{1,17},{17,1},{2,18},{18,2},{3,19},{19,3},{4,20},{20... | collective-permute-start | bytes 786440 | tf_op jit(solution)/shard_map/ppermute | solution.py:566
  28.5 2.4 %collective-permute-start.4 = (f32[24,2048]{1,0:T(8,128)S(1)}, f32[24,2048]{1,0:T(8,128)S(1)}, u32[]{:S(2)}, u32[]{:S(2)}) collective-permute-start(f32[24,2048]{1,0:T(8,128)S(1)} %get-tuple-element.36.one_ref), channel_id=1, source_target_pairs={{0,2},{2,0},{4,6},{6,4},{8,10},{10,8},{12,14},{14,12},{1,3},{3,1},... | collective-permute-start | bytes 589832 | tf_op jit(solution)/shard_map/ppermute | solution.py:545
  30.8 2.1 %collective-permute-start.5 = (f32[24,2048]{1,0:T(8,128)S(1)}, f32[24,2048]{1,0:T(8,128)S(1)}, u32[]{:S(2)}, u32[]{:S(2)}) collective-permute-start(f32[24,2048]{1,0:T(8,128)S(1)} %get-tuple-element.37.two_ref), channel_id=1, source_target_pairs={{2,4},{4,2},{6,8},{8,6},{10,12},{12,10},{3,5},{5,3},{7,9},{9,7},{1... | collective-permute-start | bytes 589832 | tf_op jit(solution)/shard_map/ppermute | solution.py:545
  32.9 1.8 %collective-permute-done.6.xhalo_ref = f32[2,16,2048]{2,1,0:T(8,128)S(1)} collective-permute-done((f32[2,16,2048]{2,1,0:T(8,128)S(1)}, f32[2,16,2048]{2,1,0:T(8,128)S(1)}, u32[]{:S(2)}, u32[]{:S(2)}) %collective-permute-start.6) | collective-permute-done | bytes 262176 | tf_op jit(solution)/shard_map/ppermute | solution.py:566
  34.8 3.3 %inner_transport.1 = (f32[256,2048]{1,0:T(8,128)S(1)}, f32[2,256,1024]{2,1,0:T(8,128)S(1)}) custom-call(f32[256,2048]{1,0:T(8,128)S(1)} %get-tuple-element.39.field_ref, f32[2,16,2048]{2,1,0:T(8,128)S(1)} %collective-permute-done.6.xhalo_ref, bf16[2,2,1024,1024]{3,2,1,0:T(8,128)(2,1)S(1)} %get-tuple-element.30.rest_4_.hi_ref.rest_0_, ...), custom_call_target="tpu_custom_call" | custom-call | flops 1 | bytes 1 | tf_op jit(solution)/shard_map/inner_transport/pallas_call | solution.py:408
  38.0 0.0 collective-permute-done.4.one_halo
  38.1 1.0 %collective-permute-done.5.two_halo = f32[24,2048]{1,0:T(8,128)S(1)} collective-permute-done((f32[24,2048]{1,0:T(8,128)S(1)}, f32[24,2048]{1,0:T(8,128)S(1)}, u32[]{:S(2)}, u32[]{:S(2)}) %collective-permute-start.5) | collective-permute-done | bytes 196640 | tf_op jit(solution)/shard_map/ppermute | solution.py:545
  39.1 1.3 %add_columns.1 = (f32[256,2048]{1,0:T(8,128)S(1)}, f32[2,256,1024]{2,1,0:T(8,128)S(1)}) custom-call(f32[24,2048]{1,0:T(8,128)S(1)} %get-tuple-element.36.one_ref, f32[24,2048]{1,0:T(8,128)S(1)} %get-tuple-element.37.two_ref, f32[2,16,2048]{2,1,0:T(8,128)S(1)} %get-tuple-element.38.far_ref, ...), custom_call_target="tpu_custom_call", output_to_operand_aliasing={{0}: (5, {}), {1}: (6, {})} | custom-call | flops 1 | bytes 1 | tf_op jit(solution)/shard_map/add_columns/pallas_call | solution.py:422
  40.4 1.9 %collective-permute-start.7 = (f32[2,256,1024]{2,1,0:T(8,128)S(1)}, f32[2,256,1024]{2,1,0:T(8,128)S(1)}, u32[]{:S(2)}, u32[]{:S(2)}) collective-permute-start(f32[2,256,1024]{2,1,0:T(8,128)S(1)} %get-tuple-element.43.fold_ref), channel_id=1, source_target_pairs={{0,1},{1,0},{2,3},{3,2},{4,5},{5,4},{6,7},{7,6},{8,9},{9,8},{10,11... | collective-permute-start | bytes 6291464 | tf_op jit(solution)/shard_map/ppermute | solution.py:574
  42.3 3.7 %own_gain.3 = (f32[2,256,1024]{2,1,0:T(8,128)S(1)}, f32[256,2048]{1,0:T(8,128)S(1)}) custom-call(f32[2,256,1024]{2,1,0:T(8,128)S(1)} %get-tuple-element.43.fold_ref, bf16[2,2,1024,1024]{3,2,1,0:T(8,128)(2,1)S(1)} %get-tuple-element.30.rest_4_.hi_ref.rest_0_, bf16[2,2,1024,1024]{3,2,1,0:T(8,128)(2,1)S(1)} %get-tuple-element.31.rest_5_.lo_ref.rest_1_, ...), custom_call_target="tpu_custom_call" | custom-call | flops 1 | bytes 1 | tf_op jit(solution)/shard_map/own_gain/pallas_call | solution.py:466
  46.0 0.1 collective-permute-done.7.fold_ref
  46.1 4.9 %collide.3 = f32[256,2048]{1,0:T(8,128)} custom-call(f32[2,256,1024]{2,1,0:T(8,128)S(1)} %collective-permute-done.7.fold_ref, bf16[2,2,1024,1024]{3,2,1,0:T(8,128)(2,1)S(1)} %get-tuple-element.30.rest_4_.hi_ref.rest_0_, bf16[2,2,1024,1024]{3,2,1,0:T(8,128)(2,1)S(1)} %get-tuple-element.31.rest_5_.lo_ref.rest_1_, ...), custom_call_target="tpu_custom_call" | custom-call | flops 1 | bytes 1 | tf_op jit(solution)/shard_map/collide/pallas_call | solution.py:531
Async XLA Ops:
  0.0 6.0 %copy-start.1 = (f32[16,16]{1,0:T(8,128)S(1)}, f32[16,16]{1,0:T(8,128)}, u32[]{:S(2)}) copy-start(f32[16,16]{1,0:T(8,128)} %param.5) | copy-start | bytes 3076
  0.0 6.1 %copy-start.2 = (s32[16,16]{1,0:T(8,128)S(1)}, s32[16,16]{1,0:T(8,128)}, u32[]{:S(2)}) copy-start(s32[16,16]{1,0:T(8,128)} %param.6) | copy-start | bytes 3076
  2.4 11.6 %collective-permute-start = (f32[2,16,2048]{2,1,0:T(8,128)}, f32[2,16,2048]{2,1,0:T(8,128)S(1)}, u32[]{:S(2)}, u32[]{:S(2)}) collective-permute-start(f32[2,16,2048]{2,1,0:T(8,128)} %get-tuple-element.27), channel_id=1, source_target_pairs={{0,16},{16,0},{1,17},{17,1},{2,18},{18,2},{3,19},{19,3},{4,20},{20... | collective-permute-start | bytes 786440 | tf_op jit(solution)/shard_map/ppermute | solution.py:566
  2.8 11.2 %collective-permute-start.1 = (f32[24,2048]{1,0:T(8,128)S(1)}, f32[24,2048]{1,0:T(8,128)S(1)}, u32[]{:S(2)}, u32[]{:S(2)}) collective-permute-start(f32[24,2048]{1,0:T(8,128)S(1)} %get-tuple-element.28.rest_2_), channel_id=1, source_target_pairs={{0,2},{2,0},{4,6},{6,4},{8,10},{10,8},{12,14},{14,12},{1,3},{3,1},... | collective-permute-start | bytes 589832 | tf_op jit(solution)/shard_map/ppermute | solution.py:545
  4.0 10.0 %collective-permute-start.2 = (f32[24,2048]{1,0:T(8,128)S(1)}, f32[24,2048]{1,0:T(8,128)S(1)}, u32[]{:S(2)}, u32[]{:S(2)}) collective-permute-start(f32[24,2048]{1,0:T(8,128)S(1)} %get-tuple-element.29.rest_3_), channel_id=1, source_target_pairs={{2,4},{4,2},{6,8},{8,6},{10,12},{12,10},{3,5},{5,3},{7,9},{9,7},{1... | collective-permute-start | bytes 589832 | tf_op jit(solution)/shard_map/ppermute | solution.py:545
  17.6 5.4 %collective-permute-start.3 = (f32[2,256,1024]{2,1,0:T(8,128)S(1)}, f32[2,256,1024]{2,1,0:T(8,128)S(1)}, u32[]{:S(2)}, u32[]{:S(2)}) collective-permute-start(f32[2,256,1024]{2,1,0:T(8,128)S(1)} %get-tuple-element.32.fold_ref), channel_id=1, source_target_pairs={{0,1},{1,0},{2,3},{3,2},{4,5},{5,4},{6,7},{7,6},{8,9},{9,8},{10,11... | collective-permute-start | bytes 6291464 | tf_op jit(solution)/shard_map/ppermute | solution.py:574
  19.2 3.8 %copy-start = (f32[2048]{0:T(1024)S(1)}, f32[2048]{0:T(1024)}, u32[]{:S(2)}) copy-start(f32[2048]{0:T(1024)} %param.7) | copy-start | bytes 24580
  27.2 7.6 %collective-permute-start.6 = (f32[2,16,2048]{2,1,0:T(8,128)S(1)}, f32[2,16,2048]{2,1,0:T(8,128)S(1)}, u32[]{:S(2)}, u32[]{:S(2)}) collective-permute-start(f32[2,16,2048]{2,1,0:T(8,128)S(1)} %get-tuple-element.40), channel_id=1, source_target_pairs={{0,16},{16,0},{1,17},{17,1},{2,18},{18,2},{3,19},{19,3},{4,20},{20... | collective-permute-start | bytes 786440 | tf_op jit(solution)/shard_map/ppermute | solution.py:566
  28.5 9.6 %collective-permute-start.4 = (f32[24,2048]{1,0:T(8,128)S(1)}, f32[24,2048]{1,0:T(8,128)S(1)}, u32[]{:S(2)}, u32[]{:S(2)}) collective-permute-start(f32[24,2048]{1,0:T(8,128)S(1)} %get-tuple-element.36.one_ref), channel_id=1, source_target_pairs={{0,2},{2,0},{4,6},{6,4},{8,10},{10,8},{12,14},{14,12},{1,3},{3,1},... | collective-permute-start | bytes 589832 | tf_op jit(solution)/shard_map/ppermute | solution.py:545
  30.8 8.2 %collective-permute-start.5 = (f32[24,2048]{1,0:T(8,128)S(1)}, f32[24,2048]{1,0:T(8,128)S(1)}, u32[]{:S(2)}, u32[]{:S(2)}) collective-permute-start(f32[24,2048]{1,0:T(8,128)S(1)} %get-tuple-element.37.two_ref), channel_id=1, source_target_pairs={{2,4},{4,2},{6,8},{8,6},{10,12},{12,10},{3,5},{5,3},{7,9},{9,7},{1... | collective-permute-start | bytes 589832 | tf_op jit(solution)/shard_map/ppermute | solution.py:545
  40.4 5.7 %collective-permute-start.7 = (f32[2,256,1024]{2,1,0:T(8,128)S(1)}, f32[2,256,1024]{2,1,0:T(8,128)S(1)}, u32[]{:S(2)}, u32[]{:S(2)}) collective-permute-start(f32[2,256,1024]{2,1,0:T(8,128)S(1)} %get-tuple-element.43.fold_ref), channel_id=1, source_target_pairs={{0,1},{1,0},{2,3},{3,2},{4,5},{5,4},{6,7},{7,6},{8,9},{9,8},{10,11... | collective-permute-start | bytes 6291464 | tf_op jit(solution)/shard_map/ppermute | solution.py:574

commit v7 on v6

--- a/solution.py
+++ b/solution.py
@@ -445,7 +445,7 @@
     return dot(high[parity], tile) + (dot(low[parity], tile) + dot(high[parity], lo_ref[source, parity, :, cols]))
 
 
-def own_body(wide, fold_ref, hi_ref, lo_ref, adv_ref, density_ref, out_ref, keep_ref, high, low):
+def own_body(wide, fold_ref, hi_ref, lo_ref, adv_ref, density_ref, type_ref, inflow_ref, out_ref, keep_ref, high, low):
     here_ref = place()
     split_into(fold_ref, high, low)
     for j in range(fold_ref.shape[2] // wide):
@@ -454,29 +454,32 @@
             out_ref[parity, :, cols] = product(high, low, hi_ref, lo_ref, 0, parity, cols)
     cells, local_len = adv_ref.shape
     rate = jnp.broadcast_to(collision_rate * density_ref[...], (cells, LANES))
+    kind = jnp.broadcast_to(type_ref[...], (cells, LANES))
+    wall, inlet = kind == 1, kind == 2
     for first in range(0, local_len, LANES):
         at = slice(first, first + LANES)
         vx, vy = velocity_parts(here_ref[0] * local_len + first + iota((1, LANES), 1))
         nu = 1.0 + (vx * vx + vy * vy) / 8.0
-        keep_ref[:, at] = adv_ref[:, at] * (1.0 - rate * nu)
-
-
-def own_gain(fold, entries, advected, density):
+        kept = adv_ref[:, at] * (1.0 - rate * nu)
+        keep_ref[:, at] = jnp.where(wall, 0.0, jnp.where(inlet, inflow_ref[:, at], kept))
+
+
+def own_gain(fold, entries, advected, density, kind, inflow):
     _, cells, size = fold.shape
     return pl.pallas_call(
         functools.partial(own_body, 2 * LANES),
-        in_specs=[WHOLE] * 5,
+        in_specs=[WHOLE] * 7,
         out_specs=[WHOLE] * 2,
         out_shape=[pltpu.VMEM(fold.shape, jnp.float32), pltpu.VMEM(advected.shape, jnp.float32)],
         scratch_shapes=[pltpu.VMEM(fold.shape, jnp.bfloat16)] * 2,
         compiler_params=room(8),
         cost_estimate=SMALL,
         name="own_gain",
-    )(*map(in_vmem, (fold, *entries, advected, density)))
+    )(*map(in_vmem, (fold, *entries, advected, density, kind)), inflow)
 
 
 def collide_body(
-    wide, rows_x, last, fold_ref, hi_ref, lo_ref, part_ref, keep_ref, density_ref, type_ref, inflow_ref, *rest
+    wide, rows_x, last, fold_ref, hi_ref, lo_ref, part_ref, keep_ref, density_ref, type_ref, *rest
 ):
     here_ref = place()
     if last:
@@ -486,10 +489,9 @@
     cells, local_len = keep_ref.shape
     split_into(fold_ref, high, low)
     even_slot, turned = fold_masks(cells)
-    gain_rate = jnp.broadcast_to(collision_rate * ENTRY_SCALE * density_ref[...], (cells, LANES))
-    kind = jnp.broadcast_to(type_ref[...], (cells, LANES))
-    wall = kind == 1
-    inlet = kind == 2
+    gas = (type_ref[...] != 1) & (type_ref[...] != 2)
+    gain_rate = jnp.where(gas, collision_rate * ENTRY_SCALE * density_ref[...], 0.0)
+    gain_rate = jnp.broadcast_to(gain_rate, (cells, LANES))
     copies = []
     for j in range(local_len // (2 * wide)):
         cols = slice(j * wide, (j + 1) * wide)
@@ -501,8 +503,7 @@
             for side, gain in enumerate(unfolded(lower[:, group], upper[:, group], even_slot, turned)):
                 first = 2 * (j * wide + part * LANES) + side * LANES
                 at = slice(first, first + LANES)
-                done = keep_ref[:, at] + gain_rate * gain
-                field[:, at] = jnp.where(wall, 0.0, jnp.where(inlet, inflow_ref[:, at], done))
+                field[:, at] = keep_ref[:, at] + gain_rate * gain
             span = slice(first - LANES, first + LANES)
             if last:
                 i = first // (2 * LANES)
@@ -515,7 +516,7 @@
         copy.wait()
 
 
-def collide(rows_x, fold, entries, part, kept, density, kind, inflow, last):
+def collide(rows_x, fold, entries, part, kept, density, kind, last):
     _, cells, size = fold.shape
     local_len = kept.shape[1]
     wide = 2 * LANES
@@ -530,14 +531,14 @@
         scratch = halves
     return pl.pallas_call(
         functools.partial(collide_body, wide, rows_x, last),
-        in_specs=[WHOLE] * 8,
+        in_specs=[WHOLE] * 7,
         out_specs=out_specs,
         out_shape=out_shape,
         scratch_shapes=scratch,
         compiler_params=room(12),
         cost_estimate=SMALL,
         name="collide",
-    )(in_vmem(fold), in_vmem(entries[0]), in_vmem(entries[1]), in_vmem(part), in_vmem(kept), density, kind, inflow)
+    )(in_vmem(fold), in_vmem(entries[0]), in_vmem(entries[1]), in_vmem(part), in_vmem(kept), density, kind)
 
 
 def swapped(block, axis, first):
@@ -572,8 +573,8 @@
             advected, fold = transport(rows_x, field, xhalo, [], entries)
             advected, fold = add_columns(rows_x, one, two, far, one_halo, two_halo, advected, fold, entries)
         other = lax.ppermute(fold, "vert", swap)
-        part, kept = own_gain(fold, entries, advected, column_density)
-        out = collide(rows_x, other, entries, part, kept, column_density, column_type, row_inflow, last)
+        part, kept = own_gain(fold, entries, advected, column_density, column_type, row_inflow)
+        out = collide(rows_x, other, entries, part, kept, column_density, column_type, last)
         if not last:
             field, one, two, send_x, far = out
     return out.reshape(rows_x, rows_y, local_len)

time: 51.7 us -> 51.5 us (level)
  transfers between devices with their start and end apart: 8 -> 8, of which waited for: 4 -> 2; matrix products, arithmetic and copies ran while one was open for 0% -> 0% of each run, Pallas kernels for 36% -> 37%
where the time goes in v7:
time: 51.5 us; the launch traced here: 50.9 us
  Pallas kernels  34.7 us (67%)
  starting transfers between devices  12.8 us (25%)
  waiting for transfers between devices  2.87 us (6%)
    pallas_call x2, Pallas kernels, collide(): pl.pallas_call(functools.partial(collide_body, wide, rows_x, last), in_sp...  8.76 us
    pallas_call x1, Pallas kernels, make_entries(): pl.pallas_call(functools.partial(entries_body, local, sources), in_specs=...  7.71 us
    ppermute x4, starting transfers between devices, swapped(): lax.ppermute(block, axis, [pair for i, j in pairs for pair in ((i, j), (j...  7.7 us
    pallas_call x2, Pallas kernels, own_gain(): pl.pallas_call(functools.partial(own_body, 2 * LANES), in_specs=[WHOLE] *...  7.58 us
    pallas_call x2, Pallas kernels, transport(): pl.pallas_call(functools.partial(transport_body, wide, rows_x, bool(yhalo...  6.94 us
    ppermute x2, starting transfers between devices, per_device(): other = lax.ppermute(fold, 'vert', swap)  3.47 us
    pallas_call x1, Pallas kernels, stage(): pl.pallas_call(functools.partial(stage_body, wide, rows_x), in_specs=[pl....  2.43 us
    ppermute x2, waiting for transfers between devices, per_device(): xhalo = lax.ppermute(send_x, 'gx', swap)  1.85 us
  transfers between devices with their start and end apart: 8, of which 2 were waited for; matrix products, arithmetic and copies ran while one was open for 0% of the time, Pallas kernels for 37%

profile of v7, /device:TPU:19, one launch (start us, length us, event | category | flops | bytes accessed | tf_op | source)
XLA Modules:
  0.0 50.9 jit_solution(3440484448321000316)
XLA Ops:
  0.0 0.0 copy-start.1
  0.0 0.0 copy-start.2
  0.0 2.4 %stage.1 = (f32[256,2048]{1,0:T(8,128)S(1)}, f32[24,2048]{1,0:T(8,128)S(1)}, f32[24,2048]{1,0:T(8,128)S(1)}, f32[2,16,2048]{2,1,0:T(8,128)}, f32[2,16,2048]{2,1,0:T(8,128)}) custom-call(f32[256,2048]{1,0:T(8,128)} %bitcast.5), custom_call_target="tpu_custom_call" | custom-call | tf_op jit(solution)/shard_map/stage/pallas_call | solution.py:213
  2.4 0.3 collective-permute-start
  2.8 1.2 %collective-permute-start.1 = (f32[24,2048]{1,0:T(8,128)S(1)}, f32[24,2048]{1,0:T(8,128)S(1)}, u32[]{:S(2)}, u32[]{:S(2)}) collective-permute-start(f32[24,2048]{1,0:T(8,128)S(1)} %get-tuple-element.28.rest_2_), channel_id=1, source_target_pairs={{0,2},{2,0},{4,6},{6,4},{8,10},{10,8},{12,14},{14,12},{1,3},{3,1},... | collective-permute-start | bytes 589832 | tf_op jit(solution)/shard_map/ppermute | solution.py:546
  4.0 2.0 %collective-permute-start.2 = (f32[24,2048]{1,0:T(8,128)S(1)}, f32[24,2048]{1,0:T(8,128)S(1)}, u32[]{:S(2)}, u32[]{:S(2)}) collective-permute-start(f32[24,2048]{1,0:T(8,128)S(1)} %get-tuple-element.29.rest_3_), channel_id=1, source_target_pairs={{2,4},{4,2},{6,8},{8,6},{10,12},{12,10},{3,5},{5,3},{7,9},{9,7},{1... | collective-permute-start | bytes 589832 | tf_op jit(solution)/shard_map/ppermute | solution.py:546
  6.0 0.0 copy-done.1
  6.0 0.1 reshape.20.rest_0_.density_ref
  6.1 0.0 copy-done.2
  6.1 0.1 reshape.21.rest_1_.type_ref
  6.2 7.7 %kernel_entries.1 = (bf16[2,2,1024,1024]{3,2,1,0:T(8,128)(2,1)S(1)}, bf16[2,2,1024,1024]{3,2,1,0:T(8,128)(2,1)S(1)}) custom-call(f32[256,1]{1,0:T(8,128)S(1)} %reshape.20.rest_0_.density_ref, s32[256,1]{1,0:T(8,128)S(1)} %reshape.21.rest_1_.type_ref), custom_call_target="tpu_custom_call" | custom-call | flops 1 | bytes 1 | tf_op jit(solution)/shard_map/kernel_entries/pallas_call | solution.py:124
  14.0 0.0 collective-permute-done.1.rest_0_
  14.0 0.0 collective-permute-done.2.rest_1_
  14.0 0.0 collective-permute-done.xhalo_ref
  14.0 0.0 copy-start
  14.0 3.6 %transport.1 = (f32[256,2048]{1,0:T(8,128)S(1)}, f32[2,256,1024]{2,1,0:T(8,128)S(1)}) custom-call(f32[256,2048]{1,0:T(8,128)S(1)} %get-tuple-element.26.field_ref, f32[2,16,2048]{2,1,0:T(8,128)S(1)} %collective-permute-done.xhalo_ref, f32[24,2048]{1,0:T(8,128)S(1)} %collective-permute-done.1.rest_0_, f32[24,2048]{1,0:T(8,128)S(1)} %collective-permute-done.2.rest_1_, ...), custom_call_target="tpu_custom_call" | custom-call | flops 1 | bytes 1 | tf_op jit(solution)/shard_map/transport/pallas_call | solution.py:408
  17.7 1.6 %collective-permute-start.3 = (f32[2,256,1024]{2,1,0:T(8,128)S(1)}, f32[2,256,1024]{2,1,0:T(8,128)S(1)}, u32[]{:S(2)}, u32[]{:S(2)}) collective-permute-start(f32[2,256,1024]{2,1,0:T(8,128)S(1)} %get-tuple-element.32.fold_ref), channel_id=1, source_target_pairs={{0,1},{1,0},{2,3},{3,2},{4,5},{5,4},{6,7},{7,6},{8,9},{9,8},{10,11... | collective-permute-start | bytes 6291464 | tf_op jit(solution)/shard_map/ppermute | solution.py:575
  19.2 0.0 copy-done
  19.2 3.8 %own_gain.2 = (f32[2,256,1024]{2,1,0:T(8,128)S(1)}, f32[256,2048]{1,0:T(8,128)S(1)}) custom-call(f32[2,256,1024]{2,1,0:T(8,128)S(1)} %get-tuple-element.32.fold_ref, bf16[2,2,1024,1024]{3,2,1,0:T(8,128)(2,1)S(1)} %get-tuple-element.30.rest_4_.hi_ref.rest_0_, bf16[2,2,1024,1024]{3,2,1,0:T(8,128)(2,1)S(1)} %get-tuple-element.31.rest_5_.lo_ref.rest_1_, ...), custom_call_target="tpu_custom_call" | custom-call | flops 1 | bytes 1 | tf_op jit(solution)/shard_map/own_gain/pallas_call | solution.py:469
  23.0 0.0 collective-permute-done.3.fold_ref
  23.0 3.9 %collide.2 = (f32[256,2048]{1,0:T(8,128)S(1)}, f32[24,2048]{1,0:T(8,128)S(1)}, f32[24,2048]{1,0:T(8,128)S(1)}, f32[2,16,2048]{2,1,0:T(8,128)S(1)}, f32[2,16,2048]{2,1,0:T(8,128)S(1)}) custom-call(f32[2,256,1024]{2,1,0:T(8,128)S(1)} %collective-permute-done.3.fold_ref, bf16[2,2,1024,1024]{3,2,1,0:T(8,128)(2,1)S(1)} %get-tuple-element.30.rest_4_.hi_ref.rest_0_, ...), custom_call_target="tpu_custom_call" | custom-call | flops 1 | bytes 1 | tf_op jit(solution)/shard_map/collide/pallas_call | solution.py:532
  26.9 1.3 %collective-permute-start.6 = (f32[2,16,2048]{2,1,0:T(8,128)S(1)}, f32[2,16,2048]{2,1,0:T(8,128)S(1)}, u32[]{:S(2)}, u32[]{:S(2)}) collective-permute-start(f32[2,16,2048]{2,1,0:T(8,128)S(1)} %get-tuple-element.40), channel_id=1, source_target_pairs={{0,16},{16,0},{1,17},{17,1},{2,18},{18,2},{3,19},{19,3},{4,20},{20... | collective-permute-start | bytes 786440 | tf_op jit(solution)/shard_map/ppermute | solution.py:567
  28.1 2.4 %collective-permute-start.4 = (f32[24,2048]{1,0:T(8,128)S(1)}, f32[24,2048]{1,0:T(8,128)S(1)}, u32[]{:S(2)}, u32[]{:S(2)}) collective-permute-start(f32[24,2048]{1,0:T(8,128)S(1)} %get-tuple-element.36.one_ref), channel_id=1, source_target_pairs={{0,2},{2,0},{4,6},{6,4},{8,10},{10,8},{12,14},{14,12},{1,3},{3,1},... | collective-permute-start | bytes 589832 | tf_op jit(solution)/shard_map/ppermute | solution.py:546
  30.5 2.1 %collective-permute-start.5 = (f32[24,2048]{1,0:T(8,128)S(1)}, f32[24,2048]{1,0:T(8,128)S(1)}, u32[]{:S(2)}, u32[]{:S(2)}) collective-permute-start(f32[24,2048]{1,0:T(8,128)S(1)} %get-tuple-element.37.two_ref), channel_id=1, source_target_pairs={{2,4},{4,2},{6,8},{8,6},{10,12},{12,10},{3,5},{5,3},{7,9},{9,7},{1... | collective-permute-start | bytes 589832 | tf_op jit(solution)/shard_map/ppermute | solution.py:546
  32.6 1.9 %collective-permute-done.6.xhalo_ref = f32[2,16,2048]{2,1,0:T(8,128)S(1)} collective-permute-done((f32[2,16,2048]{2,1,0:T(8,128)S(1)}, f32[2,16,2048]{2,1,0:T(8,128)S(1)}, u32[]{:S(2)}, u32[]{:S(2)}) %collective-permute-start.6) | collective-permute-done | bytes 262176 | tf_op jit(solution)/shard_map/ppermute | solution.py:567
  34.5 3.3 %inner_transport.1 = (f32[256,2048]{1,0:T(8,128)S(1)}, f32[2,256,1024]{2,1,0:T(8,128)S(1)}) custom-call(f32[256,2048]{1,0:T(8,128)S(1)} %get-tuple-element.39.field_ref, f32[2,16,2048]{2,1,0:T(8,128)S(1)} %collective-permute-done.6.xhalo_ref, bf16[2,2,1024,1024]{3,2,1,0:T(8,128)(2,1)S(1)} %get-tuple-element.30.rest_4_.hi_ref.rest_0_, ...), custom_call_target="tpu_custom_call" | custom-call | flops 1 | bytes 1 | tf_op jit(solution)/shard_map/inner_transport/pallas_call | solution.py:408
  37.8 0.0 collective-permute-done.4.one_halo
  37.8 1.0 %collective-permute-done.5.two_halo = f32[24,2048]{1,0:T(8,128)S(1)} collective-permute-done((f32[24,2048]{1,0:T(8,128)S(1)}, f32[24,2048]{1,0:T(8,128)S(1)}, u32[]{:S(2)}, u32[]{:S(2)}) %collective-permute-start.5) | collective-permute-done | bytes 196640 | tf_op jit(solution)/shard_map/ppermute | solution.py:546
  38.8 1.3 %add_columns.1 = (f32[256,2048]{1,0:T(8,128)S(1)}, f32[2,256,1024]{2,1,0:T(8,128)S(1)}) custom-call(f32[24,2048]{1,0:T(8,128)S(1)} %get-tuple-element.36.one_ref, f32[24,2048]{1,0:T(8,128)S(1)} %get-tuple-element.37.two_ref, f32[2,16,2048]{2,1,0:T(8,128)S(1)} %get-tuple-element.38.far_ref, ...), custom_call_target="tpu_custom_call", output_to_operand_aliasing={{0}: (5, {}), {1}: (6, {})} | custom-call | flops 1 | bytes 1 | tf_op jit(solution)/shard_map/add_columns/pallas_call | solution.py:422
  40.1 1.9 %collective-permute-start.7 = (f32[2,256,1024]{2,1,0:T(8,128)S(1)}, f32[2,256,1024]{2,1,0:T(8,128)S(1)}, u32[]{:S(2)}, u32[]{:S(2)}) collective-permute-start(f32[2,256,1024]{2,1,0:T(8,128)S(1)} %get-tuple-element.43.fold_ref), channel_id=1, source_target_pairs={{0,1},{1,0},{2,3},{3,2},{4,5},{5,4},{6,7},{7,6},{8,9},{9,8},{10,11... | collective-permute-start | bytes 6291464 | tf_op jit(solution)/shard_map/ppermute | solution.py:575
  42.0 3.8 %own_gain.3 = (f32[2,256,1024]{2,1,0:T(8,128)S(1)}, f32[256,2048]{1,0:T(8,128)S(1)}) custom-call(f32[2,256,1024]{2,1,0:T(8,128)S(1)} %get-tuple-element.43.fold_ref, bf16[2,2,1024,1024]{3,2,1,0:T(8,128)(2,1)S(1)} %get-tuple-element.30.rest_4_.hi_ref.rest_0_, bf16[2,2,1024,1024]{3,2,1,0:T(8,128)(2,1)S(1)} %get-tuple-element.31.rest_5_.lo_ref.rest_1_, ...), custom_call_target="tpu_custom_call" | custom-call | flops 1 | bytes 1 | tf_op jit(solution)/shard_map/own_gain/pallas_call | solution.py:469
  45.8 0.0 collective-permute-done.7.fold_ref
  45.8 4.9 %collide.3 = f32[256,2048]{1,0:T(8,128)} custom-call(f32[2,256,1024]{2,1,0:T(8,128)S(1)} %collective-permute-done.7.fold_ref, bf16[2,2,1024,1024]{3,2,1,0:T(8,128)(2,1)S(1)} %get-tuple-element.30.rest_4_.hi_ref.rest_0_, bf16[2,2,1024,1024]{3,2,1,0:T(8,128)(2,1)S(1)} %get-tuple-element.31.rest_5_.lo_ref.rest_1_, ...), custom_call_target="tpu_custom_call" | custom-call | flops 1 | bytes 1 | tf_op jit(solution)/shard_map/collide/pallas_call | solution.py:532
Async XLA Ops:
  0.0 6.0 %copy-start.1 = (f32[16,16]{1,0:T(8,128)S(1)}, f32[16,16]{1,0:T(8,128)}, u32[]{:S(2)}) copy-start(f32[16,16]{1,0:T(8,128)} %param.5) | copy-start | bytes 3076
  0.0 6.1 %copy-start.2 = (s32[16,16]{1,0:T(8,128)S(1)}, s32[16,16]{1,0:T(8,128)}, u32[]{:S(2)}) copy-start(s32[16,16]{1,0:T(8,128)} %param.6) | copy-start | bytes 3076
  2.4 11.6 %collective-permute-start = (f32[2,16,2048]{2,1,0:T(8,128)}, f32[2,16,2048]{2,1,0:T(8,128)S(1)}, u32[]{:S(2)}, u32[]{:S(2)}) collective-permute-start(f32[2,16,2048]{2,1,0:T(8,128)} %get-tuple-element.27), channel_id=1, source_target_pairs={{0,16},{16,0},{1,17},{17,1},{2,18},{18,2},{3,19},{19,3},{4,20},{20... | collective-permute-start | bytes 786440 | tf_op jit(solution)/shard_map/ppermute | solution.py:567
  2.8 11.2 %collective-permute-start.1 = (f32[24,2048]{1,0:T(8,128)S(1)}, f32[24,2048]{1,0:T(8,128)S(1)}, u32[]{:S(2)}, u32[]{:S(2)}) collective-permute-start(f32[24,2048]{1,0:T(8,128)S(1)} %get-tuple-element.28.rest_2_), channel_id=1, source_target_pairs={{0,2},{2,0},{4,6},{6,4},{8,10},{10,8},{12,14},{14,12},{1,3},{3,1},... | collective-permute-start | bytes 589832 | tf_op jit(solution)/shard_map/ppermute | solution.py:546
  4.0 10.0 %collective-permute-start.2 = (f32[24,2048]{1,0:T(8,128)S(1)}, f32[24,2048]{1,0:T(8,128)S(1)}, u32[]{:S(2)}, u32[]{:S(2)}) collective-permute-start(f32[24,2048]{1,0:T(8,128)S(1)} %get-tuple-element.29.rest_3_), channel_id=1, source_target_pairs={{2,4},{4,2},{6,8},{8,6},{10,12},{12,10},{3,5},{5,3},{7,9},{9,7},{1... | collective-permute-start | bytes 589832 | tf_op jit(solution)/shard_map/ppermute | solution.py:546
  14.0 5.2 %copy-start = (f32[2048]{0:T(1024)S(1)}, f32[2048]{0:T(1024)}, u32[]{:S(2)}) copy-start(f32[2048]{0:T(1024)} %param.7) | copy-start | bytes 24580
  17.7 5.4 %collective-permute-start.3 = (f32[2,256,1024]{2,1,0:T(8,128)S(1)}, f32[2,256,1024]{2,1,0:T(8,128)S(1)}, u32[]{:S(2)}, u32[]{:S(2)}) collective-permute-start(f32[2,256,1024]{2,1,0:T(8,128)S(1)} %get-tuple-element.32.fold_ref), channel_id=1, source_target_pairs={{0,1},{1,0},{2,3},{3,2},{4,5},{5,4},{6,7},{7,6},{8,9},{9,8},{10,11... | collective-permute-start | bytes 6291464 | tf_op jit(solution)/shard_map/ppermute | solution.py:575
  26.9 7.6 %collective-permute-start.6 = (f32[2,16,2048]{2,1,0:T(8,128)S(1)}, f32[2,16,2048]{2,1,0:T(8,128)S(1)}, u32[]{:S(2)}, u32[]{:S(2)}) collective-permute-start(f32[2,16,2048]{2,1,0:T(8,128)S(1)} %get-tuple-element.40), channel_id=1, source_target_pairs={{0,16},{16,0},{1,17},{17,1},{2,18},{18,2},{3,19},{19,3},{4,20},{20... | collective-permute-start | bytes 786440 | tf_op jit(solution)/shard_map/ppermute | solution.py:567
  28.1 9.6 %collective-permute-start.4 = (f32[24,2048]{1,0:T(8,128)S(1)}, f32[24,2048]{1,0:T(8,128)S(1)}, u32[]{:S(2)}, u32[]{:S(2)}) collective-permute-start(f32[24,2048]{1,0:T(8,128)S(1)} %get-tuple-element.36.one_ref), channel_id=1, source_target_pairs={{0,2},{2,0},{4,6},{6,4},{8,10},{10,8},{12,14},{14,12},{1,3},{3,1},... | collective-permute-start | bytes 589832 | tf_op jit(solution)/shard_map/ppermute | solution.py:546
  30.5 8.3 %collective-permute-start.5 = (f32[24,2048]{1,0:T(8,128)S(1)}, f32[24,2048]{1,0:T(8,128)S(1)}, u32[]{:S(2)}, u32[]{:S(2)}) collective-permute-start(f32[24,2048]{1,0:T(8,128)S(1)} %get-tuple-element.37.two_ref), channel_id=1, source_target_pairs={{2,4},{4,2},{6,8},{8,6},{10,12},{12,10},{3,5},{5,3},{7,9},{9,7},{1... | collective-permute-start | bytes 589832 | tf_op jit(solution)/shard_map/ppermute | solution.py:546
  40.1 5.7 %collective-permute-start.7 = (f32[2,256,1024]{2,1,0:T(8,128)S(1)}, f32[2,256,1024]{2,1,0:T(8,128)S(1)}, u32[]{:S(2)}, u32[]{:S(2)}) collective-permute-start(f32[2,256,1024]{2,1,0:T(8,128)S(1)} %get-tuple-element.43.fold_ref), channel_id=1, source_target_pairs={{0,1},{1,0},{2,3},{3,2},{4,5},{5,4},{6,7},{7,6},{8,9},{9,8},{10,11... | collective-permute-start | bytes 6291464 | tf_op jit(solution)/shard_map/ppermute | solution.py:575

commit v8 on v7

--- a/solution.py
+++ b/solution.py
@@ -467,7 +467,7 @@
 def own_gain(fold, entries, advected, density, kind, inflow):
     _, cells, size = fold.shape
     return pl.pallas_call(
-        functools.partial(own_body, 2 * LANES),
+        functools.partial(own_body, 4 * LANES),
         in_specs=[WHOLE] * 7,
         out_specs=[WHOLE] * 2,
         out_shape=[pltpu.VMEM(fold.shape, jnp.float32), pltpu.VMEM(advected.shape, jnp.float32)],
@@ -519,7 +519,7 @@
 def collide(rows_x, fold, entries, part, kept, density, kind, last):
     _, cells, size = fold.shape
     local_len = kept.shape[1]
-    wide = 2 * LANES
+    wide = 4 * LANES
     halves = [pltpu.VMEM(fold.shape, jnp.bfloat16)] * 2
     if last:
         out_specs = pl.BlockSpec(memory_space=pl.ANY)

time: 51.5 us -> 51.9 us (level)
  transfers between devices with their start and end apart: 8 -> 8, of which waited for: 2 -> 3; matrix products, arithmetic and copies ran while one was open for 0% -> 0% of each run, Pallas kernels for 37% -> 36%
where the time goes in v8:
time: 51.9 us; the launch traced here: 51.3 us
  Pallas kernels  35 us (67%)
  starting transfers between devices  12.8 us (25%)
  waiting for transfers between devices  2.97 us (6%)
    pallas_call x2, Pallas kernels, collide(): pl.pallas_call(functools.partial(collide_body, wide, rows_x, last), in_sp...  9.2 us
    pallas_call x1, Pallas kernels, make_entries(): pl.pallas_call(functools.partial(entries_body, local, sources), in_specs=...  7.71 us
    ppermute x4, starting transfers between devices, swapped(): lax.ppermute(block, axis, [pair for i, j in pairs for pair in ((i, j), (j...  7.7 us
    pallas_call x2, Pallas kernels, own_gain(): pl.pallas_call(functools.partial(own_body, 4 * LANES), in_specs=[WHOLE] *...  7.44 us
    pallas_call x2, Pallas kernels, transport(): pl.pallas_call(functools.partial(transport_body, wide, rows_x, bool(yhalo...  6.94 us
    ppermute x2, starting transfers between devices, per_device(): other = lax.ppermute(fold, 'vert', swap)  3.48 us
    pallas_call x1, Pallas kernels, stage(): pl.pallas_call(functools.partial(stage_body, wide, rows_x), in_specs=[pl....  2.43 us
    ppermute x2, waiting for transfers between devices, per_device(): xhalo = lax.ppermute(send_x, 'gx', swap)  1.83 us
  transfers between devices with their start and end apart: 8, of which 3 were waited for; matrix products, arithmetic and copies ran while one was open for 0% of the time, Pallas kernels for 36%

profile of v8, /device:TPU:19, one launch (start us, length us, event | category | flops | bytes accessed | tf_op | source)
XLA Modules:
  0.0 51.3 jit_solution(5253881401035792971)
XLA Ops:
  0.0 0.0 copy-start.1
  0.0 0.0 copy-start.2
  0.0 2.4 %stage.1 = (f32[256,2048]{1,0:T(8,128)S(1)}, f32[24,2048]{1,0:T(8,128)S(1)}, f32[24,2048]{1,0:T(8,128)S(1)}, f32[2,16,2048]{2,1,0:T(8,128)}, f32[2,16,2048]{2,1,0:T(8,128)}) custom-call(f32[256,2048]{1,0:T(8,128)} %bitcast.5), custom_call_target="tpu_custom_call" | custom-call | tf_op jit(solution)/shard_map/stage/pallas_call | solution.py:213
  2.4 0.3 collective-permute-start
  2.8 1.2 %collective-permute-start.1 = (f32[24,2048]{1,0:T(8,128)S(1)}, f32[24,2048]{1,0:T(8,128)S(1)}, u32[]{:S(2)}, u32[]{:S(2)}) collective-permute-start(f32[24,2048]{1,0:T(8,128)S(1)} %get-tuple-element.28.rest_2_), channel_id=1, source_target_pairs={{0,2},{2,0},{4,6},{6,4},{8,10},{10,8},{12,14},{14,12},{1,3},{3,1},... | collective-permute-start | bytes 589832 | tf_op jit(solution)/shard_map/ppermute | solution.py:546
  4.0 2.0 %collective-permute-start.2 = (f32[24,2048]{1,0:T(8,128)S(1)}, f32[24,2048]{1,0:T(8,128)S(1)}, u32[]{:S(2)}, u32[]{:S(2)}) collective-permute-start(f32[24,2048]{1,0:T(8,128)S(1)} %get-tuple-element.29.rest_3_), channel_id=1, source_target_pairs={{2,4},{4,2},{6,8},{8,6},{10,12},{12,10},{3,5},{5,3},{7,9},{9,7},{1... | collective-permute-start | bytes 589832 | tf_op jit(solution)/shard_map/ppermute | solution.py:546
  6.0 0.0 copy-done.1
  6.0 0.1 reshape.20.rest_0_.density_ref
  6.1 0.0 copy-done.2
  6.1 0.1 reshape.21.rest_1_.type_ref
  6.2 7.7 %kernel_entries.1 = (bf16[2,2,1024,1024]{3,2,1,0:T(8,128)(2,1)S(1)}, bf16[2,2,1024,1024]{3,2,1,0:T(8,128)(2,1)S(1)}) custom-call(f32[256,1]{1,0:T(8,128)S(1)} %reshape.20.rest_0_.density_ref, s32[256,1]{1,0:T(8,128)S(1)} %reshape.21.rest_1_.type_ref), custom_call_target="tpu_custom_call" | custom-call | flops 1 | bytes 1 | tf_op jit(solution)/shard_map/kernel_entries/pallas_call | solution.py:124
  14.0 0.0 collective-permute-done.1.rest_0_
  14.0 0.0 collective-permute-done.2.rest_1_
  14.0 0.0 collective-permute-done.xhalo_ref
  14.0 0.0 copy-start
  14.0 3.6 %transport.1 = (f32[256,2048]{1,0:T(8,128)S(1)}, f32[2,256,1024]{2,1,0:T(8,128)S(1)}) custom-call(f32[256,2048]{1,0:T(8,128)S(1)} %get-tuple-element.26.field_ref, f32[2,16,2048]{2,1,0:T(8,128)S(1)} %collective-permute-done.xhalo_ref, f32[24,2048]{1,0:T(8,128)S(1)} %collective-permute-done.1.rest_0_, f32[24,2048]{1,0:T(8,128)S(1)} %collective-permute-done.2.rest_1_, ...), custom_call_target="tpu_custom_call" | custom-call | flops 1 | bytes 1 | tf_op jit(solution)/shard_map/transport/pallas_call | solution.py:408
  17.7 1.6 %collective-permute-start.3 = (f32[2,256,1024]{2,1,0:T(8,128)S(1)}, f32[2,256,1024]{2,1,0:T(8,128)S(1)}, u32[]{:S(2)}, u32[]{:S(2)}) collective-permute-start(f32[2,256,1024]{2,1,0:T(8,128)S(1)} %get-tuple-element.32.fold_ref), channel_id=1, source_target_pairs={{0,1},{1,0},{2,3},{3,2},{4,5},{5,4},{6,7},{7,6},{8,9},{9,8},{10,11... | collective-permute-start | bytes 6291464 | tf_op jit(solution)/shard_map/ppermute | solution.py:575
  19.2 0.0 copy-done
  19.2 3.7 %own_gain.2 = (f32[2,256,1024]{2,1,0:T(8,128)S(1)}, f32[256,2048]{1,0:T(8,128)S(1)}) custom-call(f32[2,256,1024]{2,1,0:T(8,128)S(1)} %get-tuple-element.32.fold_ref, bf16[2,2,1024,1024]{3,2,1,0:T(8,128)(2,1)S(1)} %get-tuple-element.30.rest_4_.hi_ref.rest_0_, bf16[2,2,1024,1024]{3,2,1,0:T(8,128)(2,1)S(1)} %get-tuple-element.31.rest_5_.lo_ref.rest_1_, ...), custom_call_target="tpu_custom_call" | custom-call | flops 1 | bytes 1 | tf_op jit(solution)/shard_map/own_gain/pallas_call | solution.py:469
  22.9 0.1 collective-permute-done.3.fold_ref
  23.0 4.0 %collide.2 = (f32[256,2048]{1,0:T(8,128)S(1)}, f32[24,2048]{1,0:T(8,128)S(1)}, f32[24,2048]{1,0:T(8,128)S(1)}, f32[2,16,2048]{2,1,0:T(8,128)S(1)}, f32[2,16,2048]{2,1,0:T(8,128)S(1)}) custom-call(f32[2,256,1024]{2,1,0:T(8,128)S(1)} %collective-permute-done.3.fold_ref, bf16[2,2,1024,1024]{3,2,1,0:T(8,128)(2,1)S(1)} %get-tuple-element.30.rest_4_.hi_ref.rest_0_, ...), custom_call_target="tpu_custom_call" | custom-call | flops 1 | bytes 1 | tf_op jit(solution)/shard_map/collide/pallas_call | solution.py:532
  27.0 1.3 %collective-permute-start.6 = (f32[2,16,2048]{2,1,0:T(8,128)S(1)}, f32[2,16,2048]{2,1,0:T(8,128)S(1)}, u32[]{:S(2)}, u32[]{:S(2)}) collective-permute-start(f32[2,16,2048]{2,1,0:T(8,128)S(1)} %get-tuple-element.40), channel_id=1, source_target_pairs={{0,16},{16,0},{1,17},{17,1},{2,18},{18,2},{3,19},{19,3},{4,20},{20... | collective-permute-start | bytes 786440 | tf_op jit(solution)/shard_map/ppermute | solution.py:567
  28.3 2.4 %collective-permute-start.4 = (f32[24,2048]{1,0:T(8,128)S(1)}, f32[24,2048]{1,0:T(8,128)S(1)}, u32[]{:S(2)}, u32[]{:S(2)}) collective-permute-start(f32[24,2048]{1,0:T(8,128)S(1)} %get-tuple-element.36.one_ref), channel_id=1, source_target_pairs={{0,2},{2,0},{4,6},{6,4},{8,10},{10,8},{12,14},{14,12},{1,3},{3,1},... | collective-permute-start | bytes 589832 | tf_op jit(solution)/shard_map/ppermute | solution.py:546
  30.7 2.1 %collective-permute-start.5 = (f32[24,2048]{1,0:T(8,128)S(1)}, f32[24,2048]{1,0:T(8,128)S(1)}, u32[]{:S(2)}, u32[]{:S(2)}) collective-permute-start(f32[24,2048]{1,0:T(8,128)S(1)} %get-tuple-element.37.two_ref), channel_id=1, source_target_pairs={{2,4},{4,2},{6,8},{8,6},{10,12},{12,10},{3,5},{5,3},{7,9},{9,7},{1... | collective-permute-start | bytes 589832 | tf_op jit(solution)/shard_map/ppermute | solution.py:546
  32.8 1.8 %collective-permute-done.6.xhalo_ref = f32[2,16,2048]{2,1,0:T(8,128)S(1)} collective-permute-done((f32[2,16,2048]{2,1,0:T(8,128)S(1)}, f32[2,16,2048]{2,1,0:T(8,128)S(1)}, u32[]{:S(2)}, u32[]{:S(2)}) %collective-permute-start.6) | collective-permute-done | bytes 262176 | tf_op jit(solution)/shard_map/ppermute | solution.py:567
  34.6 3.3 %inner_transport.1 = (f32[256,2048]{1,0:T(8,128)S(1)}, f32[2,256,1024]{2,1,0:T(8,128)S(1)}) custom-call(f32[256,2048]{1,0:T(8,128)S(1)} %get-tuple-element.39.field_ref, f32[2,16,2048]{2,1,0:T(8,128)S(1)} %collective-permute-done.6.xhalo_ref, bf16[2,2,1024,1024]{3,2,1,0:T(8,128)(2,1)S(1)} %get-tuple-element.30.rest_4_.hi_ref.rest_0_, ...), custom_call_target="tpu_custom_call" | custom-call | flops 1 | bytes 1 | tf_op jit(solution)/shard_map/inner_transport/pallas_call | solution.py:408
  37.9 0.0 collective-permute-done.4.one_halo
  37.9 1.0 %collective-permute-done.5.two_halo = f32[24,2048]{1,0:T(8,128)S(1)} collective-permute-done((f32[24,2048]{1,0:T(8,128)S(1)}, f32[24,2048]{1,0:T(8,128)S(1)}, u32[]{:S(2)}, u32[]{:S(2)}) %collective-permute-start.5) | collective-permute-done | bytes 196640 | tf_op jit(solution)/shard_map/ppermute | solution.py:546
  38.9 1.3 %add_columns.1 = (f32[256,2048]{1,0:T(8,128)S(1)}, f32[2,256,1024]{2,1,0:T(8,128)S(1)}) custom-call(f32[24,2048]{1,0:T(8,128)S(1)} %get-tuple-element.36.one_ref, f32[24,2048]{1,0:T(8,128)S(1)} %get-tuple-element.37.two_ref, f32[2,16,2048]{2,1,0:T(8,128)S(1)} %get-tuple-element.38.far_ref, ...), custom_call_target="tpu_custom_call", output_to_operand_aliasing={{0}: (5, {}), {1}: (6, {})} | custom-call | flops 1 | bytes 1 | tf_op jit(solution)/shard_map/add_columns/pallas_call | solution.py:422
  40.2 1.9 %collective-permute-start.7 = (f32[2,256,1024]{2,1,0:T(8,128)S(1)}, f32[2,256,1024]{2,1,0:T(8,128)S(1)}, u32[]{:S(2)}, u32[]{:S(2)}) collective-permute-start(f32[2,256,1024]{2,1,0:T(8,128)S(1)} %get-tuple-element.43.fold_ref), channel_id=1, source_target_pairs={{0,1},{1,0},{2,3},{3,2},{4,5},{5,4},{6,7},{7,6},{8,9},{9,8},{10,11... | collective-permute-start | bytes 6291464 | tf_op jit(solution)/shard_map/ppermute | solution.py:575
  42.2 3.7 %own_gain.3 = (f32[2,256,1024]{2,1,0:T(8,128)S(1)}, f32[256,2048]{1,0:T(8,128)S(1)}) custom-call(f32[2,256,1024]{2,1,0:T(8,128)S(1)} %get-tuple-element.43.fold_ref, bf16[2,2,1024,1024]{3,2,1,0:T(8,128)(2,1)S(1)} %get-tuple-element.30.rest_4_.hi_ref.rest_0_, bf16[2,2,1024,1024]{3,2,1,0:T(8,128)(2,1)S(1)} %get-tuple-element.31.rest_5_.lo_ref.rest_1_, ...), custom_call_target="tpu_custom_call" | custom-call | flops 1 | bytes 1 | tf_op jit(solution)/shard_map/own_gain/pallas_call | solution.py:469
  45.9 0.0 collective-permute-done.7.fold_ref
  45.9 5.2 %collide.3 = f32[256,2048]{1,0:T(8,128)} custom-call(f32[2,256,1024]{2,1,0:T(8,128)S(1)} %collective-permute-done.7.fold_ref, bf16[2,2,1024,1024]{3,2,1,0:T(8,128)(2,1)S(1)} %get-tuple-element.30.rest_4_.hi_ref.rest_0_, bf16[2,2,1024,1024]{3,2,1,0:T(8,128)(2,1)S(1)} %get-tuple-element.31.rest_5_.lo_ref.rest_1_, ...), custom_call_target="tpu_custom_call" | custom-call | flops 1 | bytes 1 | tf_op jit(solution)/shard_map/collide/pallas_call | solution.py:532
Async XLA Ops:
  0.0 6.0 %copy-start.1 = (f32[16,16]{1,0:T(8,128)S(1)}, f32[16,16]{1,0:T(8,128)}, u32[]{:S(2)}) copy-start(f32[16,16]{1,0:T(8,128)} %param.5) | copy-start | bytes 3076
  0.0 6.1 %copy-start.2 = (s32[16,16]{1,0:T(8,128)S(1)}, s32[16,16]{1,0:T(8,128)}, u32[]{:S(2)}) copy-start(s32[16,16]{1,0:T(8,128)} %param.6) | copy-start | bytes 3076
  2.4 11.6 %collective-permute-start = (f32[2,16,2048]{2,1,0:T(8,128)}, f32[2,16,2048]{2,1,0:T(8,128)S(1)}, u32[]{:S(2)}, u32[]{:S(2)}) collective-permute-start(f32[2,16,2048]{2,1,0:T(8,128)} %get-tuple-element.27), channel_id=1, source_target_pairs={{0,16},{16,0},{1,17},{17,1},{2,18},{18,2},{3,19},{19,3},{4,20},{20... | collective-permute-start | bytes 786440 | tf_op jit(solution)/shard_map/ppermute | solution.py:567
  2.8 11.2 %collective-permute-start.1 = (f32[24,2048]{1,0:T(8,128)S(1)}, f32[24,2048]{1,0:T(8,128)S(1)}, u32[]{:S(2)}, u32[]{:S(2)}) collective-permute-start(f32[24,2048]{1,0:T(8,128)S(1)} %get-tuple-element.28.rest_2_), channel_id=1, source_target_pairs={{0,2},{2,0},{4,6},{6,4},{8,10},{10,8},{12,14},{14,12},{1,3},{3,1},... | collective-permute-start | bytes 589832 | tf_op jit(solution)/shard_map/ppermute | solution.py:546
  4.0 10.0 %collective-permute-start.2 = (f32[24,2048]{1,0:T(8,128)S(1)}, f32[24,2048]{1,0:T(8,128)S(1)}, u32[]{:S(2)}, u32[]{:S(2)}) collective-permute-start(f32[24,2048]{1,0:T(8,128)S(1)} %get-tuple-element.29.rest_3_), channel_id=1, source_target_pairs={{2,4},{4,2},{6,8},{8,6},{10,12},{12,10},{3,5},{5,3},{7,9},{9,7},{1... | collective-permute-start | bytes 589832 | tf_op jit(solution)/shard_map/ppermute | solution.py:546
  14.0 5.2 %copy-start = (f32[2048]{0:T(1024)S(1)}, f32[2048]{0:T(1024)}, u32[]{:S(2)}) copy-start(f32[2048]{0:T(1024)} %param.7) | copy-start | bytes 24580
  17.7 5.4 %collective-permute-start.3 = (f32[2,256,1024]{2,1,0:T(8,128)S(1)}, f32[2,256,1024]{2,1,0:T(8,128)S(1)}, u32[]{:S(2)}, u32[]{:S(2)}) collective-permute-start(f32[2,256,1024]{2,1,0:T(8,128)S(1)} %get-tuple-element.32.fold_ref), channel_id=1, source_target_pairs={{0,1},{1,0},{2,3},{3,2},{4,5},{5,4},{6,7},{7,6},{8,9},{9,8},{10,11... | collective-permute-start | bytes 6291464 | tf_op jit(solution)/shard_map/ppermute | solution.py:575
  27.0 7.6 %collective-permute-start.6 = (f32[2,16,2048]{2,1,0:T(8,128)S(1)}, f32[2,16,2048]{2,1,0:T(8,128)S(1)}, u32[]{:S(2)}, u32[]{:S(2)}) collective-permute-start(f32[2,16,2048]{2,1,0:T(8,128)S(1)} %get-tuple-element.40), channel_id=1, source_target_pairs={{0,16},{16,0},{1,17},{17,1},{2,18},{18,2},{3,19},{19,3},{4,20},{20... | collective-permute-start | bytes 786440 | tf_op jit(solution)/shard_map/ppermute | solution.py:567
  28.3 9.6 %collective-permute-start.4 = (f32[24,2048]{1,0:T(8,128)S(1)}, f32[24,2048]{1,0:T(8,128)S(1)}, u32[]{:S(2)}, u32[]{:S(2)}) collective-permute-start(f32[24,2048]{1,0:T(8,128)S(1)} %get-tuple-element.36.one_ref), channel_id=1, source_target_pairs={{0,2},{2,0},{4,6},{6,4},{8,10},{10,8},{12,14},{14,12},{1,3},{3,1},... | collective-permute-start | bytes 589832 | tf_op jit(solution)/shard_map/ppermute | solution.py:546
  30.7 8.2 %collective-permute-start.5 = (f32[24,2048]{1,0:T(8,128)S(1)}, f32[24,2048]{1,0:T(8,128)S(1)}, u32[]{:S(2)}, u32[]{:S(2)}) collective-permute-start(f32[24,2048]{1,0:T(8,128)S(1)} %get-tuple-element.37.two_ref), channel_id=1, source_target_pairs={{2,4},{4,2},{6,8},{8,6},{10,12},{12,10},{3,5},{5,3},{7,9},{9,7},{1... | collective-permute-start | bytes 589832 | tf_op jit(solution)/shard_map/ppermute | solution.py:546
  40.2 5.7 %collective-permute-start.7 = (f32[2,256,1024]{2,1,0:T(8,128)S(1)}, f32[2,256,1024]{2,1,0:T(8,128)S(1)}, u32[]{:S(2)}, u32[]{:S(2)}) collective-permute-start(f32[2,256,1024]{2,1,0:T(8,128)S(1)} %get-tuple-element.43.fold_ref), channel_id=1, source_target_pairs={{0,1},{1,0},{2,3},{3,2},{4,5},{5,4},{6,7},{7,6},{8,9},{9,8},{10,11... | collective-permute-start | bytes 6291464 | tf_op jit(solution)/shard_map/ppermute | solution.py:575
